TPU v7x, 32 devices: a whole 2x2x4 slice. The times are simulated.
32 devices in a mesh: groups: 2 (over y), frame: 4 (over z), head: 2 (over x), sub: 2 (over core).
Axes of the slice: x: 2, y: 2, z: 4, core: 2. Of those that a mesh axis runs over, the one named last changes fastest.
Arguments:
- queries: bfloat16 [3072, 2560], P(('groups', 'frame'), ('head', 'sub')), parts along dimension 0, may hold values from -6 to 6, as said below
- keyvals: bfloat16 [2, 3072, 2560], P(None, ('groups', 'frame'), ('head', 'sub')), parts along dimension 1, may hold values from -6 to 6, as said below
- residual_in: float32 [3072, 5120], P(('groups', 'frame'), ('head', 'sub')), parts along dimension 0, may hold values from -3 to 3
- gate: float32 [10240], P(('groups', 'head', 'sub')), parts along dimension 0, may hold values from -4 to 4
- out_weight: bfloat16 [2560, 5120], P(('head', 'sub'), 'frame'), may hold values from -0.125 to 0.125
- pattern: int32 [48, 8], P(('groups', 'frame')), parts along dimension 0, may hold values from 0 to 23, as said below
- live: int32 [48], P(('groups', 'frame')), parts along dimension 0, may hold values from 4 to 8
Outputs:
- updated: float32 [3072, 5120], P(('groups', 'frame'), ('head', 'sub')), parts along dimension 0
There are 2 independent parts, one for each index of `groups`. A program takes and returns all parts, laid end to end along the dimension named above; an argument that names none is the same for every part. Nothing has to cross between parts.
Inputs may be any that keep to these rules, and one draw needn't show every extreme that they name: `pattern`: entry 0 of each row is the query tile itself; entries below live of that row are distinct tiles lying in the query tile's frame or one frame before or after it; later entries repeat the query tile. `queries`: values of order one. `keyvals`: values of order one.
All inputs are finite; a program needn't handle non-finite values.
Results may differ from a plain program's by a relative error of at most 0.0065.
Values may be sent and summed in bfloat16 or wider, within the bound.
No kernel may reach another device: no remote copies, remote signals or barrier semaphores. Data moves between devices by JAX's collectives and lax.ppermute only.
A program may use at most 128 MiB of HBM per device.

v0:
```python
import math

import jax
import jax.numpy as jnp
from jax import lax
from jax.sharding import PartitionSpec as P

HEAD_DIM = 128
TILES_F = 6
KSEL = 8


def padded_2(block, sides, width):
    for axis, dim in sides:
        count = lax.axis_size(axis)
        forward = [(i, i + 1) for i in range(count - 1)]
        backward = [(target, source) for source, target in forward]
        low = lax.ppermute(
            lax.slice_in_dim(block, block.shape[dim] - width, None, axis=dim), axis, forward
        )
        high = lax.ppermute(lax.slice_in_dim(block, 0, width, axis=dim), axis, backward)
        block = jnp.concatenate([low, block, high], axis=dim)
    return block


def per_device(queries, keyvals, residual_in, gate, out_weight, pattern, live):
    rows, width = queries.shape
    tile_count = pattern.shape[0]
    tile_rows = rows // tile_count
    head_count = width // HEAD_DIM
    padded = padded_2(keyvals, (("frame", 1),), TILES_F * tile_rows)
    first_tile = lax.axis_index("frame") * tile_count - TILES_F
    local_ids = pattern - first_tile
    key_tiles = padded.reshape(2, -1, tile_rows, width)
    picked = key_tiles[:, local_ids]
    picked = picked.reshape(2, tile_count, KSEL * tile_rows, head_count, HEAD_DIM)
    query_tiles = queries.reshape(tile_count, tile_rows, head_count, HEAD_DIM)
    scores = jnp.einsum(
        "tqhd,tkhd->thqk", query_tiles, picked[0], preferred_element_type=jnp.float32
    ) * (1.0 / math.sqrt(HEAD_DIM))
    slot = jnp.arange(KSEL * tile_rows, dtype=jnp.int32) // tile_rows
    allowed = slot[None, :] < live[:, None]
    scores = jnp.where(allowed[:, None, None, :], scores, -1e30)
    row_max = jnp.max(scores, axis=-1, keepdims=True)
    expo = jnp.exp(scores - row_max)
    probs = (expo / jnp.sum(expo, axis=-1, keepdims=True)).astype(jnp.bfloat16)
    attended = jnp.einsum(
        "thqk,tkhd->tqhd", probs, picked[1], preferred_element_type=jnp.float32
    ).astype(jnp.bfloat16)
    attended = attended.reshape(rows, width)
    partial_rows = jnp.dot(
        attended,
        lax.all_gather(out_weight, "frame", axis=1, tiled=True),
        preferred_element_type=jnp.float32,
    )
    summed = lax.psum_scatter(
        partial_rows.astype(jnp.bfloat16), ("head", "sub"), scatter_dimension=1, tiled=True
    ).astype(jnp.float32)
    return residual_in + gate[None, :] * summed


def solution(mesh):
    in_specs = (
        P(("groups", "frame"), ("head", "sub")),
        P(None, ("groups", "frame"), ("head", "sub")),
        P(("groups", "frame"), ("head", "sub")),
        P(("groups", "head", "sub")),
        P(("head", "sub"), "frame"),
        P(("groups", "frame"), None),
        P(("groups", "frame")),
    )
    out_specs = P(("groups", "frame"), ("head", "sub"))
    return jax.shard_map(
        per_device, mesh=mesh, in_specs=in_specs, out_specs=out_specs, check_vma=False
    )
```

profile of v0, /device:TPU:8, one launch (start us, length us, event | category | flops | bytes accessed | tf_op | source)
XLA Modules:
  0.0 202.6 jit_solution(16965201183154617614)
XLA Ops:
  6.5 0.0 all-gather.2.cloned.1.call-start
  6.5 0.7 all-gather.2.cloned.1.call-update
  7.3 0.0 reduce-scatter.2.cloned.1.call-start
  7.3 3.5 %collective-permute-start = (bf16[2,384,640]{2,1,0:T(8,128)(2,1)}, bf16[2,384,640]{2,1,0:T(8,128)(2,1)S(1)}, u32[]{:S(2)}, u32[]{:S(2)}) collective-permute-start(bf16[2,384,640]{2,1,0:T(8,128)(2,1)} %param.8), channel_id=1, source_target_pairs={{0,4},{4,8},{8,12},{1,5},{5,9},{9,13},{2,6},{6,10},{10,14},{3,7},{... | collective-permute-start | bytes 2949128 | tf_op jit(solution)/shard_map/ppermute | solution.py:18
  10.8 2.4 %collective-permute-start.1 = (bf16[2,384,640]{2,1,0:T(8,128)(2,1)}, bf16[2,384,640]{2,1,0:T(8,128)(2,1)}, u32[]{:S(2)}, u32[]{:S(2)}) collective-permute-start(bf16[2,384,640]{2,1,0:T(8,128)(2,1)} %param.8), channel_id=1, source_target_pairs={{4,0},{8,4},{12,8},{5,1},{9,5},{13,9},{6,2},{10,6},{14,10},{7,3},{... | collective-permute-start | bytes 2949128 | tf_op jit(solution)/shard_map/ppermute | solution.py:21
  13.2 0.7 compare_select_fusion
  13.9 0.1 reshape.58
  14.0 2.4 %reshape.54 = bf16[6,64,5,128]{3,2,1,0:T(8,128)(2,1)} reshape(bf16[384,640]{1,0:T(8,128)(2,1)} %param.7) | data formatting | bytes 983040 | tf_op jit(solution)/shard_map/reshape | solution.py:37
  16.4 0.7 broadcast_compare_fusion
  17.1 40.9 %collective-permute-done = bf16[2,384,640]{2,1,0:T(8,128)(2,1)S(1)} collective-permute-done((bf16[2,384,640]{2,1,0:T(8,128)(2,1)}, bf16[2,384,640]{2,1,0:T(8,128)(2,1)S(1)}, u32[]{:S(2)}, u32[]{:S(2)}) %collective-permute-start) | collective-permute-done | bytes 983072 | tf_op jit(solution)/shard_map/ppermute | solution.py:18
  58.1 0.0 copy-start.2
  58.1 0.9 copy-done.2
  59.0 9.5 %collective-permute-done.1 = bf16[2,384,640]{2,1,0:T(8,128)(2,1)} collective-permute-done((bf16[2,384,640]{2,1,0:T(8,128)(2,1)}, bf16[2,384,640]{2,1,0:T(8,128)(2,1)}, u32[]{:S(2)}, u32[]{:S(2)}) %collective-permute-start.1) | collective-permute-done | bytes 983072 | tf_op jit(solution)/shard_map/ppermute | solution.py:21
  68.5 2.1 %pad_maximum_fusion = bf16[2,1152,640]{2,1,0:T(8,128)(2,1)S(1)} fusion(bf16[2,384,640]{2,1,0:T(8,128)(2,1)} %collective-permute-done.1, bf16[2,384,640]{2,1,0:T(8,128)(2,1)} %param.8, bf16[2,384,640]{2,1,0:T(8,128)(2,1)} %copy-done.2), kind=kLoop, calls=%fused_computation.13 | loop fusion | flops 8847360 | bytes 5898240 | tf_op jit(solution)/shard_map/concatenate | solution.py:22
  70.6 5.9 %gather_fusion = bf16[48,2,64,640]{3,2,1,0:T(8,128)(2,1)} fusion(bf16[2,18,64,640]{3,2,1,0:T(8,128)(2,1)S(1)} %bitcast.27, s32[1024]{0:T(1024)S(1)} %pad_clamp_fusion), kind=kCustom, calls=%fused_computation | custom fusion | bytes 15728832 | tf_op jit(solution)/shard_map/gather | solution.py:35
  76.5 4.1 %copy.9 = bf16[48,2,64,640]{3,2,0,1:T(8,128)(2,1)S(1)} copy(bf16[48,2,64,640]{3,2,1,0:T(8,128)(2,1)} %gather_fusion) | data formatting | bytes 15728640 | tf_op jit(solution)/shard_map/gather | solution.py:35
  80.6 3.5 %fusion.27 = (bf16[1,6,8,64,640]{4,3,2,1,0:T(8,128)(2,1)}, bf16[1,6,8,64,640]{4,3,2,1,0:T(8,128)(2,1)}) fusion(bf16[2,6,8,64,640]{4,3,2,1,0:T(8,128)(2,1)S(1)} %bitcast.28), kind=kLoop, calls=%fused_computation.36 | loop fusion | bytes 15728640 | tf_op jit(solution)/shard_map/slice | solution.py:39
  84.1 9.6 %squeeze.7 = bf16[6,512,5,128]{3,2,1,0:T(8,128)(2,1)} reshape(bf16[1,6,8,64,640]{4,3,2,1,0:T(8,128)(2,1)} %get-tuple-element.5) | data formatting | bytes 7864320 | tf_op jit(solution)/shard_map/squeeze | solution.py:39
  93.7 0.0 copy-start
  93.7 9.6 %squeeze.6 = bf16[6,512,5,128]{3,2,1,0:T(8,128)(2,1)} reshape(bf16[1,6,8,64,640]{4,3,2,1,0:T(8,128)(2,1)} %get-tuple-element.6) | data formatting | bytes 7864320 | tf_op jit(solution)/shard_map/squeeze | solution.py:48
  103.4 0.0 copy-done
  103.4 0.0 slice-start
  103.4 4.5 %fusion.5 = f32[6,5,512,64]{2,3,1,0:T(8,128)S(1)} fusion(bf16[6,512,5,128]{3,2,1,0:T(8,128)(2,1)} %squeeze.7, bf16[6,64,5,128]{3,2,1,0:T(8,128)(2,1)S(1)} %copy-done), kind=kOutput, calls=%fused_computation.9 | convolution fusion | flops 251658240 | bytes 8355840 | tf_op jit(solution)/shard_map/tqhd,tkhd->thqk/dot_general | solution.py:38
  107.9 0.0 slice-start.1
  108.0 1.8 fusion.28
  109.7 0.0 slice-done
  109.7 0.4 slice-done.1
  110.1 1.3 fusion.16
  111.5 0.4 copy.13
  111.8 27.2 %all-gather.2.cloned.1.call-done = bf16[640,5120]{1,0:T(8,128)(2,1)} async-done(((bf16[640,1280]{1,0:T(8,128)(2,1)}), bf16[640,5120]{1,0:T(8,128)(2,1)}) %all-gather.2.cloned.1.call-update) | async-done | bytes 6553616 | tf_op jit(solution)/shard_map/all_gather | solution.py:53
  139.0 7.6 %convolution_convert_fusion = bf16[384,5120]{1,0:T(8,128)(2,1)} fusion(bf16[640,5120]{1,0:T(8,128)(2,1)} %all-gather.2.cloned.1.call-done, bf16[48,8,5,128]{3,2,1,0:T(8,128)(2,1)S(1)} %bitcast.31), kind=kOutput, calls=%fused_computation.2 | convolution fusion | flops 2518548480 | bytes 10977280 | tf_op jit(solution)/shard_map/dot_general | solution.py:51
  146.6 0.0 copy-start.1
  146.6 0.0 copy-start.3
  146.6 0.0 reduce-scatter.2.cloned.1.call-update
  146.7 46.4 %reduce-scatter.2.cloned.1.call-done = bf16[384,1280]{1,0:T(8,128)(2,1)} async-done(((bf16[384,5120]{1,0:T(8,128)(2,1)}), bf16[384,1280]{1,0:T(8,128)(2,1)}) %reduce-scatter.2.cloned.1.call-update) | async-done | bytes 983056 | tf_op jit(solution)/shard_map/reduce_scatter | solution.py:56
  193.1 0.0 copy-done.1
  193.1 0.0 copy-done.3
  193.1 2.7 %multiply_add_fusion = f32[384,1280]{1,0:T(8,128)} fusion(f32[384,1280]{1,0:T(8,128)S(1)} %copy-done.1, bf16[384,1280]{1,0:T(8,128)(2,1)} %reduce-scatter.2.cloned.1.call-done, f32[1280]{0:T(1024)S(1)} %copy-done.3), kind=kLoop, calls=%fused_computation.14 | loop fusion | flops 1474560 | bytes 4920320 | tf_op jit(solution)/shard_map/add | solution.py:59
  (3 shorter events, 0.0 us)
Async XLA Ops:
  6.5 132.5 %all-gather.2.cloned.1.call-start = ((), (), s32[]{:S(2)}) async-start(), calls=%async_computation.1 | async-start | bytes 8192000 | tf_op jit(solution)/shard_map/all_gather | solution.py:53
  7.3 185.8 %reduce-scatter.2.cloned.1.call-start = ((), (), s32[]{:S(2)}) async-start(), calls=%async_computation.2 | async-start | bytes 4915200 | tf_op jit(solution)/shard_map/reduce_scatter | solution.py:56
  7.3 50.8 %collective-permute-start = (bf16[2,384,640]{2,1,0:T(8,128)(2,1)}, bf16[2,384,640]{2,1,0:T(8,128)(2,1)S(1)}, u32[]{:S(2)}, u32[]{:S(2)}) collective-permute-start(bf16[2,384,640]{2,1,0:T(8,128)(2,1)} %param.8), channel_id=1, source_target_pairs={{0,4},{4,8},{8,12},{1,5},{5,9},{9,13},{2,6},{6,10},{10,14},{3,7},{... | collective-permute-start | bytes 2949128 | tf_op jit(solution)/shard_map/ppermute | solution.py:18
  10.8 57.7 %collective-permute-start.1 = (bf16[2,384,640]{2,1,0:T(8,128)(2,1)}, bf16[2,384,640]{2,1,0:T(8,128)(2,1)}, u32[]{:S(2)}, u32[]{:S(2)}) collective-permute-start(bf16[2,384,640]{2,1,0:T(8,128)(2,1)} %param.8), channel_id=1, source_target_pairs={{4,0},{8,4},{12,8},{5,1},{9,5},{13,9},{6,2},{10,6},{14,10},{7,3},{... | collective-permute-start | bytes 2949128 | tf_op jit(solution)/shard_map/ppermute | solution.py:21
  58.1 0.9 copy-start.2
  93.7 9.7 %copy-start = (bf16[6,64,5,128]{3,2,1,0:T(8,128)(2,1)S(1)}, bf16[6,64,5,128]{3,2,1,0:T(8,128)(2,1)}, u32[]{:S(2)}) copy-start(bf16[6,64,5,128]{3,2,1,0:T(8,128)(2,1)} %reshape.54) | copy-start | bytes 1474564
  103.4 6.3 %slice-start = ((s8[6291456]{0:T(1024)(128)(4,1)}), s8[2097152]{0:T(1024)(128)(4,1)S(1)}, s32[]{:S(2)}) async-start(s8[6291456]{0:T(1024)(128)(4,1)} %bitcast.29), calls=%async_computation.3 | async-start | bytes 4194304
  107.9 2.2 %slice-start.1 = ((s8[6291456]{0:T(1024)(128)(4,1)}), s8[4194304]{0:T(1024)(128)(4,1)S(1)}, s32[]{:S(2)}) async-start(s8[6291456]{0:T(1024)(128)(4,1)} %bitcast.29), calls=%async_computation.4 | async-start | bytes 8388608
  146.6 46.4 %copy-start.1 = (f32[384,1280]{1,0:T(8,128)S(1)}, f32[384,1280]{1,0:T(8,128)}, u32[]{:S(2)}) copy-start(f32[384,1280]{1,0:T(8,128)} %param.9) | copy-start | bytes 5898244
  146.6 46.4 %copy-start.3 = (f32[1280]{0:T(1024)S(1)}, f32[1280]{0:T(1024)}, u32[]{:S(2)}) copy-start(f32[1280]{0:T(1024)} %param.10) | copy-start | bytes 15364
Sparse Core Ops, SparseCore 0:
  8.9 130.0 all-gather.1
  146.8 46.2 reduce-scatter.1
where the time goes:
time: 205 us; the launch traced here: 203 us
  waiting for transfers between devices  125 us (61%)
  local copies, waits for them, and re-layouts  36.9 us (18%)
  matrix products  13.5 us (7%)
  between operations  13.5 us (7%)
  other arithmetic  7.96 us (4%)
  starting transfers between devices  5.95 us (3%)
    reduce_scatter x1, waiting for transfers between devices, per_device(): lax.psum_scatter(partial_rows.astype(jnp.bfloat16), ('head', 'sub'), scat...  46.4 us
    ppermute x1, waiting for transfers between devices, padded_2(): lax.ppermute(lax.slice_in_dim(block, block.shape[dim] - width, None, axis...  40.9 us
    all_gather x1, waiting for transfers between devices, per_device(): lax.all_gather(out_weight, 'frame', axis=1, tiled=True)  27.2 us
    gather x2, local copies, waits for them, and re-layouts, per_device(): picked = key_tiles[:, local_ids]  10 us
    squeeze x1, local copies, waits for them, and re-layouts, per_device(): picked[1]  9.65 us
    squeeze x1, local copies, waits for them, and re-layouts, per_device(): picked[0]  9.61 us
    ppermute x1, waiting for transfers between devices, padded_2(): lax.ppermute(lax.slice_in_dim(block, 0, width, axis=dim), axis, backward)  9.52 us
    dot_general x1, matrix products, per_device(): jnp.dot(attended, lax.all_gather(out_weight, 'frame', axis=1, tiled=True)...  7.61 us
  transfers between devices with their start and end apart: 4, of which 4 were waited for; matrix products, arithmetic and copies ran while one was open for 23% of the time, Pallas kernels for 0%

commit v1 on v0

v1 whole, which is shorter than its diff:
```python
import math

import jax
import jax.numpy as jnp
from jax import lax
from jax.experimental import pallas as pl
from jax.experimental.pallas import tpu as pltpu
from jax.sharding import PartitionSpec as P

HEAD_DIM = 128
TILES_F = 6
KSEL = 8
AXES = ("groups", "frame", "head", "sub")
MIB = 1 << 20


def attend_kernel(ids, live, q_ref, own_ref, low_ref, high_ref, out_ref, kv, sems):
    tiles = ids.shape[0]
    rows, width = q_ref.shape
    tile = rows // tiles
    heads = width // HEAD_DIM
    copies = [
        pltpu.make_async_copy(src, kv.at[:, pl.ds(i * rows, rows), :], sems.at[i])
        for i, src in enumerate((low_ref, own_ref, high_ref))
    ]
    for copy in copies:
        copy.start()
    for copy in copies:
        copy.wait()
    scale = 1.0 / math.sqrt(HEAD_DIM)
    column = lax.broadcasted_iota(jnp.int32, (tile, KSEL * tile), 1)

    def one_tile(t, carry):
        row = pl.multiple_of(t * tile, tile)
        starts = [pl.multiple_of(ids[t, s] * tile, tile) for s in range(KSEL)]
        allowed = column < live[t] * tile
        for h in range(heads):
            lanes = slice(h * HEAD_DIM, (h + 1) * HEAD_DIM)
            keys = jnp.concatenate([kv[0, pl.ds(s, tile), lanes] for s in starts], axis=0)
            values = jnp.concatenate([kv[1, pl.ds(s, tile), lanes] for s in starts], axis=0)
            scores = lax.dot_general(
                q_ref[pl.ds(row, tile), lanes],
                keys,
                (((1,), (1,)), ((), ())),
                preferred_element_type=jnp.float32,
            )
            scores = jnp.where(allowed, scores * scale, -1e30)
            expo = jnp.exp(scores - jnp.max(scores, axis=-1, keepdims=True))
            probs = (expo / jnp.sum(expo, axis=-1, keepdims=True)).astype(jnp.bfloat16)
            out_ref[pl.ds(row, tile), lanes] = jnp.dot(
                probs, values, preferred_element_type=jnp.float32
            ).astype(jnp.bfloat16)
        return carry

    lax.fori_loop(0, tiles, one_tile, 0)


def attend(queries, keyvals, low, high, pattern, live):
    rows, width = queries.shape
    tile_count = pattern.shape[0]
    local_ids = pattern - (lax.axis_index("frame") * tile_count - TILES_F)
    anywhere = pl.BlockSpec(memory_space=pl.ANY)
    scalars = pl.BlockSpec(memory_space=pltpu.SMEM)
    whole = pl.BlockSpec(memory_space=pltpu.VMEM)
    return pl.pallas_call(
        attend_kernel,
        out_shape=jax.ShapeDtypeStruct((rows, width), jnp.bfloat16),
        in_specs=[scalars, scalars, whole, anywhere, anywhere, anywhere],
        out_specs=whole,
        scratch_shapes=[
            pltpu.VMEM((2, 3 * rows, width), jnp.bfloat16),
            pltpu.SemaphoreType.DMA((3,)),
        ],
        compiler_params=pltpu.CompilerParams(vmem_limit_bytes=24 * MIB),
        cost_estimate=pl.CostEstimate(
            flops=4 * rows * KSEL * rows // tile_count * width,
            bytes_accessed=16 * rows * width,
            transcendentals=rows * KSEL * rows // tile_count * (width // HEAD_DIM),
        ),
        name="attend",
    )(local_ids, live, queries, keyvals, low, high)


def halos(keyvals):
    count = lax.axis_size("frame")
    forward = [(i, i + 1) for i in range(count - 1)]
    backward = [(b, a) for a, b in forward]
    return lax.ppermute(keyvals, "frame", forward), lax.ppermute(keyvals, "frame", backward)


def plain(queries, keyvals, residual_in, gate, out_weight, pattern, live):
    low, high = halos(keyvals)
    attended = attend(queries, keyvals, low, high, pattern, live)
    weights = lax.all_gather(out_weight, "frame", axis=1, tiled=True)
    partial_rows = jnp.dot(attended, weights, preferred_element_type=jnp.float32)
    summed = lax.psum_scatter(
        partial_rows.astype(jnp.bfloat16), ("head", "sub"), scatter_dimension=1, tiled=True
    ).astype(jnp.float32)
    return residual_in + gate[None, :] * summed


def place(y, f, x, c):
    return ((y * 4 + f) * 2 + x) * 2 + c


def pairs(move, keep=lambda y, f, x, c: True):
    found = []
    for y in range(2):
        for f in range(4):
            for x in range(2):
                for c in range(2):
                    if keep(y, f, x, c):
                        found.append((place(y, f, x, c), place(*move(y, f, x, c))))
    return found


def block_at(k, f, x):
    return (f - k) % 4 if x == 0 else (f + k) % 4


def to_owner(steps, cross):
    def move(y, f, x, c):
        g = block_at(steps[x], f, x)
        return c, f, g // 2, g % 2

    return pairs(move, lambda y, f, x, c: (y ^ c) == cross)


def send(array, route):
    return lax.ppermute(array, AXES, route)


def finish_kernel(spot, *refs):
    direct, crossed = refs[:4], refs[4:8]
    residual, gate, out = refs[8:]
    half = direct[0].shape[1]
    for cross, parts in ((0, direct), (1, crossed)):
        start = pl.multiple_of((spot[0] ^ cross) * half, half)
        lanes = pl.ds(start, half)
        total = parts[0][...].astype(jnp.float32)
        for part in parts[1:]:
            total = total + part[...].astype(jnp.float32)
        out[:, lanes] = residual[:, lanes] + gate[:, lanes] * total


def finish(direct, crossed, residual_in, gate, spot):
    rows, width = residual_in.shape
    step = 128
    narrow = pl.BlockSpec((step, width // 2), lambda i: (i, 0))
    wide = pl.BlockSpec((step, width), lambda i: (i, 0))
    return pl.pallas_call(
        finish_kernel,
        grid=(rows // step,),
        out_shape=jax.ShapeDtypeStruct((rows, width), jnp.float32),
        in_specs=[pl.BlockSpec(memory_space=pltpu.SMEM)]
        + [narrow] * 8
        + [wide, pl.BlockSpec((1, width), lambda i: (0, 0))],
        out_specs=wide,
        compiler_params=pltpu.CompilerParams(vmem_limit_bytes=32 * MIB),
        name="finish",
    )(spot, *direct, *crossed, residual_in, gate[None, :])


def ringed(queries, keyvals, residual_in, gate, out_weight, pattern, live):
    y = lax.axis_index("groups")
    x = lax.axis_index("head")
    c = lax.axis_index("sub")
    columns = out_weight.shape[1] // 2
    low, high = halos(keyvals)

    ring = pairs(lambda y, f, x, c: (y, (f + 1) % 4 if x == 0 else (f - 1) % 4, x, c))
    sibling = pairs(lambda y, f, x, c: (y, f, x, 1 - c))
    mine = lax.dynamic_slice_in_dim(out_weight, y * columns, columns, axis=1)
    held = [mine]
    for _ in range(3):
        held.append(send(held[-1], ring))
    other = [send(w, sibling) for w in held]

    attended = attend(queries, keyvals, low, high, pattern, live)
    first = send(
        attended,
        pairs(lambda y, f, x, c: (1 - y, f, x, c) if c == y else (y, f, x, 1 - c)),
    )
    second = send(
        attended,
        pairs(lambda y, f, x, c: (1 - y, f, x, 1 - c), lambda y, f, x, c: c != y),
    )
    here = y == c
    rows_own = jnp.where(here, attended, first)
    rows_sib = jnp.where(here, first, second)

    def sums(k):
        total = jnp.dot(rows_own, held[k], preferred_element_type=jnp.float32)
        total = total + jnp.dot(rows_sib, other[k], preferred_element_type=jnp.float32)
        return total.astype(jnp.bfloat16)

    s0, s1, s2, s3 = [sums(k) for k in range(4)]
    left = x == 0
    mixed = (jnp.where(left, s0, s2), jnp.where(left, s2, s0))
    direct, crossed = [], []
    for array, steps in ((s1, (1, 1)), (mixed[0], (0, 2)), (mixed[1], (2, 0)), (s3, (3, 3))):
        direct.append(send(array, to_owner(steps, 0)))
        crossed.append(send(array, to_owner(steps, 1)))
    return finish(direct, crossed, residual_in, gate, jnp.reshape(y, (1,)))


def solution(mesh):
    sizes = tuple(mesh.shape[axis] for axis in AXES)
    in_specs = (
        P(("groups", "frame"), ("head", "sub")),
        P(None, ("groups", "frame"), ("head", "sub")),
        P(("groups", "frame"), ("head", "sub")),
        P(("groups", "head", "sub")),
        P(("head", "sub"), "frame"),
        P(("groups", "frame"), None),
        P(("groups", "frame")),
    )
    return jax.shard_map(
        ringed if sizes == (2, 4, 2, 2) else plain,
        mesh=mesh,
        in_specs=in_specs,
        out_specs=P(("groups", "frame"), ("head", "sub")),
        check_vma=False,
    )
```

time: 205 us -> 136 us (0.66)
  the two profiles are of different devices: /device:TPU:8 before, /device:TPU:12 now
where the time goes in v1:
time: 136 us; the launch traced here: 135 us
  waiting for transfers between devices  56.6 us (42%)
  starting transfers between devices  50.1 us (37%)
  Pallas kernels  15.3 us (11%)
  matrix products  8.35 us (6%)
  local copies, waits for them, and re-layouts  2.68 us (2%)
  other arithmetic  1.81 us (1%)
    ppermute x17, starting transfers between devices, send(): return lax.ppermute(array, AXES, route)  43 us
    ppermute x17, waiting for transfers between devices, send(): return lax.ppermute(array, AXES, route)  36.3 us
    ppermute x1, waiting for transfers between devices, halos(): lax.ppermute(keyvals, 'frame', forward)  17.7 us
    pallas_call x1, Pallas kernels, attend(): pl.pallas_call(attend_kernel, out_shape=jax.ShapeDtypeStruct((rows, width...  13.1 us
    dot_general x4, matrix products, sums(): total = jnp.dot(rows_own, held[k], preferred_element_type=jnp.float32)  4.72 us
    ppermute x1, starting transfers between devices, halos(): lax.ppermute(keyvals, 'frame', forward)  3.74 us
    dot_general x4, matrix products, sums(): jnp.dot(rows_sib, other[k], preferred_element_type=jnp.float32)  3.63 us
    ppermute x1, starting transfers between devices, halos(): lax.ppermute(keyvals, 'frame', backward)  3.32 us
  transfers between devices with their start and end apart: 19, of which 9 were waited for; matrix products, arithmetic and copies ran while one was open for 8% of the time, Pallas kernels for 10%

profile of v1, /device:TPU:12, one launch (start us, length us, event | category | flops | bytes accessed | tf_op | source)
XLA Modules:
  0.0 135.1 jit_solution(15088115353369770596)
XLA Ops:
  0.0 3.7 %collective-permute-start = (bf16[2,384,640]{2,1,0:T(8,128)(2,1)}, bf16[2,384,640]{2,1,0:T(8,128)(2,1)}, u32[]{:S(2)}, u32[]{:S(2)}) collective-permute-start(bf16[2,384,640]{2,1,0:T(8,128)(2,1)} %own_ref.1), channel_id=1, source_target_pairs={{0,4},{4,8},{8,12},{1,5},{5,9},{9,13},{2,6},{6,10},{10,14},{3,7},{... | collective-permute-start | bytes 2949128 | tf_op jit(solution)/shard_map/ppermute | solution.py:88
  3.8 3.3 %collective-permute-start.1 = (bf16[2,384,640]{2,1,0:T(8,128)(2,1)}, bf16[2,384,640]{2,1,0:T(8,128)(2,1)}, u32[]{:S(2)}, u32[]{:S(2)}) collective-permute-start(bf16[2,384,640]{2,1,0:T(8,128)(2,1)} %own_ref.1), channel_id=1, source_target_pairs={{4,0},{8,4},{12,8},{5,1},{9,5},{13,9},{6,2},{10,6},{14,10},{7,3},{... | collective-permute-start | bytes 2949128 | tf_op jit(solution)/shard_map/ppermute | solution.py:88
  7.1 1.0 constant_dynamic-slice_fusion
  8.1 0.6 collective-permute-start.3
  8.7 0.0 collective-permute-start.7
  8.7 0.7 broadcast_subtract_fusion.ids
  9.4 17.7 %collective-permute-done.low_ref = bf16[2,384,640]{2,1,0:T(8,128)(2,1)} collective-permute-done((bf16[2,384,640]{2,1,0:T(8,128)(2,1)}, bf16[2,384,640]{2,1,0:T(8,128)(2,1)}, u32[]{:S(2)}, u32[]{:S(2)}) %collective-permute-start) | collective-permute-done | bytes 983072 | tf_op jit(solution)/shard_map/ppermute | solution.py:88
  27.1 2.5 %collective-permute-done.1.high_ref = bf16[2,384,640]{2,1,0:T(8,128)(2,1)} collective-permute-done((bf16[2,384,640]{2,1,0:T(8,128)(2,1)}, bf16[2,384,640]{2,1,0:T(8,128)(2,1)}, u32[]{:S(2)}, u32[]{:S(2)}) %collective-permute-start.1) | collective-permute-done | bytes 983072 | tf_op jit(solution)/shard_map/ppermute | solution.py:88
  29.6 1.0 copy-done.3
  30.7 0.7 copy-done.4
  31.3 13.1 %attend.1 = bf16[384,640]{1,0:T(8,128)(2,1)S(1)} custom-call(s32[6,8]{1,0:T(8,128)S(1)} %broadcast_subtract_fusion.ids, s32[6]{0:T(128)S(1)} %copy-done.4, bf16[384,640]{1,0:T(8,128)(2,1)S(1)} %copy-done.3, bf16[2,384,640]{2,1,0:T(8,128)(2,1)S(1)} %copy-done.2, bf16[2,384,640]{2,1,0:T(8,128)(2,1)} %collective-permute-done.low_ref, ...), custom_call_target="tpu_custom_call" | custom-call | flops 503316480 | bytes 3932160 | tf_op jit(solution)/shard_map/attend/pallas_call | solution.py:65
  44.4 0.0 collective-permute-start.2
  44.4 2.5 %collective-permute-start.4 = (bf16[384,640]{1,0:T(8,128)(2,1)S(1)}, bf16[384,640]{1,0:T(8,128)(2,1)}, u32[]{:S(2)}, u32[]{:S(2)}) collective-permute-start(bf16[384,640]{1,0:T(8,128)(2,1)S(1)} %attend.1), channel_id=1, source_target_pairs={{1,16},{3,18},{5,20},{7,22},{9,24},{11,26},{13,28},{15,30},{16,1},... | collective-permute-start | bytes 1474568 | tf_op jit(solution)/shard_map/ppermute | solution.py:130
  46.9 2.6 %collective-permute-start.8 = (bf16[640,640]{1,0:T(8,128)(2,1)}, bf16[640,640]{1,0:T(8,128)(2,1)S(1)}, u32[]{:S(2)}, u32[]{:S(2)}) collective-permute-start(bf16[640,640]{1,0:T(8,128)(2,1)} %collective-permute-done.3), channel_id=1, source_target_pairs={{0,4},{1,5},{2,14},{3,15},{4,8},{5,9},{6,2},{7,3},{8,12},{9,13},{1... | collective-permute-start | bytes 2457608 | tf_op jit(solution)/shard_map/ppermute | solution.py:130
  49.6 7.5 %collective-permute-done.2 = bf16[384,640]{1,0:T(8,128)(2,1)S(1)} collective-permute-done((bf16[384,640]{1,0:T(8,128)(2,1)S(1)}, bf16[384,640]{1,0:T(8,128)(2,1)S(1)}, u32[]{:S(2)}, u32[]{:S(2)}) %collective-permute-start.2) | collective-permute-done | bytes 491552 | tf_op jit(solution)/shard_map/ppermute | solution.py:130
  57.1 1.5 %collective-permute-done.4 = bf16[384,640]{1,0:T(8,128)(2,1)} collective-permute-done((bf16[384,640]{1,0:T(8,128)(2,1)S(1)}, bf16[384,640]{1,0:T(8,128)(2,1)}, u32[]{:S(2)}, u32[]{:S(2)}) %collective-permute-start.4) | collective-permute-done | bytes 491552 | tf_op jit(solution)/shard_map/ppermute | solution.py:130
  58.6 1.1 broadcast_select_fusion.2
  59.7 0.0 collective-permute-done.7
  59.7 1.8 %fusion.5 = f32[384,640]{1,0:T(8,128)S(1)} fusion(bf16[384,640]{1,0:T(8,128)(2,1)S(1)} %get-tuple-element.7, bf16[640,640]{1,0:T(8,128)(2,1)} %collective-permute-done.7), kind=kOutput, calls=%fused_computation.15 | convolution fusion | flops 314572800 | bytes 2293760 | tf_op jit(solution)/shard_map/dot_general | solution.py:194
  61.5 5.0 %collective-permute-done.8 = bf16[640,640]{1,0:T(8,128)(2,1)S(1)} collective-permute-done((bf16[640,640]{1,0:T(8,128)(2,1)}, bf16[640,640]{1,0:T(8,128)(2,1)S(1)}, u32[]{:S(2)}, u32[]{:S(2)}) %collective-permute-start.8) | collective-permute-done | bytes 819232 | tf_op jit(solution)/shard_map/ppermute | solution.py:130
  66.5 0.0 collective-permute-start.12
  66.5 1.8 %fusion.1 = bf16[384,640]{1,0:T(8,128)(2,1)S(1)} fusion(f32[384,640]{1,0:T(8,128)S(1)} %fusion.5, bf16[384,640]{1,0:T(8,128)(2,1)S(1)} %get-tuple-element.8, bf16[640,640]{1,0:T(8,128)(2,1)} %constant_dynamic-slice_fusion), kind=kOutput, calls=%fused_computation.5 | convolution fusion | flops 315064320 | bytes 2785280 | tf_op jit(solution)/shard_map/dot_general | solution.py:193
  68.2 0.1 collective-permute-start.9
  68.3 1.8 %fusion.4 = f32[384,640]{1,0:T(8,128)S(1)} fusion(bf16[384,640]{1,0:T(8,128)(2,1)S(1)} %get-tuple-element.8, bf16[640,640]{1,0:T(8,128)(2,1)} %collective-permute-done.3), kind=kOutput, calls=%fused_computation.14 | convolution fusion | flops 314572800 | bytes 2293760 | tf_op jit(solution)/shard_map/dot_general | solution.py:193
  70.1 0.0 collective-permute-done.5
  70.1 0.6 fusion
  70.7 1.3 collective-permute-start.6
  72.0 6.3 %collective-permute-start.15 = (bf16[384,640]{1,0:T(8,128)(2,1)S(1)}, bf16[384,640]{1,0:T(8,128)(2,1)S(1)}, u32[]{:S(2)}, u32[]{:S(2)}) collective-permute-start(bf16[384,640]{1,0:T(8,128)(2,1)S(1)} %fusion), channel_id=1, source_target_pairs={{1,19},{3,17},{5,20},{7,22},{9,25},{11,27},{13,30},{15,28},{16,3},... | collective-permute-start | bytes 1474568 | tf_op jit(solution)/shard_map/ppermute | solution.py:130
  78.3 7.8 %collective-permute-done.12 = bf16[640,640]{1,0:T(8,128)(2,1)S(1)} collective-permute-done((bf16[640,640]{1,0:T(8,128)(2,1)S(1)}, bf16[640,640]{1,0:T(8,128)(2,1)S(1)}, u32[]{:S(2)}, u32[]{:S(2)}) %collective-permute-start.12) | collective-permute-done | bytes 819232 | tf_op jit(solution)/shard_map/ppermute | solution.py:130
  86.1 0.6 fusion.6
  86.8 0.0 collective-permute-done.9
  86.8 0.7 broadcast_select_fusion
  87.4 0.7 collective-permute-start.10
  88.1 6.3 %collective-permute-start.16 = (bf16[384,640]{1,0:T(8,128)(2,1)S(1)}, bf16[384,640]{1,0:T(8,128)(2,1)S(1)}, u32[]{:S(2)}, u32[]{:S(2)}) collective-permute-start(bf16[384,640]{1,0:T(8,128)(2,1)S(1)} %get-tuple-element.6), channel_id=1, source_target_pairs={{1,16},{3,18},{5,21},{7,23},{9,26},{11,24},{13,31},{15,29},{16,0},... | collective-permute-start | bytes 1474568 | tf_op jit(solution)/shard_map/ppermute | solution.py:130
  94.5 0.6 fusion.7
  95.1 0.0 copy-start.5
  95.1 0.0 copy-start.1
  95.1 0.8 collective-permute-start.11
  96.0 0.6 fusion.3
  96.6 0.0 collective-permute-done.6.refs_0_
  96.6 16.5 %collective-permute-start.17 = (bf16[384,640]{1,0:T(8,128)(2,1)S(1)}, bf16[384,640]{1,0:T(8,128)(2,1)S(1)}, u32[]{:S(2)}, u32[]{:S(2)}) collective-permute-start(bf16[384,640]{1,0:T(8,128)(2,1)S(1)} %get-tuple-element.5), channel_id=1, source_target_pairs={{1,18},{3,16},{5,23},{7,21},{9,24},{11,26},{13,29},{15,31},{16,2},... | collective-permute-start | bytes 1474568 | tf_op jit(solution)/shard_map/ppermute | solution.py:130
  113.1 0.0 collective-permute-done.15.refs_4_
  113.1 1.3 collective-permute-start.14
  114.4 4.0 %collective-permute-start.18 = (bf16[384,640]{1,0:T(8,128)(2,1)S(1)}, bf16[384,640]{1,0:T(8,128)(2,1)S(1)}, u32[]{:S(2)}, u32[]{:S(2)}) collective-permute-start(bf16[384,640]{1,0:T(8,128)(2,1)S(1)} %fusion.3), channel_id=1, source_target_pairs={{1,17},{3,19},{5,22},{7,20},{9,27},{11,25},{13,28},{15,30},{16,1},... | collective-permute-start | bytes 1474568 | tf_op jit(solution)/shard_map/ppermute | solution.py:130
  118.4 5.5 %collective-permute-done.17.refs_6_ = bf16[384,640]{1,0:T(8,128)(2,1)S(1)} collective-permute-done((bf16[384,640]{1,0:T(8,128)(2,1)S(1)}, bf16[384,640]{1,0:T(8,128)(2,1)S(1)}, u32[]{:S(2)}, u32[]{:S(2)}) %collective-permute-start.17) | collective-permute-done | bytes 491552 | tf_op jit(solution)/shard_map/ppermute | solution.py:130
  123.9 4.6 %collective-permute-done.14.refs_3_ = bf16[384,640]{1,0:T(8,128)(2,1)S(1)} collective-permute-done((bf16[384,640]{1,0:T(8,128)(2,1)S(1)}, bf16[384,640]{1,0:T(8,128)(2,1)S(1)}, u32[]{:S(2)}, u32[]{:S(2)}) %collective-permute-start.14) | collective-permute-done | bytes 491552 | tf_op jit(solution)/shard_map/ppermute | solution.py:130
  128.5 4.3 %collective-permute-done.18.refs_7_ = bf16[384,640]{1,0:T(8,128)(2,1)S(1)} collective-permute-done((bf16[384,640]{1,0:T(8,128)(2,1)S(1)}, bf16[384,640]{1,0:T(8,128)(2,1)S(1)}, u32[]{:S(2)}, u32[]{:S(2)}) %collective-permute-start.18) | collective-permute-done | bytes 491552 | tf_op jit(solution)/shard_map/ppermute | solution.py:130
  132.9 2.2 %finish.1 = f32[384,1280]{1,0:T(8,128)} custom-call(s32[1]{0:T(128)} %bitcast.spot, bf16[384,640]{1,0:T(8,128)(2,1)S(1)} %collective-permute-done.6.refs_0_, bf16[384,640]{1,0:T(8,128)(2,1)S(1)} %collective-permute-done.10.refs_1_, bf16[384,640]{1,0:T(8,128)(2,1)S(1)} %collective-permute-done.11.refs_2_, ...), custom_call_target="tpu_custom_call" | custom-call | tf_op jit(solution)/shard_map/finish/pallas_call | solution.py:151
  (16 shorter events, 0.0 us)
Async XLA Ops:
  0.0 7.1 %copy-start = (bf16[640,1280]{1,0:T(8,128)(2,1)S(1)}, bf16[640,1280]{1,0:T(8,128)(2,1)}, u32[]{:S(2)}) copy-start(bf16[640,1280]{1,0:T(8,128)(2,1)} %param.11) | copy-start | bytes 4915204
  0.0 29.6 %copy-start.2 = (bf16[2,384,640]{2,1,0:T(8,128)(2,1)S(1)}, bf16[2,384,640]{2,1,0:T(8,128)(2,1)}, u32[]{:S(2)}) copy-start(bf16[2,384,640]{2,1,0:T(8,128)(2,1)} %own_ref.1) | copy-start | bytes 2949124
  0.0 27.1 %collective-permute-start = (bf16[2,384,640]{2,1,0:T(8,128)(2,1)}, bf16[2,384,640]{2,1,0:T(8,128)(2,1)}, u32[]{:S(2)}, u32[]{:S(2)}) collective-permute-start(bf16[2,384,640]{2,1,0:T(8,128)(2,1)} %own_ref.1), channel_id=1, source_target_pairs={{0,4},{4,8},{8,12},{1,5},{5,9},{9,13},{2,6},{6,10},{10,14},{3,7},{... | collective-permute-start | bytes 2949128 | tf_op jit(solution)/shard_map/ppermute | solution.py:88
  3.8 25.9 %collective-permute-start.1 = (bf16[2,384,640]{2,1,0:T(8,128)(2,1)}, bf16[2,384,640]{2,1,0:T(8,128)(2,1)}, u32[]{:S(2)}, u32[]{:S(2)}) collective-permute-start(bf16[2,384,640]{2,1,0:T(8,128)(2,1)} %own_ref.1), channel_id=1, source_target_pairs={{4,0},{8,4},{12,8},{5,1},{9,5},{13,9},{6,2},{10,6},{14,10},{7,3},{... | collective-permute-start | bytes 2949128 | tf_op jit(solution)/shard_map/ppermute | solution.py:88
  8.1 38.9 %collective-permute-start.3 = (bf16[640,640]{1,0:T(8,128)(2,1)}, bf16[640,640]{1,0:T(8,128)(2,1)}, u32[]{:S(2)}, u32[]{:S(2)}) collective-permute-start(bf16[640,640]{1,0:T(8,128)(2,1)} %constant_dynamic-slice_fusion), channel_id=1, source_target_pairs={{0,4},{1,5},{2,14},{3,15},{4,8},{5,9},{6,2},{7,3},{8,12},{9,13},{1... | collective-permute-start | bytes 2457608 | tf_op jit(solution)/shard_map/ppermute | solution.py:130
  8.7 51.1 %collective-permute-start.7 = (bf16[640,640]{1,0:T(8,128)(2,1)}, bf16[640,640]{1,0:T(8,128)(2,1)}, u32[]{:S(2)}, u32[]{:S(2)}) collective-permute-start(bf16[640,640]{1,0:T(8,128)(2,1)} %constant_dynamic-slice_fusion), channel_id=1, source_target_pairs={{0,1},{1,0},{2,3},{3,2},{4,5},{5,4},{6,7},{7,6},{8,9},{9,8},{10,11... | collective-permute-start | bytes 2457608 | tf_op jit(solution)/shard_map/ppermute | solution.py:130
  29.6 1.0 copy-start.3
  30.7 0.7 copy-start.4
  44.4 12.7 %collective-permute-start.2 = (bf16[384,640]{1,0:T(8,128)(2,1)S(1)}, bf16[384,640]{1,0:T(8,128)(2,1)S(1)}, u32[]{:S(2)}, u32[]{:S(2)}) collective-permute-start(bf16[384,640]{1,0:T(8,128)(2,1)S(1)} %attend.1), channel_id=1, source_target_pairs={{0,16},{1,0},{2,18},{3,2},{4,20},{5,4},{6,22},{7,6},{8,24},{9,8},{... | collective-permute-start | bytes 1474568 | tf_op jit(solution)/shard_map/ppermute | solution.py:130
  44.4 14.2 %collective-permute-start.4 = (bf16[384,640]{1,0:T(8,128)(2,1)S(1)}, bf16[384,640]{1,0:T(8,128)(2,1)}, u32[]{:S(2)}, u32[]{:S(2)}) collective-permute-start(bf16[384,640]{1,0:T(8,128)(2,1)S(1)} %attend.1), channel_id=1, source_target_pairs={{1,16},{3,18},{5,20},{7,22},{9,24},{11,26},{13,28},{15,30},{16,1},... | collective-permute-start | bytes 1474568 | tf_op jit(solution)/shard_map/ppermute | solution.py:130
  46.9 19.5 %collective-permute-start.8 = (bf16[640,640]{1,0:T(8,128)(2,1)}, bf16[640,640]{1,0:T(8,128)(2,1)S(1)}, u32[]{:S(2)}, u32[]{:S(2)}) collective-permute-start(bf16[640,640]{1,0:T(8,128)(2,1)} %collective-permute-done.3), channel_id=1, source_target_pairs={{0,4},{1,5},{2,14},{3,15},{4,8},{5,9},{6,2},{7,3},{8,12},{9,13},{1... | collective-permute-start | bytes 2457608 | tf_op jit(solution)/shard_map/ppermute | solution.py:130
  49.6 20.5 %collective-permute-start.5 = (bf16[640,640]{1,0:T(8,128)(2,1)}, bf16[640,640]{1,0:T(8,128)(2,1)S(1)}, u32[]{:S(2)}, u32[]{:S(2)}) collective-permute-start(bf16[640,640]{1,0:T(8,128)(2,1)} %collective-permute-done.3), channel_id=1, source_target_pairs={{0,1},{1,0},{2,3},{3,2},{4,5},{5,4},{6,7},{7,6},{8,9},{9,8},{10,11... | collective-permute-start | bytes 2457608 | tf_op jit(solution)/shard_map/ppermute | solution.py:130
  66.5 19.7 %collective-permute-start.12 = (bf16[640,640]{1,0:T(8,128)(2,1)S(1)}, bf16[640,640]{1,0:T(8,128)(2,1)S(1)}, u32[]{:S(2)}, u32[]{:S(2)}) collective-permute-start(bf16[640,640]{1,0:T(8,128)(2,1)S(1)} %collective-permute-done.8), channel_id=1, source_target_pairs={{0,4},{1,5},{2,14},{3,15},{4,8},{5,9},{6,2},{7,3},{8,12},{9,13},{1... | collective-permute-start | bytes 2457608 | tf_op jit(solution)/shard_map/ppermute | solution.py:130
  68.2 18.5 %collective-permute-start.9 = (bf16[640,640]{1,0:T(8,128)(2,1)S(1)}, bf16[640,640]{1,0:T(8,128)(2,1)S(1)}, u32[]{:S(2)}, u32[]{:S(2)}) collective-permute-start(bf16[640,640]{1,0:T(8,128)(2,1)S(1)} %collective-permute-done.8), channel_id=1, source_target_pairs={{0,1},{1,0},{2,3},{3,2},{4,5},{5,4},{6,7},{7,6},{8,9},{9,8},{10,11... | collective-permute-start | bytes 2457608 | tf_op jit(solution)/shard_map/ppermute | solution.py:130
  70.7 25.9 %collective-permute-start.6 = (bf16[384,640]{1,0:T(8,128)(2,1)S(1)}, bf16[384,640]{1,0:T(8,128)(2,1)S(1)}, u32[]{:S(2)}, u32[]{:S(2)}) collective-permute-start(bf16[384,640]{1,0:T(8,128)(2,1)S(1)} %fusion), channel_id=1, source_target_pairs={{0,3},{2,1},{4,4},{6,6},{8,9},{10,11},{12,14},{14,12},{17,19},{19,... | collective-permute-start | bytes 1474568 | tf_op jit(solution)/shard_map/ppermute | solution.py:130
  72.0 41.0 %collective-permute-start.15 = (bf16[384,640]{1,0:T(8,128)(2,1)S(1)}, bf16[384,640]{1,0:T(8,128)(2,1)S(1)}, u32[]{:S(2)}, u32[]{:S(2)}) collective-permute-start(bf16[384,640]{1,0:T(8,128)(2,1)S(1)} %fusion), channel_id=1, source_target_pairs={{1,19},{3,17},{5,20},{7,22},{9,25},{11,27},{13,30},{15,28},{16,3},... | collective-permute-start | bytes 1474568 | tf_op jit(solution)/shard_map/ppermute | solution.py:130
  86.1 9.0 %collective-permute-start.13 = (bf16[640,640]{1,0:T(8,128)(2,1)S(1)}, bf16[640,640]{1,0:T(8,128)(2,1)S(1)}, u32[]{:S(2)}, u32[]{:S(2)}) collective-permute-start(bf16[640,640]{1,0:T(8,128)(2,1)S(1)} %collective-permute-done.12), channel_id=1, source_target_pairs={{0,1},{1,0},{2,3},{3,2},{4,5},{5,4},{6,7},{7,6},{8,9},{9,8},{10,11... | collective-permute-start | bytes 2457608 | tf_op jit(solution)/shard_map/ppermute | solution.py:130
  87.4 26.9 %collective-permute-start.10 = (bf16[384,640]{1,0:T(8,128)(2,1)S(1)}, bf16[384,640]{1,0:T(8,128)(2,1)S(1)}, u32[]{:S(2)}, u32[]{:S(2)}) collective-permute-start(bf16[384,640]{1,0:T(8,128)(2,1)S(1)} %get-tuple-element.6), channel_id=1, source_target_pairs={{0,0},{2,2},{4,5},{6,7},{8,10},{10,8},{12,15},{14,13},{17,16},{19,... | collective-permute-start | bytes 1474568 | tf_op jit(solution)/shard_map/ppermute | solution.py:130
  88.1 30.2 %collective-permute-start.16 = (bf16[384,640]{1,0:T(8,128)(2,1)S(1)}, bf16[384,640]{1,0:T(8,128)(2,1)S(1)}, u32[]{:S(2)}, u32[]{:S(2)}) collective-permute-start(bf16[384,640]{1,0:T(8,128)(2,1)S(1)} %get-tuple-element.6), channel_id=1, source_target_pairs={{1,16},{3,18},{5,21},{7,23},{9,26},{11,24},{13,31},{15,29},{16,0},... | collective-permute-start | bytes 1474568 | tf_op jit(solution)/shard_map/ppermute | solution.py:130
  95.1 23.2 %copy-start.5 = (f32[1280]{0:T(1024)S(1)}, f32[1280]{0:T(1024)}, u32[]{:S(2)}) copy-start(f32[1280]{0:T(1024)} %param.10) | copy-start | bytes 15364
  95.1 37.8 %copy-start.1 = (f32[384,1280]{1,0:T(8,128)S(1)}, f32[384,1280]{1,0:T(8,128)}, u32[]{:S(2)}) copy-start(f32[384,1280]{1,0:T(8,128)} %refs_8_.1) | copy-start | bytes 5898244
  95.1 23.2 %collective-permute-start.11 = (bf16[384,640]{1,0:T(8,128)(2,1)S(1)}, bf16[384,640]{1,0:T(8,128)(2,1)S(1)}, u32[]{:S(2)}, u32[]{:S(2)}) collective-permute-start(bf16[384,640]{1,0:T(8,128)(2,1)S(1)} %get-tuple-element.5), channel_id=1, source_target_pairs={{0,2},{2,0},{4,7},{6,5},{8,8},{10,10},{12,13},{14,15},{17,18},{19,... | collective-permute-start | bytes 1474568 | tf_op jit(solution)/shard_map/ppermute | solution.py:130
  96.6 27.3 %collective-permute-start.17 = (bf16[384,640]{1,0:T(8,128)(2,1)S(1)}, bf16[384,640]{1,0:T(8,128)(2,1)S(1)}, u32[]{:S(2)}, u32[]{:S(2)}) collective-permute-start(bf16[384,640]{1,0:T(8,128)(2,1)S(1)} %get-tuple-element.5), channel_id=1, source_target_pairs={{1,18},{3,16},{5,23},{7,21},{9,24},{11,26},{13,29},{15,31},{16,2},... | collective-permute-start | bytes 1474568 | tf_op jit(solution)/shard_map/ppermute | solution.py:130
  113.1 15.5 %collective-permute-start.14 = (bf16[384,640]{1,0:T(8,128)(2,1)S(1)}, bf16[384,640]{1,0:T(8,128)(2,1)S(1)}, u32[]{:S(2)}, u32[]{:S(2)}) collective-permute-start(bf16[384,640]{1,0:T(8,128)(2,1)S(1)} %fusion.3), channel_id=1, source_target_pairs={{0,1},{2,3},{4,6},{6,4},{8,11},{10,9},{12,12},{14,14},{17,17},{19,... | collective-permute-start | bytes 1474568 | tf_op jit(solution)/shard_map/ppermute | solution.py:130
  114.4 18.5 %collective-permute-start.18 = (bf16[384,640]{1,0:T(8,128)(2,1)S(1)}, bf16[384,640]{1,0:T(8,128)(2,1)S(1)}, u32[]{:S(2)}, u32[]{:S(2)}) collective-permute-start(bf16[384,640]{1,0:T(8,128)(2,1)S(1)} %fusion.3), channel_id=1, source_target_pairs={{1,17},{3,19},{5,22},{7,20},{9,27},{11,25},{13,28},{15,30},{16,1},... | collective-permute-start | bytes 1474568 | tf_op jit(solution)/shard_map/ppermute | solution.py:130

commit v2 on v1

v2 whole, which is shorter than its diff:
```python
import math

import jax
import jax.numpy as jnp
from jax import lax
from jax.experimental import pallas as pl
from jax.experimental.pallas import tpu as pltpu
from jax.sharding import PartitionSpec as P

HEAD_DIM = 128
TILES_F = 6
KSEL = 8
AXES = ("groups", "frame", "head", "sub")
MIB = 1 << 20


def attend_kernel(ids, live, q_ref, own_ref, low_ref, high_ref, out_ref, kv, sems):
    tiles = ids.shape[0]
    rows, width = q_ref.shape
    tile = rows // tiles
    heads = width // HEAD_DIM
    copies = [
        pltpu.make_async_copy(src, kv.at[:, pl.ds(i * rows, rows), :], sems.at[i])
        for i, src in enumerate((low_ref, own_ref, high_ref))
    ]
    for copy in copies:
        copy.start()
    for copy in copies:
        copy.wait()
    scale = math.log2(math.e) / math.sqrt(HEAD_DIM)
    key_row = lax.broadcasted_iota(jnp.int32, (KSEL * tile, 1), 0)
    lanes = [slice(h * HEAD_DIM, (h + 1) * HEAD_DIM) for h in range(heads)]

    def one_tile(t, carry):
        row = pl.multiple_of(t * tile, tile)
        starts = [pl.multiple_of(ids[t, s] * tile, tile) for s in range(KSEL)]

        def listed(which, lane):
            return jnp.concatenate([kv[which, pl.ds(s, tile), lane] for s in starts], axis=0)

        scores = jnp.concatenate(
            [
                lax.dot_general(
                    listed(0, lane),
                    q_ref[pl.ds(row, tile), lane],
                    (((1,), (1,)), ((), ())),
                    preferred_element_type=jnp.float32,
                )
                for lane in lanes
            ],
            axis=1,
        )
        scores = jnp.where(key_row < live[t] * tile, scores * scale, -1e30)
        expo = jnp.exp2(scores - jnp.max(scores, axis=0, keepdims=True))
        probs = (expo * (1.0 / jnp.sum(expo, axis=0, keepdims=True))).astype(jnp.bfloat16)
        for h, lane in enumerate(lanes):
            out_ref[pl.ds(row, tile), lane] = lax.dot_general(
                probs[:, h * tile : (h + 1) * tile],
                listed(1, lane),
                (((0,), (0,)), ((), ())),
                preferred_element_type=jnp.float32,
            ).astype(jnp.bfloat16)
        return carry

    lax.fori_loop(0, tiles, one_tile, 0)


def attend(queries, keyvals, low, high, pattern, live):
    rows, width = queries.shape
    tile_count = pattern.shape[0]
    local_ids = pattern - (lax.axis_index("frame") * tile_count - TILES_F)
    local_ids = jnp.clip(local_ids, 0, 3 * tile_count - 1)
    anywhere = pl.BlockSpec(memory_space=pl.ANY)
    scalars = pl.BlockSpec(memory_space=pltpu.SMEM)
    whole = pl.BlockSpec(memory_space=pltpu.VMEM)
    return pl.pallas_call(
        attend_kernel,
        out_shape=jax.ShapeDtypeStruct((rows, width), jnp.bfloat16),
        in_specs=[scalars, scalars, whole, anywhere, anywhere, anywhere],
        out_specs=whole,
        scratch_shapes=[
            pltpu.VMEM((2, 3 * rows, width), jnp.bfloat16),
            pltpu.SemaphoreType.DMA((3,)),
        ],
        compiler_params=pltpu.CompilerParams(vmem_limit_bytes=24 * MIB),
        cost_estimate=pl.CostEstimate(flops=1, bytes_accessed=1, transcendentals=0),
        name="attend",
    )(local_ids, live, queries, keyvals, low, high)


def halos(keyvals):
    count = lax.axis_size("frame")
    forward = [(i, i + 1) for i in range(count - 1)]
    backward = [(b, a) for a, b in forward]
    return lax.ppermute(keyvals, "frame", forward), lax.ppermute(keyvals, "frame", backward)


def plain(queries, keyvals, residual_in, gate, out_weight, pattern, live):
    low, high = halos(keyvals)
    attended = attend(queries, keyvals, low, high, pattern, live)
    weights = lax.all_gather(out_weight, "frame", axis=1, tiled=True)
    partial_rows = jnp.dot(attended, weights, preferred_element_type=jnp.float32)
    summed = lax.psum_scatter(
        partial_rows.astype(jnp.bfloat16), ("head", "sub"), scatter_dimension=1, tiled=True
    ).astype(jnp.float32)
    return residual_in + gate[None, :] * summed


def place(y, f, x, c):
    return ((y * 4 + f) * 2 + x) * 2 + c


def pairs(move, keep=lambda y, f, x, c: True):
    found = []
    for y in range(2):
        for f in range(4):
            for x in range(2):
                for c in range(2):
                    if keep(y, f, x, c):
                        found.append((place(y, f, x, c), place(*move(y, f, x, c))))
    return found


def block_at(k, f, x):
    return (f - k) % 4 if x == 0 else (f + k) % 4


def to_owner(steps, crosses):
    def move(y, f, x, c):
        g = block_at(steps[y ^ c][x], f, x)
        return c, f, g // 2, g % 2

    return pairs(move, lambda y, f, x, c: (y ^ c) in crosses)


def send(array, route, name):
    with jax.named_scope(name):
        return lax.ppermute(array, AXES, route)


def after(value, *earlier):
    return lax.optimization_barrier((value, *earlier))[0]


def finish_kernel(spot, *refs):
    residual, gate, out = refs[-3:]
    half = residual.shape[1] // 2
    count = (len(refs) - 3) // 2
    for cross, parts in ((0, refs[:count]), (1, refs[count : 2 * count])):
        lanes = pl.ds(pl.multiple_of((spot[0] ^ cross) * half, half), half)
        total = parts[0][...].astype(jnp.float32)
        for part in parts[1:]:
            total = total + part[...].astype(jnp.float32)
        out[:, lanes] = residual[:, lanes] + gate[:, lanes] * total


def finish(direct, crossed, residual_in, gate, spot):
    rows, width = residual_in.shape
    step = 128
    parts = [pl.BlockSpec((step, part.shape[1]), lambda i: (i, 0)) for part in direct + crossed]
    wide = pl.BlockSpec((step, width), lambda i: (i, 0))
    return pl.pallas_call(
        finish_kernel,
        grid=(rows // step,),
        out_shape=jax.ShapeDtypeStruct((rows, width), jnp.float32),
        in_specs=[pl.BlockSpec(memory_space=pltpu.SMEM)]
        + parts
        + [wide, pl.BlockSpec((1, width), lambda i: (0, 0))],
        out_specs=wide,
        compiler_params=pltpu.CompilerParams(vmem_limit_bytes=32 * MIB),
        name="finish",
    )(spot, *direct, *crossed, residual_in, gate[None, :])


def ringed(queries, keyvals, residual_in, gate, out_weight, pattern, live):
    y = lax.axis_index("groups")
    x = lax.axis_index("head")
    c = lax.axis_index("sub")
    half = out_weight.shape[1] // 2
    low, high = halos(keyvals)

    ring = pairs(lambda y, f, x, c: (y, (f + 1) % 4 if x == 0 else (f - 1) % 4, x, c))
    here = y == c
    left = x == 0

    def sums(weights, name):
        def product(rows):
            return jnp.dot(rows, weights, preferred_element_type=jnp.float32)

        swapped = send(
            product(given).astype(jnp.bfloat16),
            pairs(lambda y, f, x, c: (y, f, x, 1 - c)),
            "core_swap_" + name,
        )
        return (product(kept) + swapped.astype(jnp.float32)).astype(jnp.bfloat16)

    def to_owners(array, steps, name):
        return [
            send(array, to_owner((steps,) * 2, (0,)), "sums_" + name),
            send(array, to_owner((steps,) * 2, (1,)), "sums_cross_" + name),
        ]

    w0 = lax.dynamic_slice_in_dim(out_weight, y * half, half, axis=1)
    w1 = send(after(w0, low), ring, "ring_1")
    attended = attend(queries, keyvals, low, high, pattern, live)
    w2 = send(w1, ring, "ring_2")
    others = send(attended, pairs(lambda y, f, x, c: (1 - y, f, x, c)), "rows_of_other_group")
    kept = jnp.where(here, attended, others)
    given = jnp.where(here, others, attended)
    s1 = sums(w1, "1")
    middle = to_owners(s1, (1, 1), "1")
    s0 = sums(w0, "0")
    w2 = after(w2, s0, s1)
    w3 = send(w2, ring, "ring_3")
    w2, *middle = lax.optimization_barrier((w2, *middle))
    s2 = sums(w2, "2")
    low_sum, high_sum = jnp.where(left, s0, s2), jnp.where(left, s2, s0)
    early = to_owners(low_sum, (0, 2), "02") + to_owners(high_sum, (2, 0), "20")
    w3, *early = lax.optimization_barrier((w3, *early))
    s3 = sums(w3, "3")
    last = to_owners(s3, (3, 3), "3")
    return finish(
        [middle[0], early[0], early[2], last[0]],
        [middle[1], early[1], early[3], last[1]],
        residual_in,
        gate,
        jnp.reshape(y, (1,)),
    )


def solution(mesh):
    sizes = tuple(mesh.shape[axis] for axis in AXES)
    in_specs = (
        P(("groups", "frame"), ("head", "sub")),
        P(None, ("groups", "frame"), ("head", "sub")),
        P(("groups", "frame"), ("head", "sub")),
        P(("groups", "head", "sub")),
        P(("head", "sub"), "frame"),
        P(("groups", "frame"), None),
        P(("groups", "frame")),
    )
    return jax.shard_map(
        ringed if sizes == (2, 4, 2, 2) else plain,
        mesh=mesh,
        in_specs=in_specs,
        out_specs=P(("groups", "frame"), ("head", "sub")),
        check_vma=False,
    )
```

time: 136 us -> 123 us (0.904)
  the two profiles are of different devices: /device:TPU:12 before, /device:TPU:8 now
where the time goes in v2:
time: 123 us; the launch traced here: 121 us
  waiting for transfers between devices  63.2 us (51%)
  starting transfers between devices  29.7 us (24%)
  matrix products  16 us (13%)
  Pallas kernels  9.81 us (8%)
  local copies, waits for them, and re-layouts  1.66 us (1%)
    ppermute x16, waiting for transfers between devices, send(): return lax.ppermute(array, AXES, route)  43.9 us
    ppermute x16, starting transfers between devices, send(): return lax.ppermute(array, AXES, route)  22.7 us
    ppermute x1, waiting for transfers between devices, halos(): lax.ppermute(keyvals, 'frame', forward)  17.9 us
    dot_general x8, matrix products, product(): return jnp.dot(rows, weights, preferred_element_type=jnp.float32)  16 us
    pallas_call x1, Pallas kernels, attend(): pl.pallas_call(attend_kernel, out_shape=jax.ShapeDtypeStruct((rows, width...  7.65 us
    ppermute x1, starting transfers between devices, halos(): lax.ppermute(keyvals, 'frame', forward)  3.74 us
    ppermute x1, starting transfers between devices, halos(): lax.ppermute(keyvals, 'frame', backward)  3.32 us
  transfers between devices with their start and end apart: 18, of which 9 were waited for; matrix products, arithmetic and copies ran while one was open for 8% of the time, Pallas kernels for 6%

profile of v2, /device:TPU:8, one launch (start us, length us, event | category | flops | bytes accessed | tf_op | source)
XLA Modules:
  0.0 121.4 jit_solution(15339094753403367635)
XLA Ops:
  0.0 3.7 %collective-permute-start = (bf16[2,384,640]{2,1,0:T(8,128)(2,1)}, bf16[2,384,640]{2,1,0:T(8,128)(2,1)}, u32[]{:S(2)}, u32[]{:S(2)}) collective-permute-start(bf16[2,384,640]{2,1,0:T(8,128)(2,1)} %own_ref.1), channel_id=1, source_target_pairs={{0,4},{4,8},{8,12},{1,5},{5,9},{9,13},{2,6},{6,10},{10,14},{3,7},{... | collective-permute-start | bytes 2949128 | tf_op jit(solution)/shard_map/ppermute | solution.py:95
  3.8 3.3 %collective-permute-start.3 = (bf16[2,384,640]{2,1,0:T(8,128)(2,1)}, bf16[2,384,640]{2,1,0:T(8,128)(2,1)}, u32[]{:S(2)}, u32[]{:S(2)}) collective-permute-start(bf16[2,384,640]{2,1,0:T(8,128)(2,1)} %own_ref.1), channel_id=1, source_target_pairs={{4,0},{8,4},{12,8},{5,1},{9,5},{13,9},{6,2},{10,6},{14,10},{7,3},{... | collective-permute-start | bytes 2949128 | tf_op jit(solution)/shard_map/ppermute | solution.py:95
  7.1 1.0 constant_dynamic-slice_fusion
  8.1 17.9 %collective-permute-done.low_ref = bf16[2,384,640]{2,1,0:T(8,128)(2,1)} collective-permute-done((bf16[2,384,640]{2,1,0:T(8,128)(2,1)}, bf16[2,384,640]{2,1,0:T(8,128)(2,1)}, u32[]{:S(2)}, u32[]{:S(2)}) %collective-permute-start) | collective-permute-done | bytes 983072 | tf_op jit(solution)/shard_map/ppermute | solution.py:95
  26.0 1.6 %collective-permute-start.1 = (bf16[640,640]{1,0:T(8,128)(2,1)}, bf16[640,640]{1,0:T(8,128)(2,1)}, u32[]{:S(2)}, u32[]{:S(2)}) collective-permute-start(bf16[640,640]{1,0:T(8,128)(2,1)} %constant_dynamic-slice_fusion), channel_id=1, source_target_pairs={{0,4},{1,5},{2,14},{3,15},{4,8},{5,9},{6,2},{7,3},{8,12},{9,13},{1... | collective-permute-start | bytes 2457608 | tf_op jit(solution)/shard_map/ring_1/ppermute | solution.py:138
  27.5 0.7 subtract_clamp_fusion.ids
  28.2 1.4 %collective-permute-done.3.high_ref = bf16[2,384,640]{2,1,0:T(8,128)(2,1)} collective-permute-done((bf16[2,384,640]{2,1,0:T(8,128)(2,1)}, bf16[2,384,640]{2,1,0:T(8,128)(2,1)}, u32[]{:S(2)}, u32[]{:S(2)}) %collective-permute-start.3) | collective-permute-done | bytes 983072 | tf_op jit(solution)/shard_map/ppermute | solution.py:95
  29.6 0.7 copy-done.4
  30.3 7.7 %attend.1 = bf16[384,640]{1,0:T(8,128)(2,1)S(1)} custom-call(s32[6,8]{1,0:T(8,128)S(1)} %subtract_clamp_fusion.ids, s32[6]{0:T(128)S(1)} %copy-done.4, bf16[384,640]{1,0:T(8,128)(2,1)S(1)} %copy-done.3, bf16[2,384,640]{2,1,0:T(8,128)(2,1)S(1)} %copy-done.2, bf16[2,384,640]{2,1,0:T(8,128)(2,1)} %collective-permute-done.low_ref, ...), custom_call_target="tpu_custom_call" | custom-call | flops 1 | bytes 1 | tf_op jit(solution)/shard_map/attend/pallas_call | solution.py:76
  38.0 1.6 %collective-permute-start.4 = (bf16[384,640]{1,0:T(8,128)(2,1)S(1)}, bf16[384,640]{1,0:T(8,128)(2,1)S(1)}, u32[]{:S(2)}, u32[]{:S(2)}) collective-permute-start(bf16[384,640]{1,0:T(8,128)(2,1)S(1)} %attend.1), channel_id=1, source_target_pairs={{0,16},{1,17},{2,18},{3,19},{4,20},{5,21},{6,22},{7,23},{8,24},{9,... | collective-permute-start | bytes 1474568 | tf_op jit(solution)/shard_map/rows_of_other_group/ppermute | solution.py:138
  39.5 9.8 %collective-permute-done.4 = bf16[384,640]{1,0:T(8,128)(2,1)S(1)} collective-permute-done((bf16[384,640]{1,0:T(8,128)(2,1)S(1)}, bf16[384,640]{1,0:T(8,128)(2,1)S(1)}, u32[]{:S(2)}, u32[]{:S(2)}) %collective-permute-start.4) | collective-permute-done | bytes 491552 | tf_op jit(solution)/shard_map/rows_of_other_group/ppermute | solution.py:138
  49.3 0.1 broadcast_select_fusion.2
  49.5 1.9 %convolution_convert_fusion.2 = bf16[384,640]{1,0:T(8,128)(2,1)S(1)} fusion(bf16[384,640]{1,0:T(8,128)(2,1)S(1)} %get-tuple-element.27, bf16[640,640]{1,0:T(8,128)(2,1)} %collective-permute-done.1), kind=kOutput, calls=%fused_computation.6 | convolution fusion | flops 314818560 | bytes 1802240 | tf_op jit(solution)/shard_map/dot_general | solution.py:188
  51.4 0.1 collective-permute-start.6
  51.5 1.6 %collective-permute-start.2 = (bf16[640,640]{1,0:T(8,128)(2,1)}, bf16[640,640]{1,0:T(8,128)(2,1)}, u32[]{:S(2)}, u32[]{:S(2)}) collective-permute-start(bf16[640,640]{1,0:T(8,128)(2,1)} %collective-permute-done.1), channel_id=1, source_target_pairs={{0,4},{1,5},{2,14},{3,15},{4,8},{5,9},{6,2},{7,3},{8,12},{9,13},{1... | collective-permute-start | bytes 2457608 | tf_op jit(solution)/shard_map/ring_2/ppermute | solution.py:138
  53.1 1.7 %convolution_convert_fusion.3 = bf16[384,640]{1,0:T(8,128)(2,1)S(1)} fusion(bf16[384,640]{1,0:T(8,128)(2,1)S(1)} %get-tuple-element.27, bf16[640,640]{1,0:T(8,128)(2,1)} %constant_dynamic-slice_fusion), kind=kOutput, calls=%fused_computation.7 | convolution fusion | flops 314818560 | bytes 1802240 | tf_op jit(solution)/shard_map/dot_general | solution.py:188
  54.9 0.2 collective-permute-start.5
  55.1 0.0 collective-permute-done.6
  55.1 1.7 %fusion.1 = bf16[384,640]{1,0:T(8,128)(2,1)S(1)} fusion(bf16[384,640]{1,0:T(8,128)(2,1)S(1)} %get-tuple-element.28, bf16[640,640]{1,0:T(8,128)(2,1)} %collective-permute-done.1, bf16[384,640]{1,0:T(8,128)(2,1)S(1)} %collective-permute-done.6), kind=kOutput, calls=%fused_computation.9 | convolution fusion | flops 315310080 | bytes 2293760 | tf_op jit(solution)/shard_map/dot_general | solution.py:188
  56.8 1.3 %collective-permute-start.8 = (bf16[384,640]{1,0:T(8,128)(2,1)S(1)}, bf16[384,640]{1,0:T(8,128)(2,1)S(1)}, u32[]{:S(2)}, u32[]{:S(2)}) collective-permute-start(bf16[384,640]{1,0:T(8,128)(2,1)S(1)} %fusion.1), channel_id=1, source_target_pairs={{1,19},{3,17},{5,20},{7,22},{9,25},{11,27},{13,30},{15,28},{16,3},... | collective-permute-start | bytes 1474568 | tf_op jit(solution)/shard_map/sums_cross_1/ppermute | solution.py:138
  58.1 0.7 collective-permute-start.7
  58.8 0.0 collective-permute-done.5
  58.8 2.6 %fusion = bf16[384,640]{1,0:T(8,128)(2,1)} fusion(bf16[384,640]{1,0:T(8,128)(2,1)S(1)} %get-tuple-element.28, bf16[640,640]{1,0:T(8,128)(2,1)} %constant_dynamic-slice_fusion, bf16[384,640]{1,0:T(8,128)(2,1)S(1)} %collective-permute-done.5), kind=kOutput, calls=%fused_computation.8 | convolution fusion | flops 315310080 | bytes 2293760 | tf_op jit(solution)/shard_map/dot_general | solution.py:188
  61.4 11.0 %collective-permute-done.2 = bf16[640,640]{1,0:T(8,128)(2,1)} collective-permute-done((bf16[640,640]{1,0:T(8,128)(2,1)}, bf16[640,640]{1,0:T(8,128)(2,1)}, u32[]{:S(2)}, u32[]{:S(2)}) %collective-permute-start.2) | collective-permute-done | bytes 819232 | tf_op jit(solution)/shard_map/ring_2/ppermute | solution.py:138
  72.4 0.0 collective-permute-done.8.refs_4_
  72.4 0.0 collective-permute-done.7.refs_0_
  72.4 2.5 %convolution_convert_fusion.1 = bf16[384,640]{1,0:T(8,128)(2,1)} fusion(bf16[384,640]{1,0:T(8,128)(2,1)S(1)} %get-tuple-element.27, bf16[640,640]{1,0:T(8,128)(2,1)} %collective-permute-done.2), kind=kOutput, calls=%fused_computation.5 | convolution fusion | flops 314818560 | bytes 1802240 | tf_op jit(solution)/shard_map/dot_general | solution.py:188
  75.0 0.0 collective-permute-start.10
  75.0 1.6 %collective-permute-start.9 = (bf16[640,640]{1,0:T(8,128)(2,1)}, bf16[640,640]{1,0:T(8,128)(2,1)}, u32[]{:S(2)}, u32[]{:S(2)}) collective-permute-start(bf16[640,640]{1,0:T(8,128)(2,1)} %collective-permute-done.2), channel_id=1, source_target_pairs={{0,4},{1,5},{2,14},{3,15},{4,8},{5,9},{6,2},{7,3},{8,12},{9,13},{1... | collective-permute-start | bytes 2457608 | tf_op jit(solution)/shard_map/ring_3/ppermute | solution.py:138
  76.6 0.6 collective-permute-done.10
  77.2 2.0 %broadcast_select_fusion = (bf16[384,640]{1,0:T(8,128)(2,1)S(1)}, bf16[384,640]{1,0:T(8,128)(2,1)S(1)}) fusion(bf16[384,640]{1,0:T(8,128)(2,1)} %fusion, pred[]{:T(512)S(6)} %eq.7, bf16[384,640]{1,0:T(8,128)(2,1)} %collective-permute-done.10, bf16[384,640]{1,0:T(8,128)(2,1)S(1)} %get-tuple-element.28, bf16[640,640]{1,0:T(8,128)(2,1)} %collective-permute-done.2), kind=kOutput, calls=%fused_computation.12 | convolution fusion | flops 315801600 | bytes 3276801 | tf_op jit(solution)/shard_map/dot_general | solution.py:188
  79.2 0.7 collective-permute-start.14
  79.9 5.6 %collective-permute-start.13 = (bf16[384,640]{1,0:T(8,128)(2,1)S(1)}, bf16[384,640]{1,0:T(8,128)(2,1)S(1)}, u32[]{:S(2)}, u32[]{:S(2)}) collective-permute-start(bf16[384,640]{1,0:T(8,128)(2,1)S(1)} %get-tuple-element.25), channel_id=1, source_target_pairs={{0,2},{2,0},{4,7},{6,5},{8,8},{10,10},{12,13},{14,15},{17,18},{19,... | collective-permute-start | bytes 1474568 | tf_op jit(solution)/shard_map/sums_20/ppermute | solution.py:138
  85.5 0.0 copy-start.7
  85.5 0.0 copy-start.1
  85.5 0.8 collective-permute-start.12
  86.4 2.7 %collective-permute-start.11 = (bf16[384,640]{1,0:T(8,128)(2,1)S(1)}, bf16[384,640]{1,0:T(8,128)(2,1)S(1)}, u32[]{:S(2)}, u32[]{:S(2)}) collective-permute-start(bf16[384,640]{1,0:T(8,128)(2,1)S(1)} %get-tuple-element.26), channel_id=1, source_target_pairs={{0,0},{2,2},{4,5},{6,7},{8,10},{10,8},{12,15},{14,13},{17,16},{19,... | collective-permute-start | bytes 1474568 | tf_op jit(solution)/shard_map/sums_02/ppermute | solution.py:138
  89.1 8.4 %collective-permute-done.9 = bf16[640,640]{1,0:T(8,128)(2,1)} collective-permute-done((bf16[640,640]{1,0:T(8,128)(2,1)}, bf16[640,640]{1,0:T(8,128)(2,1)}, u32[]{:S(2)}, u32[]{:S(2)}) %collective-permute-start.9) | collective-permute-done | bytes 819232 | tf_op jit(solution)/shard_map/ring_3/ppermute | solution.py:138
  97.4 0.0 collective-permute-done.14.refs_6_
  97.5 1.7 %convolution_convert_fusion = bf16[384,640]{1,0:T(8,128)(2,1)S(1)} fusion(bf16[384,640]{1,0:T(8,128)(2,1)S(1)} %copy-done.6, bf16[640,640]{1,0:T(8,128)(2,1)} %collective-permute-done.9), kind=kOutput, calls=%fused_computation.4 | convolution fusion | flops 314818560 | bytes 1802240 | tf_op jit(solution)/shard_map/dot_general | solution.py:188
  99.2 0.2 collective-permute-start.15
  99.4 1.7 %collective-permute-done.15 = bf16[384,640]{1,0:T(8,128)(2,1)S(1)} collective-permute-done((bf16[384,640]{1,0:T(8,128)(2,1)S(1)}, bf16[384,640]{1,0:T(8,128)(2,1)S(1)}, u32[]{:S(2)}, u32[]{:S(2)}) %collective-permute-start.15) | collective-permute-done | bytes 491552 | tf_op jit(solution)/shard_map/core_swap_3/ppermute | solution.py:138
  101.1 1.7 %fusion.3 = bf16[384,640]{1,0:T(8,128)(2,1)S(1)} fusion(bf16[384,640]{1,0:T(8,128)(2,1)S(1)} %get-tuple-element.28, bf16[640,640]{1,0:T(8,128)(2,1)} %collective-permute-done.9, bf16[384,640]{1,0:T(8,128)(2,1)S(1)} %collective-permute-done.15), kind=kOutput, calls=%fused_computation.11 | convolution fusion | flops 315310080 | bytes 2293760 | tf_op jit(solution)/shard_map/dot_general | solution.py:188
  102.9 1.3 %collective-permute-start.17 = (bf16[384,640]{1,0:T(8,128)(2,1)S(1)}, bf16[384,640]{1,0:T(8,128)(2,1)S(1)}, u32[]{:S(2)}, u32[]{:S(2)}) collective-permute-start(bf16[384,640]{1,0:T(8,128)(2,1)S(1)} %fusion.3), channel_id=1, source_target_pairs={{1,17},{3,19},{5,22},{7,20},{9,27},{11,25},{13,28},{15,30},{16,1},... | collective-permute-start | bytes 1474568 | tf_op jit(solution)/shard_map/sums_cross_3/ppermute | solution.py:138
  104.2 2.7 %collective-permute-start.16 = (bf16[384,640]{1,0:T(8,128)(2,1)S(1)}, bf16[384,640]{1,0:T(8,128)(2,1)S(1)}, u32[]{:S(2)}, u32[]{:S(2)}) collective-permute-start(bf16[384,640]{1,0:T(8,128)(2,1)S(1)} %fusion.3), channel_id=1, source_target_pairs={{0,1},{2,3},{4,6},{6,4},{8,11},{10,9},{12,12},{14,14},{17,17},{19,... | collective-permute-start | bytes 1474568 | tf_op jit(solution)/shard_map/sums_3/ppermute | solution.py:138
  106.9 10.6 %collective-permute-done.17.refs_7_ = bf16[384,640]{1,0:T(8,128)(2,1)S(1)} collective-permute-done((bf16[384,640]{1,0:T(8,128)(2,1)S(1)}, bf16[384,640]{1,0:T(8,128)(2,1)S(1)}, u32[]{:S(2)}, u32[]{:S(2)}) %collective-permute-start.17) | collective-permute-done | bytes 491552 | tf_op jit(solution)/shard_map/sums_cross_3/ppermute | solution.py:138
  117.6 1.7 %collective-permute-done.16.refs_3_ = bf16[384,640]{1,0:T(8,128)(2,1)S(1)} collective-permute-done((bf16[384,640]{1,0:T(8,128)(2,1)S(1)}, bf16[384,640]{1,0:T(8,128)(2,1)S(1)}, u32[]{:S(2)}, u32[]{:S(2)}) %collective-permute-start.16) | collective-permute-done | bytes 491552 | tf_op jit(solution)/shard_map/sums_3/ppermute | solution.py:138
  119.3 2.2 %finish.1 = f32[384,1280]{1,0:T(8,128)} custom-call(s32[1]{0:T(128)} %bitcast.spot, bf16[384,640]{1,0:T(8,128)(2,1)S(1)} %collective-permute-done.7.refs_0_, bf16[384,640]{1,0:T(8,128)(2,1)S(1)} %collective-permute-done.11.refs_1_, bf16[384,640]{1,0:T(8,128)(2,1)S(1)} %collective-permute-done.13.refs_2_, ...), custom_call_target="tpu_custom_call" | custom-call | tf_op jit(solution)/shard_map/finish/pallas_call | solution.py:162
  (18 shorter events, 0.0 us)
Async XLA Ops:
  0.0 7.1 %copy-start = (bf16[640,1280]{1,0:T(8,128)(2,1)S(1)}, bf16[640,1280]{1,0:T(8,128)(2,1)}, u32[]{:S(2)}) copy-start(bf16[640,1280]{1,0:T(8,128)(2,1)} %param.11) | copy-start | bytes 4915204
  0.0 29.6 %copy-start.2 = (bf16[2,384,640]{2,1,0:T(8,128)(2,1)S(1)}, bf16[2,384,640]{2,1,0:T(8,128)(2,1)}, u32[]{:S(2)}) copy-start(bf16[2,384,640]{2,1,0:T(8,128)(2,1)} %own_ref.1) | copy-start | bytes 2949124
  0.0 26.0 %collective-permute-start = (bf16[2,384,640]{2,1,0:T(8,128)(2,1)}, bf16[2,384,640]{2,1,0:T(8,128)(2,1)}, u32[]{:S(2)}, u32[]{:S(2)}) collective-permute-start(bf16[2,384,640]{2,1,0:T(8,128)(2,1)} %own_ref.1), channel_id=1, source_target_pairs={{0,4},{4,8},{8,12},{1,5},{5,9},{9,13},{2,6},{6,10},{10,14},{3,7},{... | collective-permute-start | bytes 2949128 | tf_op jit(solution)/shard_map/ppermute | solution.py:95
  3.8 25.9 %collective-permute-start.3 = (bf16[2,384,640]{2,1,0:T(8,128)(2,1)}, bf16[2,384,640]{2,1,0:T(8,128)(2,1)}, u32[]{:S(2)}, u32[]{:S(2)}) collective-permute-start(bf16[2,384,640]{2,1,0:T(8,128)(2,1)} %own_ref.1), channel_id=1, source_target_pairs={{4,0},{8,4},{12,8},{5,1},{9,5},{13,9},{6,2},{10,6},{14,10},{7,3},{... | collective-permute-start | bytes 2949128 | tf_op jit(solution)/shard_map/ppermute | solution.py:95
  7.1 22.5 %copy-start.3 = (bf16[384,640]{1,0:T(8,128)(2,1)S(1)}, bf16[384,640]{1,0:T(8,128)(2,1)}, u32[]{:S(2)}) copy-start(bf16[384,640]{1,0:T(8,128)(2,1)} %q_ref.1) | copy-start | bytes 1474564
  26.0 23.5 %collective-permute-start.1 = (bf16[640,640]{1,0:T(8,128)(2,1)}, bf16[640,640]{1,0:T(8,128)(2,1)}, u32[]{:S(2)}, u32[]{:S(2)}) collective-permute-start(bf16[640,640]{1,0:T(8,128)(2,1)} %constant_dynamic-slice_fusion), channel_id=1, source_target_pairs={{0,4},{1,5},{2,14},{3,15},{4,8},{5,9},{6,2},{7,3},{8,12},{9,13},{1... | collective-permute-start | bytes 2457608 | tf_op jit(solution)/shard_map/ring_1/ppermute | solution.py:138
  29.6 0.7 copy-start.4
  38.0 11.4 %collective-permute-start.4 = (bf16[384,640]{1,0:T(8,128)(2,1)S(1)}, bf16[384,640]{1,0:T(8,128)(2,1)S(1)}, u32[]{:S(2)}, u32[]{:S(2)}) collective-permute-start(bf16[384,640]{1,0:T(8,128)(2,1)S(1)} %attend.1), channel_id=1, source_target_pairs={{0,16},{1,17},{2,18},{3,19},{4,20},{5,21},{6,22},{7,23},{8,24},{9,... | collective-permute-start | bytes 1474568 | tf_op jit(solution)/shard_map/rows_of_other_group/ppermute | solution.py:138
  49.4 23.0 %copy-start.5 = (bf16[384,640]{1,0:T(8,128)(2,1)}, bf16[384,640]{1,0:T(8,128)(2,1)S(1)}, u32[]{:S(2)}) copy-start(bf16[384,640]{1,0:T(8,128)(2,1)S(1)} %get-tuple-element.27) | copy-start | bytes 1474564
  51.4 3.7 %collective-permute-start.6 = (bf16[384,640]{1,0:T(8,128)(2,1)S(1)}, bf16[384,640]{1,0:T(8,128)(2,1)S(1)}, u32[]{:S(2)}, u32[]{:S(2)}) collective-permute-start(bf16[384,640]{1,0:T(8,128)(2,1)S(1)} %convolution_convert_fusion.2), channel_id=1, source_target_pairs={{0,1},{1,0},{2,3},{3,2},{4,5},{5,4},{6,7},{7,6},{8,9},{9,8},{10,11... | collective-permute-start | bytes 1474568 | tf_op jit(solution)/shard_map/core_swap_1/ppermute | solution.py:138
  51.5 21.0 %collective-permute-start.2 = (bf16[640,640]{1,0:T(8,128)(2,1)}, bf16[640,640]{1,0:T(8,128)(2,1)}, u32[]{:S(2)}, u32[]{:S(2)}) collective-permute-start(bf16[640,640]{1,0:T(8,128)(2,1)} %collective-permute-done.1), channel_id=1, source_target_pairs={{0,4},{1,5},{2,14},{3,15},{4,8},{5,9},{6,2},{7,3},{8,12},{9,13},{1... | collective-permute-start | bytes 2457608 | tf_op jit(solution)/shard_map/ring_2/ppermute | solution.py:138
  54.9 4.0 %collective-permute-start.5 = (bf16[384,640]{1,0:T(8,128)(2,1)S(1)}, bf16[384,640]{1,0:T(8,128)(2,1)S(1)}, u32[]{:S(2)}, u32[]{:S(2)}) collective-permute-start(bf16[384,640]{1,0:T(8,128)(2,1)S(1)} %convolution_convert_fusion.3), channel_id=1, source_target_pairs={{0,1},{1,0},{2,3},{3,2},{4,5},{5,4},{6,7},{7,6},{8,9},{9,8},{10,11... | collective-permute-start | bytes 1474568 | tf_op jit(solution)/shard_map/core_swap_0/ppermute | solution.py:138
  56.8 15.6 %collective-permute-start.8 = (bf16[384,640]{1,0:T(8,128)(2,1)S(1)}, bf16[384,640]{1,0:T(8,128)(2,1)S(1)}, u32[]{:S(2)}, u32[]{:S(2)}) collective-permute-start(bf16[384,640]{1,0:T(8,128)(2,1)S(1)} %fusion.1), channel_id=1, source_target_pairs={{1,19},{3,17},{5,20},{7,22},{9,25},{11,27},{13,30},{15,28},{16,3},... | collective-permute-start | bytes 1474568 | tf_op jit(solution)/shard_map/sums_cross_1/ppermute | solution.py:138
  58.1 14.3 %collective-permute-start.7 = (bf16[384,640]{1,0:T(8,128)(2,1)S(1)}, bf16[384,640]{1,0:T(8,128)(2,1)S(1)}, u32[]{:S(2)}, u32[]{:S(2)}) collective-permute-start(bf16[384,640]{1,0:T(8,128)(2,1)S(1)} %fusion.1), channel_id=1, source_target_pairs={{0,3},{2,1},{4,4},{6,6},{8,9},{10,11},{12,14},{14,12},{17,19},{19,... | collective-permute-start | bytes 1474568 | tf_op jit(solution)/shard_map/sums_1/ppermute | solution.py:138
  75.0 2.2 %collective-permute-start.10 = (bf16[384,640]{1,0:T(8,128)(2,1)}, bf16[384,640]{1,0:T(8,128)(2,1)}, u32[]{:S(2)}, u32[]{:S(2)}) collective-permute-start(bf16[384,640]{1,0:T(8,128)(2,1)} %convolution_convert_fusion.1), channel_id=1, source_target_pairs={{0,1},{1,0},{2,3},{3,2},{4,5},{5,4},{6,7},{7,6},{8,9},{9,8},{10,11... | collective-permute-start | bytes 1474568 | tf_op jit(solution)/shard_map/core_swap_2/ppermute | solution.py:138
  75.0 22.5 %collective-permute-start.9 = (bf16[640,640]{1,0:T(8,128)(2,1)}, bf16[640,640]{1,0:T(8,128)(2,1)}, u32[]{:S(2)}, u32[]{:S(2)}) collective-permute-start(bf16[640,640]{1,0:T(8,128)(2,1)} %collective-permute-done.2), channel_id=1, source_target_pairs={{0,4},{1,5},{2,14},{3,15},{4,8},{5,9},{6,2},{7,3},{8,12},{9,13},{1... | collective-permute-start | bytes 2457608 | tf_op jit(solution)/shard_map/ring_3/ppermute | solution.py:138
  76.6 20.9 %copy-start.6 = (bf16[384,640]{1,0:T(8,128)(2,1)S(1)}, bf16[384,640]{1,0:T(8,128)(2,1)}, u32[]{:S(2)}) copy-start(bf16[384,640]{1,0:T(8,128)(2,1)} %copy-done.5) | copy-start | bytes 1474564
  79.2 18.2 %collective-permute-start.14 = (bf16[384,640]{1,0:T(8,128)(2,1)S(1)}, bf16[384,640]{1,0:T(8,128)(2,1)S(1)}, u32[]{:S(2)}, u32[]{:S(2)}) collective-permute-start(bf16[384,640]{1,0:T(8,128)(2,1)S(1)} %get-tuple-element.25), channel_id=1, source_target_pairs={{1,18},{3,16},{5,23},{7,21},{9,24},{11,26},{13,29},{15,31},{16,2},... | collective-permute-start | bytes 1474568 | tf_op jit(solution)/shard_map/sums_cross_20/ppermute | solution.py:138
  79.9 17.5 %collective-permute-start.13 = (bf16[384,640]{1,0:T(8,128)(2,1)S(1)}, bf16[384,640]{1,0:T(8,128)(2,1)S(1)}, u32[]{:S(2)}, u32[]{:S(2)}) collective-permute-start(bf16[384,640]{1,0:T(8,128)(2,1)S(1)} %get-tuple-element.25), channel_id=1, source_target_pairs={{0,2},{2,0},{4,7},{6,5},{8,8},{10,10},{12,13},{14,15},{17,18},{19,... | collective-permute-start | bytes 1474568 | tf_op jit(solution)/shard_map/sums_20/ppermute | solution.py:138
  85.5 21.4 %copy-start.7 = (f32[1280]{0:T(1024)S(1)}, f32[1280]{0:T(1024)}, u32[]{:S(2)}) copy-start(f32[1280]{0:T(1024)} %param.10) | copy-start | bytes 15364
  85.5 33.7 %copy-start.1 = (f32[384,1280]{1,0:T(8,128)S(1)}, f32[384,1280]{1,0:T(8,128)}, u32[]{:S(2)}) copy-start(f32[384,1280]{1,0:T(8,128)} %refs_8_.1) | copy-start | bytes 5898244
  85.5 11.9 %collective-permute-start.12 = (bf16[384,640]{1,0:T(8,128)(2,1)S(1)}, bf16[384,640]{1,0:T(8,128)(2,1)S(1)}, u32[]{:S(2)}, u32[]{:S(2)}) collective-permute-start(bf16[384,640]{1,0:T(8,128)(2,1)S(1)} %get-tuple-element.26), channel_id=1, source_target_pairs={{1,16},{3,18},{5,21},{7,23},{9,26},{11,24},{13,31},{15,29},{16,0},... | collective-permute-start | bytes 1474568 | tf_op jit(solution)/shard_map/sums_cross_02/ppermute | solution.py:138
  86.4 11.1 %collective-permute-start.11 = (bf16[384,640]{1,0:T(8,128)(2,1)S(1)}, bf16[384,640]{1,0:T(8,128)(2,1)S(1)}, u32[]{:S(2)}, u32[]{:S(2)}) collective-permute-start(bf16[384,640]{1,0:T(8,128)(2,1)S(1)} %get-tuple-element.26), channel_id=1, source_target_pairs={{0,0},{2,2},{4,5},{6,7},{8,10},{10,8},{12,15},{14,13},{17,16},{19,... | collective-permute-start | bytes 1474568 | tf_op jit(solution)/shard_map/sums_02/ppermute | solution.py:138
  99.2 1.9 %collective-permute-start.15 = (bf16[384,640]{1,0:T(8,128)(2,1)S(1)}, bf16[384,640]{1,0:T(8,128)(2,1)S(1)}, u32[]{:S(2)}, u32[]{:S(2)}) collective-permute-start(bf16[384,640]{1,0:T(8,128)(2,1)S(1)} %convolution_convert_fusion), channel_id=1, source_target_pairs={{0,1},{1,0},{2,3},{3,2},{4,5},{5,4},{6,7},{7,6},{8,9},{9,8},{10,11... | collective-permute-start | bytes 1474568 | tf_op jit(solution)/shard_map/core_swap_3/ppermute | solution.py:138
  102.9 14.7 %collective-permute-start.17 = (bf16[384,640]{1,0:T(8,128)(2,1)S(1)}, bf16[384,640]{1,0:T(8,128)(2,1)S(1)}, u32[]{:S(2)}, u32[]{:S(2)}) collective-permute-start(bf16[384,640]{1,0:T(8,128)(2,1)S(1)} %fusion.3), channel_id=1, source_target_pairs={{1,17},{3,19},{5,22},{7,20},{9,27},{11,25},{13,28},{15,30},{16,1},... | collective-permute-start | bytes 1474568 | tf_op jit(solution)/shard_map/sums_cross_3/ppermute | solution.py:138
  104.2 15.1 %collective-permute-start.16 = (bf16[384,640]{1,0:T(8,128)(2,1)S(1)}, bf16[384,640]{1,0:T(8,128)(2,1)S(1)}, u32[]{:S(2)}, u32[]{:S(2)}) collective-permute-start(bf16[384,640]{1,0:T(8,128)(2,1)S(1)} %fusion.3), channel_id=1, source_target_pairs={{0,1},{2,3},{4,6},{6,4},{8,11},{10,9},{12,12},{14,14},{17,17},{19,... | collective-permute-start | bytes 1474568 | tf_op jit(solution)/shard_map/sums_3/ppermute | solution.py:138

commit v3 on v2

--- a/solution.py
+++ b/solution.py
@@ -12,6 +12,30 @@
 KSEL = 8
 AXES = ("groups", "frame", "head", "sub")
 MIB = 1 << 20
+
+
+def weight(microseconds):
+    return pl.CostEstimate(
+        flops=int(microseconds * 1e9), bytes_accessed=int(microseconds * 3e6), transcendentals=0
+    )
+
+
+def fence_kernel(token, out):
+    out[0] = token[0]
+
+
+def fence(token, *arrays):
+    *arrays, token = lax.optimization_barrier((*arrays, token))
+    scalar = pl.BlockSpec(memory_space=pltpu.SMEM)
+    token = pl.pallas_call(
+        fence_kernel,
+        out_shape=jax.ShapeDtypeStruct((1,), jnp.int32),
+        in_specs=[scalar],
+        out_specs=scalar,
+        cost_estimate=weight(50),
+        name="fence",
+    )(token)
+    return (*arrays, token)
 
 
 def attend_kernel(ids, live, q_ref, own_ref, low_ref, high_ref, out_ref, kv, sems):
@@ -83,7 +107,7 @@
             pltpu.SemaphoreType.DMA((3,)),
         ],
         compiler_params=pltpu.CompilerParams(vmem_limit_bytes=24 * MIB),
-        cost_estimate=pl.CostEstimate(flops=1, bytes_accessed=1, transcendentals=0),
+        cost_estimate=weight(8),
         name="attend",
     )(local_ids, live, queries, keyvals, low, high)
 
@@ -177,22 +201,12 @@
     x = lax.axis_index("head")
     c = lax.axis_index("sub")
     half = out_weight.shape[1] // 2
-    low, high = halos(keyvals)
+    tie = lax.optimization_barrier
 
     ring = pairs(lambda y, f, x, c: (y, (f + 1) % 4 if x == 0 else (f - 1) % 4, x, c))
+    sibling = pairs(lambda y, f, x, c: (y, f, x, 1 - c))
     here = y == c
     left = x == 0
-
-    def sums(weights, name):
-        def product(rows):
-            return jnp.dot(rows, weights, preferred_element_type=jnp.float32)
-
-        swapped = send(
-            product(given).astype(jnp.bfloat16),
-            pairs(lambda y, f, x, c: (y, f, x, 1 - c)),
-            "core_swap_" + name,
-        )
-        return (product(kept) + swapped.astype(jnp.float32)).astype(jnp.bfloat16)
 
     def to_owners(array, steps, name):
         return [
@@ -200,32 +214,71 @@
             send(array, to_owner((steps,) * 2, (1,)), "sums_cross_" + name),
         ]
 
+    low, high = halos(keyvals)
     w0 = lax.dynamic_slice_in_dim(out_weight, y * half, half, axis=1)
-    w1 = send(after(w0, low), ring, "ring_1")
+    v0 = send(w0, sibling, "core_swap_0")
+    w0, v0, low, high = tie((w0, v0, low, high))
+    w1 = send(w0, ring, "ring_1")
     attended = attend(queries, keyvals, low, high, pattern, live)
+    first = send(
+        attended,
+        pairs(lambda y, f, x, c: (1 - y, f, x, c) if c == y else (y, f, x, 1 - c)),
+        "rows_1",
+    )
+    second = send(
+        attended,
+        pairs(lambda y, f, x, c: (1 - y, f, x, 1 - c), lambda y, f, x, c: c != y),
+        "rows_2",
+    )
+
+    def region(token, body, *operands):
+        shapes = jax.eval_shape(body, *operands)
+        return lax.cond(
+            token[0] > 0,
+            body,
+            lambda *_: jax.tree.map(lambda leaf: jnp.zeros(leaf.shape, leaf.dtype), shapes),
+            *operands,
+        )
+
+    def sums(rows_own, rows_sib, own, sib):
+        total = jnp.dot(rows_own, own, preferred_element_type=jnp.float32)
+        total = total + jnp.dot(rows_sib, sib, preferred_element_type=jnp.float32)
+        return total.astype(jnp.bfloat16)
+
+    def swapped(w):
+        return send(w, sibling, "core_swap")
+
+    def begin(rows_own, rows_sib, w1):
+        return sums(rows_own, rows_sib, w1, swapped(w1))
+
+    def mix(rows_own, rows_sib, s0, w2):
+        s2 = sums(rows_own, rows_sib, w2, swapped(w2))
+        return jnp.where(left, s0, s2), jnp.where(left, s2, s0)
+
+    def end(rows_own, rows_sib, w3):
+        return sums(rows_own, rows_sib, w3, swapped(w3))
+
     w2 = send(w1, ring, "ring_2")
-    others = send(attended, pairs(lambda y, f, x, c: (1 - y, f, x, c)), "rows_of_other_group")
-    kept = jnp.where(here, attended, others)
-    given = jnp.where(here, others, attended)
-    s1 = sums(w1, "1")
+    w1, token = fence(live[:1], w1)
+    first, second, token = tie((first, second, token))
+    rows_own = jnp.where(here, attended, first)
+    rows_sib = jnp.where(here, first, second)
+    s1 = region(token, begin, rows_own, rows_sib, w1)
     middle = to_owners(s1, (1, 1), "1")
-    s0 = sums(w0, "0")
-    w2 = after(w2, s0, s1)
+    s0 = region(token, sums, rows_own, rows_sib, w0, v0)
+    w2, s0 = tie((w2, s0))
     w3 = send(w2, ring, "ring_3")
-    w2, *middle = lax.optimization_barrier((w2, *middle))
-    s2 = sums(w2, "2")
-    low_sum, high_sum = jnp.where(left, s0, s2), jnp.where(left, s2, s0)
+    w2, *middle = tie((w2, *middle))
+    low_sum, high_sum = region(token, mix, rows_own, rows_sib, s0, w2)
     early = to_owners(low_sum, (0, 2), "02") + to_owners(high_sum, (2, 0), "20")
-    w3, *early = lax.optimization_barrier((w3, *early))
-    s3 = sums(w3, "3")
+    w3, low_sum, high_sum = tie((w3, low_sum, high_sum))
+    s3 = region(token, end, rows_own, rows_sib, w3)
+    s3, *early = tie((s3, *early))
+    middle += early
     last = to_owners(s3, (3, 3), "3")
-    return finish(
-        [middle[0], early[0], early[2], last[0]],
-        [middle[1], early[1], early[3], last[1]],
-        residual_in,
-        gate,
-        jnp.reshape(y, (1,)),
-    )
+    spot = jnp.reshape(y, (1,))
+    base = finish(middle[::2], middle[1::2], residual_in, gate, spot)
+    return finish(last[::2], last[1::2], base, gate, spot)
 
 
 def solution(mesh):

time: 123 us -> 118 us (0.959)
  waiting for transfers between devices: 63.2 us -> 46.6 us
  local copies, waits for them, and re-layouts: 1.66 us -> 5.41 us
  Pallas kernels: 9.81 us -> 13.3 us
  starting transfers between devices: 29.7 us -> 31.7 us
    ppermute x16 -> x17, waiting for transfers between devices: 43.9 us -> 27.1 us  [send(): return lax.ppermute(array, AXES, route)]
    unnamed x16 -> x14, local copies, waits for them, and re-layouts: 0.69 us -> 4.44 us
    ppermute x16 -> x17, starting transfers between devices: 22.7 us -> 25.6 us  [send(): return lax.ppermute(array, AXES, route)]
    pallas_call x1 -> x2, Pallas kernels: 2.15 us -> 4.45 us  [finish(): pl.pallas_call(finish_kernel, grid=(rows // step,), out_shape=jax.ShapeDt...]
    ppermute x1, waiting for transfers between devices: 1.39 us -> 3.32 us  [halos(): lax.ppermute(keyvals, 'frame', backward)]
    ppermute x1, waiting for transfers between devices: 17.9 us -> 16.1 us  [halos(): lax.ppermute(keyvals, 'frame', forward)]
  transfers between devices with their start and end apart: 18 -> 19, of which waited for: 9 -> 12; matrix products, arithmetic and copies ran while one was open for 8% -> 17% of each run, Pallas kernels for 6% -> 10%
where the time goes in v3:
time: 118 us; the launch traced here: 117 us
  waiting for transfers between devices  46.6 us (39%)
  starting transfers between devices  31.7 us (27%)
  matrix products  17.1 us (14%)
  Pallas kernels  13.3 us (11%)
  local copies, waits for them, and re-layouts  5.41 us (5%)
  other arithmetic  1.76 us (1%)
    ppermute x17, waiting for transfers between devices, send(): return lax.ppermute(array, AXES, route)  27.1 us
    ppermute x17, starting transfers between devices, send(): return lax.ppermute(array, AXES, route)  25.6 us
    ppermute x1, waiting for transfers between devices, halos(): lax.ppermute(keyvals, 'frame', forward)  16.1 us
    dot_general x4, matrix products, sums(): total = total + jnp.dot(rows_sib, sib, preferred_element_type=jnp.float32)  9.41 us
    pallas_call x1, Pallas kernels, attend(): pl.pallas_call(attend_kernel, out_shape=jax.ShapeDtypeStruct((rows, width...  7.69 us
    dot_general x4, matrix products, sums(): total = jnp.dot(rows_own, own, preferred_element_type=jnp.float32)  7.65 us
    pallas_call x2, Pallas kernels, finish(): pl.pallas_call(finish_kernel, grid=(rows // step,), out_shape=jax.ShapeDt...  4.45 us
    unnamed x14, local copies, waits for them, and re-layouts  4.44 us
  transfers between devices with their start and end apart: 19, of which 12 were waited for; matrix products, arithmetic and copies ran while one was open for 17% of the time, Pallas kernels for 10%

profile of v3, /device:TPU:8, one launch (start us, length us, event | category | flops | bytes accessed | tf_op | source)
XLA Modules:
  0.0 116.7 jit_solution(8315292458619445164)
XLA Ops:
  0.0 3.6 %collective-permute-start.4 = (bf16[2,384,640]{2,1,0:T(8,128)(2,1)}, bf16[2,384,640]{2,1,0:T(8,128)(2,1)S(1)}, u32[]{:S(2)}, u32[]{:S(2)}) collective-permute-start(bf16[2,384,640]{2,1,0:T(8,128)(2,1)} %own_ref.1), channel_id=1, source_target_pairs={{0,4},{4,8},{8,12},{1,5},{5,9},{9,13},{2,6},{6,10},{10,14},{3,7},{... | collective-permute-start | bytes 2949128 | tf_op jit(solution)/shard_map/ppermute | solution.py:119
  3.6 2.4 %collective-permute-start.5 = (bf16[2,384,640]{2,1,0:T(8,128)(2,1)}, bf16[2,384,640]{2,1,0:T(8,128)(2,1)}, u32[]{:S(2)}, u32[]{:S(2)}) collective-permute-start(bf16[2,384,640]{2,1,0:T(8,128)(2,1)} %own_ref.1), channel_id=1, source_target_pairs={{4,0},{8,4},{12,8},{5,1},{9,5},{13,9},{6,2},{10,6},{14,10},{7,3},{... | collective-permute-start | bytes 2949128 | tf_op jit(solution)/shard_map/ppermute | solution.py:119
  6.1 1.0 constant_dynamic-slice_fusion
  7.0 2.5 %collective-permute-done.3 = bf16[640,640]{1,0:T(8,128)(2,1)S(1)} collective-permute-done((bf16[640,640]{1,0:T(8,128)(2,1)}, bf16[640,640]{1,0:T(8,128)(2,1)S(1)}, u32[]{:S(2)}, u32[]{:S(2)}) %collective-permute-start.3) | collective-permute-done | bytes 819232 | tf_op jit(solution)/shard_map/core_swap_0/ppermute | solution.py:162
  9.6 16.1 %collective-permute-done.4.low_ref = bf16[2,384,640]{2,1,0:T(8,128)(2,1)S(1)} collective-permute-done((bf16[2,384,640]{2,1,0:T(8,128)(2,1)}, bf16[2,384,640]{2,1,0:T(8,128)(2,1)S(1)}, u32[]{:S(2)}, u32[]{:S(2)}) %collective-permute-start.4) | collective-permute-done | bytes 983072 | tf_op jit(solution)/shard_map/ppermute | solution.py:119
  25.7 3.3 %collective-permute-done.5.high_ref = bf16[2,384,640]{2,1,0:T(8,128)(2,1)} collective-permute-done((bf16[2,384,640]{2,1,0:T(8,128)(2,1)}, bf16[2,384,640]{2,1,0:T(8,128)(2,1)}, u32[]{:S(2)}, u32[]{:S(2)}) %collective-permute-start.5) | collective-permute-done | bytes 983072 | tf_op jit(solution)/shard_map/ppermute | solution.py:119
  29.0 1.6 %collective-permute-start.8 = (bf16[640,640]{1,0:T(8,128)(2,1)}, bf16[640,640]{1,0:T(8,128)(2,1)}, u32[]{:S(2)}, u32[]{:S(2)}) collective-permute-start(bf16[640,640]{1,0:T(8,128)(2,1)} %constant_dynamic-slice_fusion), channel_id=1, source_target_pairs={{0,4},{1,5},{2,14},{3,15},{4,8},{5,9},{6,2},{7,3},{8,12},{9,13},{1... | collective-permute-start | bytes 2457608 | tf_op jit(solution)/shard_map/ring_1/ppermute | solution.py:162
  30.6 0.7 subtract_clamp_fusion.ids
  31.3 1.2 %copy-done.2 = bf16[2,384,640]{2,1,0:T(8,128)(2,1)S(1)} copy-done((bf16[2,384,640]{2,1,0:T(8,128)(2,1)S(1)}, bf16[2,384,640]{2,1,0:T(8,128)(2,1)}, u32[]{:S(2)}) %copy-start.2) | copy-done | bytes 983064
  32.5 1.0 copy-done.3
  33.6 0.7 copy-done.4
  34.2 7.7 %attend.1 = bf16[384,640]{1,0:T(8,128)(2,1)S(1)} custom-call(s32[6,8]{1,0:T(8,128)S(1)} %subtract_clamp_fusion.ids, s32[6]{0:T(128)S(1)} %copy-done.4, bf16[384,640]{1,0:T(8,128)(2,1)S(1)} %copy-done.3, bf16[2,384,640]{2,1,0:T(8,128)(2,1)S(1)} %copy-done.2, bf16[2,384,640]{2,1,0:T(8,128)(2,1)S(1)} %collective-permute-done.4.low_ref, ...), custom_call_target="tpu_custom_call" | custom-call | flops 8000000000 | bytes 24000000 | tf_op jit(solution)/shard_map/attend/pallas_call | solution.py:100
  41.9 1.5 %collective-permute-start.6 = (bf16[384,640]{1,0:T(8,128)(2,1)S(1)}, bf16[384,640]{1,0:T(8,128)(2,1)S(1)}, u32[]{:S(2)}, u32[]{:S(2)}) collective-permute-start(bf16[384,640]{1,0:T(8,128)(2,1)S(1)} %attend.1), channel_id=1, source_target_pairs={{0,16},{1,0},{2,18},{3,2},{4,20},{5,4},{6,22},{7,6},{8,24},{9,8},{... | collective-permute-start | bytes 1474568 | tf_op jit(solution)/shard_map/rows_1/ppermute | solution.py:162
  43.4 0.7 collective-permute-start.7
  44.1 4.0 %collective-permute-done.8 = bf16[640,640]{1,0:T(8,128)(2,1)} collective-permute-done((bf16[640,640]{1,0:T(8,128)(2,1)}, bf16[640,640]{1,0:T(8,128)(2,1)}, u32[]{:S(2)}, u32[]{:S(2)}) %collective-permute-start.8) | collective-permute-done | bytes 819232 | tf_op jit(solution)/shard_map/ring_1/ppermute | solution.py:162
  48.2 1.6 %collective-permute-start.9 = (bf16[640,640]{1,0:T(8,128)(2,1)}, bf16[640,640]{1,0:T(8,128)(2,1)}, u32[]{:S(2)}, u32[]{:S(2)}) collective-permute-start(bf16[640,640]{1,0:T(8,128)(2,1)} %collective-permute-done.8), channel_id=1, source_target_pairs={{0,4},{1,5},{2,14},{3,15},{4,8},{5,9},{6,2},{7,3},{8,12},{9,13},{1... | collective-permute-start | bytes 2457608 | tf_op jit(solution)/shard_map/ring_2/ppermute | solution.py:162
  49.7 1.2 fence.1
  50.9 2.8 %collective-permute-done.6 = bf16[384,640]{1,0:T(8,128)(2,1)S(1)} collective-permute-done((bf16[384,640]{1,0:T(8,128)(2,1)S(1)}, bf16[384,640]{1,0:T(8,128)(2,1)S(1)}, u32[]{:S(2)}, u32[]{:S(2)}) %collective-permute-start.6) | collective-permute-done | bytes 491552 | tf_op jit(solution)/shard_map/rows_1/ppermute | solution.py:162
  54.4 1.1 broadcast_select_fusion.2
  55.4 6.1 %conditional.5 = (bf16[384,640]{1,0:T(8,128)(2,1)}) conditional(s32[]{:T(128)} %bitcast.1, () %tuple.46, (bf16[384,640]{1,0:T(8,128)(2,1)}, bf16[640,640]{1,0:T(8,128)(2,1)}, bf16[384,640]{1,0:T(8,128)(2,1)}) %tuple.47), branch_computations={%region_2.3_spmd, %region_3.4_spmd} | conditional | flops 629637120 | bytes 8355888 | solution.py:236
  55.4 1.5 %collective-permute-start = (bf16[640,640]{1,0:T(8,128)(2,1)}, bf16[640,640]{1,0:T(8,128)(2,1)S(1)}, u32[]{:S(2)}, u32[]{:S(2)}) collective-permute-start(bf16[640,640]{1,0:T(8,128)(2,1)} %get-tuple-element.51), channel_id=1, source_target_pairs={{0,1},{1,0},{2,3},{3,2},{4,5},{5,4},{6,7},{7,6},{8,9},{9,8},{10,11... | collective-permute-start | bytes 2457608 | tf_op jit(solution)/shard_map/cond/branch_1_fun/core_swap/ppermute | solution.py:162
  56.9 1.9 %fusion.5 = f32[384,640]{1,0:T(8,128)S(1)} fusion(bf16[384,640]{1,0:T(8,128)(2,1)} %get-tuple-element.50, bf16[640,640]{1,0:T(8,128)(2,1)} %get-tuple-element.51), kind=kOutput, calls=%fused_computation.15 | convolution fusion | flops 314572800 | bytes 2293760 | tf_op jit(solution)/shard_map/cond/branch_1_fun/dot_general | solution.py:244
  59.1 2.4 %fusion.1 = bf16[384,640]{1,0:T(8,128)(2,1)} fusion(f32[384,640]{1,0:T(8,128)S(1)} %fusion.5, bf16[384,640]{1,0:T(8,128)(2,1)} %get-tuple-element.52, bf16[640,640]{1,0:T(8,128)(2,1)S(1)} %collective-permute-done), kind=kOutput, calls=%fused_computation.3 | convolution fusion | flops 315064320 | bytes 2785280 | tf_op jit(solution)/shard_map/cond/branch_1_fun/dot_general | solution.py:245
  61.5 1.7 %collective-permute-start.11 = (bf16[384,640]{1,0:T(8,128)(2,1)}, bf16[384,640]{1,0:T(8,128)(2,1)S(1)}, u32[]{:S(2)}, u32[]{:S(2)}) collective-permute-start(bf16[384,640]{1,0:T(8,128)(2,1)} %get-tuple-element.114), channel_id=1, source_target_pairs={{0,3},{2,1},{4,4},{6,6},{8,9},{10,11},{12,14},{14,12},{17,19},{19,... | collective-permute-start | bytes 1474568 | tf_op jit(solution)/shard_map/sums_1/ppermute | solution.py:162
  63.2 1.3 %collective-permute-start.12 = (bf16[384,640]{1,0:T(8,128)(2,1)}, bf16[384,640]{1,0:T(8,128)(2,1)S(1)}, u32[]{:S(2)}, u32[]{:S(2)}) collective-permute-start(bf16[384,640]{1,0:T(8,128)(2,1)} %get-tuple-element.114), channel_id=1, source_target_pairs={{1,19},{3,17},{5,20},{7,22},{9,25},{11,27},{13,30},{15,28},{16,3},... | collective-permute-start | bytes 1474568 | tf_op jit(solution)/shard_map/sums_cross_1/ppermute | solution.py:162
  64.5 3.6 %conditional.4 = (bf16[384,640]{1,0:T(8,128)(2,1)S(1)}) conditional(s32[]{:T(128)} %bitcast.1, () %tuple.42, (bf16[384,640]{1,0:T(8,128)(2,1)}, bf16[640,640]{1,0:T(8,128)(2,1)}, bf16[384,640]{1,0:T(8,128)(2,1)}, bf16[640,640]{1,0:T(8,128)(2,1)}) %tuple.63), branch_computations={%region_0.1_spmd, %region_1.2_spmd} | conditional | flops 629637120 | bytes 8355876 | solution.py:236
  64.5 2.0 %fusion.4 = f32[384,640]{1,0:T(8,128)S(1)} fusion(bf16[384,640]{1,0:T(8,128)(2,1)} %get-tuple-element.46, bf16[640,640]{1,0:T(8,128)(2,1)} %get-tuple-element.47), kind=kOutput, calls=%fused_computation.14 | convolution fusion | flops 314572800 | bytes 2293760 | tf_op jit(solution)/shard_map/cond/branch_1_fun/dot_general | solution.py:244
  66.5 1.6 %fusion = bf16[384,640]{1,0:T(8,128)(2,1)S(1)} fusion(f32[384,640]{1,0:T(8,128)S(1)} %fusion.4, bf16[384,640]{1,0:T(8,128)(2,1)} %get-tuple-element.48, bf16[640,640]{1,0:T(8,128)(2,1)S(1)} %copy-done.6), kind=kOutput, calls=%fused_computation.1 | convolution fusion | flops 315064320 | bytes 2785280 | tf_op jit(solution)/shard_map/cond/branch_1_fun/dot_general | solution.py:245
  68.2 6.2 %collective-permute-done.12.refs_3_ = bf16[384,640]{1,0:T(8,128)(2,1)S(1)} collective-permute-done((bf16[384,640]{1,0:T(8,128)(2,1)}, bf16[384,640]{1,0:T(8,128)(2,1)S(1)}, u32[]{:S(2)}, u32[]{:S(2)}) %collective-permute-start.12) | collective-permute-done | bytes 491552 | tf_op jit(solution)/shard_map/sums_cross_1/ppermute | solution.py:162
  74.5 5.6 %conditional.6 = (bf16[384,640]{1,0:T(8,128)(2,1)}, bf16[384,640]{1,0:T(8,128)(2,1)}) conditional(s32[]{:T(128)} %bitcast.1, () %tuple.45, (s32[]{:T(128)}, bf16[384,640]{1,0:T(8,128)(2,1)}, bf16[640,640]{1,0:T(8,128)(2,1)}, bf16[384,640]{1,0:T(8,128)(2,1)}, bf16[384,640]{1,0:T(8,128)(2,1)S(1)}) %tuple.49), branch_computations={%region_4.5_spmd, %region_5.6_spmd} | conditional | flops 630128640 | bytes 9338946 | solution.py:236
  74.5 1.9 %fusion.6 = f32[384,640]{1,0:T(8,128)S(1)} fusion(bf16[384,640]{1,0:T(8,128)(2,1)} %get-tuple-element.55, bf16[640,640]{1,0:T(8,128)(2,1)} %get-tuple-element.56), kind=kOutput, calls=%fused_computation.16 | convolution fusion | flops 314572800 | bytes 2293760 | tf_op jit(solution)/shard_map/cond/branch_1_fun/dot_general | solution.py:244
  76.4 0.8 collective-permute-done.1
  77.1 2.9 %broadcast_select_fusion = (bf16[384,640]{1,0:T(8,128)(2,1)}, bf16[384,640]{1,0:T(8,128)(2,1)}) fusion(bf16[384,640]{1,0:T(8,128)(2,1)S(1)} %get-tuple-element.54, pred[]{:T(512)S(6)} %eq.5, f32[384,640]{1,0:T(8,128)S(1)} %fusion.6, bf16[384,640]{1,0:T(8,128)(2,1)} %get-tuple-element.57, bf16[640,640]{1,0:T(8,128)(2,1)} %collective-permute-done.1), kind=kOutput, calls=%fused_computation.6 | convolution fusion | flops 315555840 | bytes 3768321 | tf_op jit(solution)/shard_map/cond/branch_1_fun/dot_general | solution.py:245
  80.1 2.1 %collective-permute-start.13 = (bf16[384,640]{1,0:T(8,128)(2,1)}, bf16[384,640]{1,0:T(8,128)(2,1)S(1)}, u32[]{:S(2)}, u32[]{:S(2)}) collective-permute-start(bf16[384,640]{1,0:T(8,128)(2,1)} %get-tuple-element.95), channel_id=1, source_target_pairs={{0,0},{2,2},{4,5},{6,7},{8,10},{10,8},{12,15},{14,13},{17,16},{19,... | collective-permute-start | bytes 1474568 | tf_op jit(solution)/shard_map/sums_02/ppermute | solution.py:162
  82.1 1.5 %collective-permute-start.14 = (bf16[384,640]{1,0:T(8,128)(2,1)}, bf16[384,640]{1,0:T(8,128)(2,1)}, u32[]{:S(2)}, u32[]{:S(2)}) collective-permute-start(bf16[384,640]{1,0:T(8,128)(2,1)} %get-tuple-element.95), channel_id=1, source_target_pairs={{1,16},{3,18},{5,21},{7,23},{9,26},{11,24},{13,31},{15,29},{16,0},... | collective-permute-start | bytes 1474568 | tf_op jit(solution)/shard_map/sums_cross_02/ppermute | solution.py:162
  83.6 4.1 %collective-permute-start.15 = (bf16[384,640]{1,0:T(8,128)(2,1)}, bf16[384,640]{1,0:T(8,128)(2,1)}, u32[]{:S(2)}, u32[]{:S(2)}) collective-permute-start(bf16[384,640]{1,0:T(8,128)(2,1)} %get-tuple-element.96), channel_id=1, source_target_pairs={{0,2},{2,0},{4,7},{6,5},{8,8},{10,10},{12,13},{14,15},{17,18},{19,... | collective-permute-start | bytes 1474568 | tf_op jit(solution)/shard_map/sums_20/ppermute | solution.py:162
  87.7 1.4 %collective-permute-start.16 = (bf16[384,640]{1,0:T(8,128)(2,1)}, bf16[384,640]{1,0:T(8,128)(2,1)}, u32[]{:S(2)}, u32[]{:S(2)}) collective-permute-start(bf16[384,640]{1,0:T(8,128)(2,1)} %get-tuple-element.96), channel_id=1, source_target_pairs={{1,18},{3,16},{5,23},{7,21},{9,24},{11,26},{13,29},{15,31},{16,2},... | collective-permute-start | bytes 1474568 | tf_op jit(solution)/shard_map/sums_cross_20/ppermute | solution.py:162
  89.1 5.1 %conditional.7 = (bf16[384,640]{1,0:T(8,128)(2,1)}) conditional(s32[]{:T(128)} %bitcast.1, () %tuple.41, (bf16[384,640]{1,0:T(8,128)(2,1)}, bf16[640,640]{1,0:T(8,128)(2,1)}, bf16[384,640]{1,0:T(8,128)(2,1)}) %tuple.51), branch_computations={%region_6.7_spmd, %region_7.8_spmd} | conditional | flops 629637120 | bytes 8355888 | solution.py:236
  89.7 1.9 %fusion.7 = f32[384,640]{1,0:T(8,128)S(1)} fusion(bf16[384,640]{1,0:T(8,128)(2,1)} %get-tuple-element.58, bf16[640,640]{1,0:T(8,128)(2,1)} %get-tuple-element.59), kind=kOutput, calls=%fused_computation.17 | convolution fusion | flops 314572800 | bytes 2293760 | tf_op jit(solution)/shard_map/cond/branch_1_fun/dot_general | solution.py:244
  91.9 2.4 %fusion.3 = bf16[384,640]{1,0:T(8,128)(2,1)} fusion(f32[384,640]{1,0:T(8,128)S(1)} %fusion.7, bf16[384,640]{1,0:T(8,128)(2,1)} %get-tuple-element.60, bf16[640,640]{1,0:T(8,128)(2,1)S(1)} %collective-permute-done.2), kind=kOutput, calls=%fused_computation.9 | convolution fusion | flops 315064320 | bytes 2785280 | tf_op jit(solution)/shard_map/cond/branch_1_fun/dot_general | solution.py:245
  94.3 2.7 %collective-permute-done.15.refs_2_ = bf16[384,640]{1,0:T(8,128)(2,1)} collective-permute-done((bf16[384,640]{1,0:T(8,128)(2,1)}, bf16[384,640]{1,0:T(8,128)(2,1)}, u32[]{:S(2)}, u32[]{:S(2)}) %collective-permute-start.15) | collective-permute-done | bytes 491552 | tf_op jit(solution)/shard_map/sums_20/ppermute | solution.py:162
  97.0 4.8 %collective-permute-start.17 = (bf16[384,640]{1,0:T(8,128)(2,1)}, bf16[384,640]{1,0:T(8,128)(2,1)S(1)}, u32[]{:S(2)}, u32[]{:S(2)}) collective-permute-start(bf16[384,640]{1,0:T(8,128)(2,1)} %get-tuple-element.115), channel_id=1, source_target_pairs={{0,1},{2,3},{4,6},{6,4},{8,11},{10,9},{12,12},{14,14},{17,17},{19,... | collective-permute-start | bytes 1474568 | tf_op jit(solution)/shard_map/sums_3/ppermute | solution.py:162
  101.8 1.3 %collective-permute-start.18 = (bf16[384,640]{1,0:T(8,128)(2,1)}, bf16[384,640]{1,0:T(8,128)(2,1)S(1)}, u32[]{:S(2)}, u32[]{:S(2)}) collective-permute-start(bf16[384,640]{1,0:T(8,128)(2,1)} %get-tuple-element.115), channel_id=1, source_target_pairs={{1,17},{3,19},{5,22},{7,20},{9,27},{11,25},{13,28},{15,30},{16,1},... | collective-permute-start | bytes 1474568 | tf_op jit(solution)/shard_map/sums_cross_3/ppermute | solution.py:162
  103.1 1.5 %copy-done.1 = f32[384,1280]{1,0:T(8,128)S(1)} copy-done((f32[384,1280]{1,0:T(8,128)S(1)}, f32[384,1280]{1,0:T(8,128)}, u32[]{:S(2)}) %copy-start.1) | copy-done | bytes 1966104
  104.7 2.6 %finish.2.refs_2_ = f32[384,1280]{1,0:T(8,128)S(1)} custom-call(s32[1]{0:T(128)} %bitcast.spot, bf16[384,640]{1,0:T(8,128)(2,1)S(1)} %collective-permute-done.11.refs_0_, bf16[384,640]{1,0:T(8,128)(2,1)S(1)} %collective-permute-done.13.refs_1_, bf16[384,640]{1,0:T(8,128)(2,1)} %collective-permute-done.15.refs_2_, ...), custom_call_target="tpu_custom_call" | custom-call | tf_op jit(solution)/shard_map/finish/pallas_call | solution.py:186
  107.3 6.6 %collective-permute-done.17.refs_0_ = bf16[384,640]{1,0:T(8,128)(2,1)S(1)} collective-permute-done((bf16[384,640]{1,0:T(8,128)(2,1)}, bf16[384,640]{1,0:T(8,128)(2,1)S(1)}, u32[]{:S(2)}, u32[]{:S(2)}) %collective-permute-start.17) | collective-permute-done | bytes 491552 | tf_op jit(solution)/shard_map/sums_3/ppermute | solution.py:162
  113.9 0.9 collective-permute-done.18.refs_1_
  114.9 1.9 %finish.3 = f32[384,1280]{1,0:T(8,128)} custom-call(s32[1]{0:T(128)} %bitcast.spot, bf16[384,640]{1,0:T(8,128)(2,1)S(1)} %collective-permute-done.17.refs_0_, bf16[384,640]{1,0:T(8,128)(2,1)S(1)} %collective-permute-done.18.refs_1_, f32[384,1280]{1,0:T(8,128)S(1)} %finish.2.refs_2_, f32[1,1280]{1,0:T(1,128)S(1)} %broadcast_in_dim.4.refs_7_.refs_3_), custom_call_target="tpu_custom_call" | custom-call | tf_op jit(solution)/shard_map/finish/pallas_call | solution.py:186
  (26 shorter events, 1.2 us)
Async XLA Ops:
  0.0 6.1 %copy-start = (bf16[640,1280]{1,0:T(8,128)(2,1)S(1)}, bf16[640,1280]{1,0:T(8,128)(2,1)}, u32[]{:S(2)}) copy-start(bf16[640,1280]{1,0:T(8,128)(2,1)} %param.19) | copy-start | bytes 4915204
  0.0 25.7 %collective-permute-start.4 = (bf16[2,384,640]{2,1,0:T(8,128)(2,1)}, bf16[2,384,640]{2,1,0:T(8,128)(2,1)S(1)}, u32[]{:S(2)}, u32[]{:S(2)}) collective-permute-start(bf16[2,384,640]{2,1,0:T(8,128)(2,1)} %own_ref.1), channel_id=1, source_target_pairs={{0,4},{4,8},{8,12},{1,5},{5,9},{9,13},{2,6},{6,10},{10,14},{3,7},{... | collective-permute-start | bytes 2949128 | tf_op jit(solution)/shard_map/ppermute | solution.py:119
  3.6 25.4 %collective-permute-start.5 = (bf16[2,384,640]{2,1,0:T(8,128)(2,1)}, bf16[2,384,640]{2,1,0:T(8,128)(2,1)}, u32[]{:S(2)}, u32[]{:S(2)}) collective-permute-start(bf16[2,384,640]{2,1,0:T(8,128)(2,1)} %own_ref.1), channel_id=1, source_target_pairs={{4,0},{8,4},{12,8},{5,1},{9,5},{13,9},{6,2},{10,6},{14,10},{7,3},{... | collective-permute-start | bytes 2949128 | tf_op jit(solution)/shard_map/ppermute | solution.py:119
  7.0 2.5 %collective-permute-start.3 = (bf16[640,640]{1,0:T(8,128)(2,1)}, bf16[640,640]{1,0:T(8,128)(2,1)S(1)}, u32[]{:S(2)}, u32[]{:S(2)}) collective-permute-start(bf16[640,640]{1,0:T(8,128)(2,1)} %constant_dynamic-slice_fusion), channel_id=1, source_target_pairs={{0,1},{1,0},{2,3},{3,2},{4,5},{5,4},{6,7},{7,6},{8,9},{9,8},{10,11... | collective-permute-start | bytes 2457608 | tf_op jit(solution)/shard_map/core_swap_0/ppermute | solution.py:162
  9.6 19.5 %copy-start.5 = (bf16[640,640]{1,0:T(8,128)(2,1)}, bf16[640,640]{1,0:T(8,128)(2,1)S(1)}, u32[]{:S(2)}) copy-start(bf16[640,640]{1,0:T(8,128)(2,1)S(1)} %collective-permute-done.3) | copy-start | bytes 2457604
  29.0 19.1 %collective-permute-start.8 = (bf16[640,640]{1,0:T(8,128)(2,1)}, bf16[640,640]{1,0:T(8,128)(2,1)}, u32[]{:S(2)}, u32[]{:S(2)}) collective-permute-start(bf16[640,640]{1,0:T(8,128)(2,1)} %constant_dynamic-slice_fusion), channel_id=1, source_target_pairs={{0,4},{1,5},{2,14},{3,15},{4,8},{5,9},{6,2},{7,3},{8,12},{9,13},{1... | collective-permute-start | bytes 2457608 | tf_op jit(solution)/shard_map/ring_1/ppermute | solution.py:162
  31.3 1.2 %copy-start.2 = (bf16[2,384,640]{2,1,0:T(8,128)(2,1)S(1)}, bf16[2,384,640]{2,1,0:T(8,128)(2,1)}, u32[]{:S(2)}) copy-start(bf16[2,384,640]{2,1,0:T(8,128)(2,1)} %own_ref.1) | copy-start | bytes 2949124
  32.5 1.0 copy-start.3
  33.5 0.7 copy-start.4
  41.9 11.8 %collective-permute-start.6 = (bf16[384,640]{1,0:T(8,128)(2,1)S(1)}, bf16[384,640]{1,0:T(8,128)(2,1)S(1)}, u32[]{:S(2)}, u32[]{:S(2)}) collective-permute-start(bf16[384,640]{1,0:T(8,128)(2,1)S(1)} %attend.1), channel_id=1, source_target_pairs={{0,16},{1,0},{2,18},{3,2},{4,20},{5,4},{6,22},{7,6},{8,24},{9,8},{... | collective-permute-start | bytes 1474568 | tf_op jit(solution)/shard_map/rows_1/ppermute | solution.py:162
  43.4 10.2 %collective-permute-start.7 = (bf16[384,640]{1,0:T(8,128)(2,1)S(1)}, bf16[384,640]{1,0:T(8,128)(2,1)S(1)}, u32[]{:S(2)}, u32[]{:S(2)}) collective-permute-start(bf16[384,640]{1,0:T(8,128)(2,1)S(1)} %attend.1), channel_id=1, source_target_pairs={{1,16},{3,18},{5,20},{7,22},{9,24},{11,26},{13,28},{15,30},{16,1},... | collective-permute-start | bytes 1474568 | tf_op jit(solution)/shard_map/rows_2/ppermute | solution.py:162
  48.2 20.0 %collective-permute-start.9 = (bf16[640,640]{1,0:T(8,128)(2,1)}, bf16[640,640]{1,0:T(8,128)(2,1)}, u32[]{:S(2)}, u32[]{:S(2)}) collective-permute-start(bf16[640,640]{1,0:T(8,128)(2,1)} %collective-permute-done.8), channel_id=1, source_target_pairs={{0,4},{1,5},{2,14},{3,15},{4,8},{5,9},{6,2},{7,3},{8,12},{9,13},{1... | collective-permute-start | bytes 2457608 | tf_op jit(solution)/shard_map/ring_2/ppermute | solution.py:162
  55.4 3.7 %collective-permute-start = (bf16[640,640]{1,0:T(8,128)(2,1)}, bf16[640,640]{1,0:T(8,128)(2,1)S(1)}, u32[]{:S(2)}, u32[]{:S(2)}) collective-permute-start(bf16[640,640]{1,0:T(8,128)(2,1)} %get-tuple-element.51), channel_id=1, source_target_pairs={{0,1},{1,0},{2,3},{3,2},{4,5},{5,4},{6,7},{7,6},{8,9},{9,8},{10,11... | collective-permute-start | bytes 2457608 | tf_op jit(solution)/shard_map/cond/branch_1_fun/core_swap/ppermute | solution.py:162
  61.5 6.7 %collective-permute-start.11 = (bf16[384,640]{1,0:T(8,128)(2,1)}, bf16[384,640]{1,0:T(8,128)(2,1)S(1)}, u32[]{:S(2)}, u32[]{:S(2)}) collective-permute-start(bf16[384,640]{1,0:T(8,128)(2,1)} %get-tuple-element.114), channel_id=1, source_target_pairs={{0,3},{2,1},{4,4},{6,6},{8,9},{10,11},{12,14},{14,12},{17,19},{19,... | collective-permute-start | bytes 1474568 | tf_op jit(solution)/shard_map/sums_1/ppermute | solution.py:162
  63.2 11.3 %collective-permute-start.12 = (bf16[384,640]{1,0:T(8,128)(2,1)}, bf16[384,640]{1,0:T(8,128)(2,1)S(1)}, u32[]{:S(2)}, u32[]{:S(2)}) collective-permute-start(bf16[384,640]{1,0:T(8,128)(2,1)} %get-tuple-element.114), channel_id=1, source_target_pairs={{1,19},{3,17},{5,20},{7,22},{9,25},{11,27},{13,30},{15,28},{16,3},... | collective-permute-start | bytes 1474568 | tf_op jit(solution)/shard_map/sums_cross_1/ppermute | solution.py:162
  64.5 2.0 %copy-start.6 = (bf16[640,640]{1,0:T(8,128)(2,1)S(1)}, bf16[640,640]{1,0:T(8,128)(2,1)}, u32[]{:S(2)}) copy-start(bf16[640,640]{1,0:T(8,128)(2,1)} %get-tuple-element.49) | copy-start | bytes 2457604 | tf_op jit(solution)/shard_map/cond
  68.1 21.0 %collective-permute-start.10 = (bf16[640,640]{1,0:T(8,128)(2,1)}, bf16[640,640]{1,0:T(8,128)(2,1)}, u32[]{:S(2)}, u32[]{:S(2)}) collective-permute-start(bf16[640,640]{1,0:T(8,128)(2,1)} %collective-permute-done.9), channel_id=1, source_target_pairs={{0,4},{1,5},{2,14},{3,15},{4,8},{5,9},{6,2},{7,3},{8,12},{9,13},{1... | collective-permute-start | bytes 2457608 | tf_op jit(solution)/shard_map/ring_3/ppermute | solution.py:162
  74.5 2.7 %collective-permute-start.1 = (bf16[640,640]{1,0:T(8,128)(2,1)}, bf16[640,640]{1,0:T(8,128)(2,1)}, u32[]{:S(2)}, u32[]{:S(2)}) collective-permute-start(bf16[640,640]{1,0:T(8,128)(2,1)} %get-tuple-element.56), channel_id=1, source_target_pairs={{0,1},{1,0},{2,3},{3,2},{4,5},{5,4},{6,7},{7,6},{8,9},{9,8},{10,11... | collective-permute-start | bytes 2457608 | tf_op jit(solution)/shard_map/cond/branch_1_fun/core_swap/ppermute | solution.py:162
  80.1 14.2 %collective-permute-start.13 = (bf16[384,640]{1,0:T(8,128)(2,1)}, bf16[384,640]{1,0:T(8,128)(2,1)S(1)}, u32[]{:S(2)}, u32[]{:S(2)}) collective-permute-start(bf16[384,640]{1,0:T(8,128)(2,1)} %get-tuple-element.95), channel_id=1, source_target_pairs={{0,0},{2,2},{4,5},{6,7},{8,10},{10,8},{12,15},{14,13},{17,16},{19,... | collective-permute-start | bytes 1474568 | tf_op jit(solution)/shard_map/sums_02/ppermute | solution.py:162
  82.1 12.1 %collective-permute-start.14 = (bf16[384,640]{1,0:T(8,128)(2,1)}, bf16[384,640]{1,0:T(8,128)(2,1)}, u32[]{:S(2)}, u32[]{:S(2)}) collective-permute-start(bf16[384,640]{1,0:T(8,128)(2,1)} %get-tuple-element.95), channel_id=1, source_target_pairs={{1,16},{3,18},{5,21},{7,23},{9,26},{11,24},{13,31},{15,29},{16,0},... | collective-permute-start | bytes 1474568 | tf_op jit(solution)/shard_map/sums_cross_02/ppermute | solution.py:162
  83.6 13.3 %collective-permute-start.15 = (bf16[384,640]{1,0:T(8,128)(2,1)}, bf16[384,640]{1,0:T(8,128)(2,1)}, u32[]{:S(2)}, u32[]{:S(2)}) collective-permute-start(bf16[384,640]{1,0:T(8,128)(2,1)} %get-tuple-element.96), channel_id=1, source_target_pairs={{0,2},{2,0},{4,7},{6,5},{8,8},{10,10},{12,13},{14,15},{17,18},{19,... | collective-permute-start | bytes 1474568 | tf_op jit(solution)/shard_map/sums_20/ppermute | solution.py:162
  87.7 9.3 %collective-permute-start.16 = (bf16[384,640]{1,0:T(8,128)(2,1)}, bf16[384,640]{1,0:T(8,128)(2,1)}, u32[]{:S(2)}, u32[]{:S(2)}) collective-permute-start(bf16[384,640]{1,0:T(8,128)(2,1)} %get-tuple-element.96), channel_id=1, source_target_pairs={{1,18},{3,16},{5,23},{7,21},{9,24},{11,26},{13,29},{15,31},{16,2},... | collective-permute-start | bytes 1474568 | tf_op jit(solution)/shard_map/sums_cross_20/ppermute | solution.py:162
  89.1 14.0 %copy-start.7 = (f32[1280]{0:T(1024)S(1)}, f32[1280]{0:T(1024)}, u32[]{:S(2)}) copy-start(f32[1280]{0:T(1024)} %param.18) | copy-start | bytes 15364
  89.1 2.7 %collective-permute-start.2 = (bf16[640,640]{1,0:T(8,128)(2,1)}, bf16[640,640]{1,0:T(8,128)(2,1)S(1)}, u32[]{:S(2)}, u32[]{:S(2)}) collective-permute-start(bf16[640,640]{1,0:T(8,128)(2,1)} %get-tuple-element.59), channel_id=1, source_target_pairs={{0,1},{1,0},{2,3},{3,2},{4,5},{5,4},{6,7},{7,6},{8,9},{9,8},{10,11... | collective-permute-start | bytes 2457608 | tf_op jit(solution)/shard_map/cond/branch_1_fun/core_swap/ppermute | solution.py:162
  97.0 17.0 %collective-permute-start.17 = (bf16[384,640]{1,0:T(8,128)(2,1)}, bf16[384,640]{1,0:T(8,128)(2,1)S(1)}, u32[]{:S(2)}, u32[]{:S(2)}) collective-permute-start(bf16[384,640]{1,0:T(8,128)(2,1)} %get-tuple-element.115), channel_id=1, source_target_pairs={{0,1},{2,3},{4,6},{6,4},{8,11},{10,9},{12,12},{14,14},{17,17},{19,... | collective-permute-start | bytes 1474568 | tf_op jit(solution)/shard_map/sums_3/ppermute | solution.py:162
  101.8 13.1 %collective-permute-start.18 = (bf16[384,640]{1,0:T(8,128)(2,1)}, bf16[384,640]{1,0:T(8,128)(2,1)S(1)}, u32[]{:S(2)}, u32[]{:S(2)}) collective-permute-start(bf16[384,640]{1,0:T(8,128)(2,1)} %get-tuple-element.115), channel_id=1, source_target_pairs={{1,17},{3,19},{5,22},{7,20},{9,27},{11,25},{13,28},{15,30},{16,1},... | collective-permute-start | bytes 1474568 | tf_op jit(solution)/shard_map/sums_cross_3/ppermute | solution.py:162
  103.1 1.5 %copy-start.1 = (f32[384,1280]{1,0:T(8,128)S(1)}, f32[384,1280]{1,0:T(8,128)}, u32[]{:S(2)}) copy-start(f32[384,1280]{1,0:T(8,128)} %refs_6_.1) | copy-start | bytes 5898244

commit v4 on v3

--- a/solution.py
+++ b/solution.py
@@ -248,8 +248,10 @@
     def swapped(w):
         return send(w, sibling, "core_swap")
 
-    def begin(rows_own, rows_sib, w1):
-        return sums(rows_own, rows_sib, w1, swapped(w1))
+    def begin(rows_own, rows_sib, w0, v0, w1):
+        v1 = swapped(w1)
+        s0 = sums(rows_own, rows_sib, w0, v0)
+        return s0, sums(rows_own, rows_sib, w1, v1)
 
     def mix(rows_own, rows_sib, s0, w2):
         s2 = sums(rows_own, rows_sib, w2, swapped(w2))
@@ -263,17 +265,15 @@
     first, second, token = tie((first, second, token))
     rows_own = jnp.where(here, attended, first)
     rows_sib = jnp.where(here, first, second)
-    s1 = region(token, begin, rows_own, rows_sib, w1)
+    s0, s1 = region(token, begin, rows_own, rows_sib, w0, v0, w1)
     middle = to_owners(s1, (1, 1), "1")
-    s0 = region(token, sums, rows_own, rows_sib, w0, v0)
     w2, s0 = tie((w2, s0))
     w3 = send(w2, ring, "ring_3")
-    w2, *middle = tie((w2, *middle))
     low_sum, high_sum = region(token, mix, rows_own, rows_sib, s0, w2)
+    low_sum, high_sum, *middle = tie((low_sum, high_sum, *middle))
     early = to_owners(low_sum, (0, 2), "02") + to_owners(high_sum, (2, 0), "20")
     w3, low_sum, high_sum = tie((w3, low_sum, high_sum))
     s3 = region(token, end, rows_own, rows_sib, w3)
-    s3, *early = tie((s3, *early))
     middle += early
     last = to_owners(s3, (3, 3), "3")
     spot = jnp.reshape(y, (1,))

time: 118 us -> 116 us (0.983)
  waiting for transfers between devices: 46.6 us -> 40 us
  starting transfers between devices: 31.7 us -> 35 us
    ppermute x17, waiting for transfers between devices: 27.1 us -> 20.6 us  [send(): return lax.ppermute(array, AXES, route)]
    ppermute x17, starting transfers between devices: 25.6 us -> 29 us  [send(): return lax.ppermute(array, AXES, route)]
    unnamed x14 -> x16, local copies, waits for them, and re-layouts: 4.44 us -> 4.44 us
  transfers between devices with their start and end apart: 19 -> 19, of which waited for: 12 -> 10; matrix products, arithmetic and copies ran while one was open for 17% -> 18% of each run, Pallas kernels for 10% -> 10%
where the time goes in v4:
time: 116 us; the launch traced here: 114 us
  waiting for transfers between devices  40 us (34%)
  starting transfers between devices  35 us (30%)
  matrix products  17 us (15%)
  Pallas kernels  13.3 us (11%)
  local copies, waits for them, and re-layouts  5.41 us (5%)
  other arithmetic  2.78 us (2%)
    ppermute x17, starting transfers between devices, send(): return lax.ppermute(array, AXES, route)  29 us
    ppermute x17, waiting for transfers between devices, send(): return lax.ppermute(array, AXES, route)  20.6 us
    ppermute x1, waiting for transfers between devices, halos(): lax.ppermute(keyvals, 'frame', forward)  16.1 us
    dot_general x4, matrix products, sums(): total = total + jnp.dot(rows_sib, sib, preferred_element_type=jnp.float32)  9.39 us
    pallas_call x1, Pallas kernels, attend(): pl.pallas_call(attend_kernel, out_shape=jax.ShapeDtypeStruct((rows, width...  7.69 us
    dot_general x4, matrix products, sums(): total = jnp.dot(rows_own, own, preferred_element_type=jnp.float32)  7.58 us
    pallas_call x2, Pallas kernels, finish(): pl.pallas_call(finish_kernel, grid=(rows // step,), out_shape=jax.ShapeDt...  4.45 us
    unnamed x16, local copies, waits for them, and re-layouts  4.44 us
  transfers between devices with their start and end apart: 19, of which 10 were waited for; matrix products, arithmetic and copies ran while one was open for 18% of the time, Pallas kernels for 10%

profile of v4, /device:TPU:8, one launch (start us, length us, event | category | flops | bytes accessed | tf_op | source)
XLA Modules:
  0.0 114.4 jit_solution(10781673845541607770)
XLA Ops:
  0.0 3.6 %collective-permute-start.4 = (bf16[2,384,640]{2,1,0:T(8,128)(2,1)}, bf16[2,384,640]{2,1,0:T(8,128)(2,1)S(1)}, u32[]{:S(2)}, u32[]{:S(2)}) collective-permute-start(bf16[2,384,640]{2,1,0:T(8,128)(2,1)} %own_ref.1), channel_id=1, source_target_pairs={{0,4},{4,8},{8,12},{1,5},{5,9},{9,13},{2,6},{6,10},{10,14},{3,7},{... | collective-permute-start | bytes 2949128 | tf_op jit(solution)/shard_map/ppermute | solution.py:119
  3.6 2.4 %collective-permute-start.5 = (bf16[2,384,640]{2,1,0:T(8,128)(2,1)}, bf16[2,384,640]{2,1,0:T(8,128)(2,1)}, u32[]{:S(2)}, u32[]{:S(2)}) collective-permute-start(bf16[2,384,640]{2,1,0:T(8,128)(2,1)} %own_ref.1), channel_id=1, source_target_pairs={{4,0},{8,4},{12,8},{5,1},{9,5},{13,9},{6,2},{10,6},{14,10},{7,3},{... | collective-permute-start | bytes 2949128 | tf_op jit(solution)/shard_map/ppermute | solution.py:119
  6.1 1.0 constant_dynamic-slice_fusion
  7.0 2.5 %collective-permute-done.3 = bf16[640,640]{1,0:T(8,128)(2,1)S(1)} collective-permute-done((bf16[640,640]{1,0:T(8,128)(2,1)}, bf16[640,640]{1,0:T(8,128)(2,1)S(1)}, u32[]{:S(2)}, u32[]{:S(2)}) %collective-permute-start.3) | collective-permute-done | bytes 819232 | tf_op jit(solution)/shard_map/core_swap_0/ppermute | solution.py:162
  9.6 16.1 %collective-permute-done.4.low_ref = bf16[2,384,640]{2,1,0:T(8,128)(2,1)S(1)} collective-permute-done((bf16[2,384,640]{2,1,0:T(8,128)(2,1)}, bf16[2,384,640]{2,1,0:T(8,128)(2,1)S(1)}, u32[]{:S(2)}, u32[]{:S(2)}) %collective-permute-start.4) | collective-permute-done | bytes 983072 | tf_op jit(solution)/shard_map/ppermute | solution.py:119
  25.7 3.3 %collective-permute-done.5.high_ref = bf16[2,384,640]{2,1,0:T(8,128)(2,1)} collective-permute-done((bf16[2,384,640]{2,1,0:T(8,128)(2,1)}, bf16[2,384,640]{2,1,0:T(8,128)(2,1)}, u32[]{:S(2)}, u32[]{:S(2)}) %collective-permute-start.5) | collective-permute-done | bytes 983072 | tf_op jit(solution)/shard_map/ppermute | solution.py:119
  29.0 1.6 %collective-permute-start.8 = (bf16[640,640]{1,0:T(8,128)(2,1)}, bf16[640,640]{1,0:T(8,128)(2,1)}, u32[]{:S(2)}, u32[]{:S(2)}) collective-permute-start(bf16[640,640]{1,0:T(8,128)(2,1)} %constant_dynamic-slice_fusion), channel_id=1, source_target_pairs={{0,4},{1,5},{2,14},{3,15},{4,8},{5,9},{6,2},{7,3},{8,12},{9,13},{1... | collective-permute-start | bytes 2457608 | tf_op jit(solution)/shard_map/ring_1/ppermute | solution.py:162
  30.6 0.7 subtract_clamp_fusion.ids
  31.3 1.2 %copy-done.2 = bf16[2,384,640]{2,1,0:T(8,128)(2,1)S(1)} copy-done((bf16[2,384,640]{2,1,0:T(8,128)(2,1)S(1)}, bf16[2,384,640]{2,1,0:T(8,128)(2,1)}, u32[]{:S(2)}) %copy-start.2) | copy-done | bytes 983064
  32.5 1.0 copy-done.3
  33.6 0.7 copy-done.4
  34.2 7.7 %attend.1 = bf16[384,640]{1,0:T(8,128)(2,1)S(1)} custom-call(s32[6,8]{1,0:T(8,128)S(1)} %subtract_clamp_fusion.ids, s32[6]{0:T(128)S(1)} %copy-done.4, bf16[384,640]{1,0:T(8,128)(2,1)S(1)} %copy-done.3, bf16[2,384,640]{2,1,0:T(8,128)(2,1)S(1)} %copy-done.2, bf16[2,384,640]{2,1,0:T(8,128)(2,1)S(1)} %collective-permute-done.4.low_ref, ...), custom_call_target="tpu_custom_call" | custom-call | flops 8000000000 | bytes 24000000 | tf_op jit(solution)/shard_map/attend/pallas_call | solution.py:100
  41.9 1.5 %collective-permute-start.6 = (bf16[384,640]{1,0:T(8,128)(2,1)S(1)}, bf16[384,640]{1,0:T(8,128)(2,1)}, u32[]{:S(2)}, u32[]{:S(2)}) collective-permute-start(bf16[384,640]{1,0:T(8,128)(2,1)S(1)} %attend.1), channel_id=1, source_target_pairs={{0,16},{1,0},{2,18},{3,2},{4,20},{5,4},{6,22},{7,6},{8,24},{9,8},{... | collective-permute-start | bytes 1474568 | tf_op jit(solution)/shard_map/rows_1/ppermute | solution.py:162
  43.4 1.4 %collective-permute-start.7 = (bf16[384,640]{1,0:T(8,128)(2,1)S(1)}, bf16[384,640]{1,0:T(8,128)(2,1)}, u32[]{:S(2)}, u32[]{:S(2)}) collective-permute-start(bf16[384,640]{1,0:T(8,128)(2,1)S(1)} %attend.1), channel_id=1, source_target_pairs={{1,16},{3,18},{5,20},{7,22},{9,24},{11,26},{13,28},{15,30},{16,1},... | collective-permute-start | bytes 1474568 | tf_op jit(solution)/shard_map/rows_2/ppermute | solution.py:162
  44.9 3.3 %collective-permute-done.8 = bf16[640,640]{1,0:T(8,128)(2,1)} collective-permute-done((bf16[640,640]{1,0:T(8,128)(2,1)}, bf16[640,640]{1,0:T(8,128)(2,1)}, u32[]{:S(2)}, u32[]{:S(2)}) %collective-permute-start.8) | collective-permute-done | bytes 819232 | tf_op jit(solution)/shard_map/ring_1/ppermute | solution.py:162
  48.2 1.6 %collective-permute-start.9 = (bf16[640,640]{1,0:T(8,128)(2,1)}, bf16[640,640]{1,0:T(8,128)(2,1)}, u32[]{:S(2)}, u32[]{:S(2)}) collective-permute-start(bf16[640,640]{1,0:T(8,128)(2,1)} %collective-permute-done.8), channel_id=1, source_target_pairs={{0,4},{1,5},{2,14},{3,15},{4,8},{5,9},{6,2},{7,3},{8,12},{9,13},{1... | collective-permute-start | bytes 2457608 | tf_op jit(solution)/shard_map/ring_2/ppermute | solution.py:162
  49.7 1.2 %fence.1 = s32[1]{0:T(128)} custom-call(s32[1]{0:T(128)} %bitcast.19), custom_call_target="tpu_custom_call" | custom-call | flops 49999998976 | bytes 150000000 | tf_op jit(solution)/shard_map/fence/pallas_call | solution.py:30
  50.9 2.8 %collective-permute-done.6 = bf16[384,640]{1,0:T(8,128)(2,1)} collective-permute-done((bf16[384,640]{1,0:T(8,128)(2,1)S(1)}, bf16[384,640]{1,0:T(8,128)(2,1)}, u32[]{:S(2)}, u32[]{:S(2)}) %collective-permute-start.6) | collective-permute-done | bytes 491552 | tf_op jit(solution)/shard_map/rows_1/ppermute | solution.py:162
  54.3 2.1 %broadcast_select_fusion.2 = (bf16[384,640]{1,0:T(8,128)(2,1)}, bf16[384,640]{1,0:T(8,128)(2,1)}) fusion(bf16[384,640]{1,0:T(8,128)(2,1)} %collective-permute-done.6, bf16[384,640]{1,0:T(8,128)(2,1)} %collective-permute-done.7, pred[]{:T(512)S(6)} %eq.7, bf16[384,640]{1,0:T(8,128)(2,1)S(1)} %attend.1), kind=kLoop, calls=%fused_computation.10 | loop fusion | flops 491520 | bytes 2457601 | tf_op jit(solution)/shard_map/jit(_where)/select_n | solution.py:267
  56.4 9.5 %conditional.3 = (bf16[384,640]{1,0:T(8,128)(2,1)S(1)}, bf16[384,640]{1,0:T(8,128)(2,1)}) conditional(s32[]{:T(128)} %bitcast.1, () %tuple.37, (bf16[384,640]{1,0:T(8,128)(2,1)}, bf16[640,640]{1,0:T(8,128)(2,1)}, bf16[384,640]{1,0:T(8,128)(2,1)}, bf16[640,640]{1,0:T(8,128)(2,1)S(1)}, bf16[640,640]{1,0:T(8,128)(2,1)}) %tuple.53), branch_computations={%region_0.1_spmd, %region_1.2_spmd} | conditional | flops 1259274240 | bytes 13434936 | solution.py:236
  56.4 1.6 %collective-permute-start = (bf16[640,640]{1,0:T(8,128)(2,1)}, bf16[640,640]{1,0:T(8,128)(2,1)S(1)}, u32[]{:S(2)}, u32[]{:S(2)}) collective-permute-start(bf16[640,640]{1,0:T(8,128)(2,1)} %get-tuple-element.40), channel_id=1, source_target_pairs={{0,1},{1,0},{2,3},{3,2},{4,5},{5,4},{6,7},{7,6},{8,9},{9,8},{10,11... | collective-permute-start | bytes 2457608 | tf_op jit(solution)/shard_map/cond/branch_1_fun/core_swap/ppermute | solution.py:162
  58.0 1.9 %fusion.5 = f32[384,640]{1,0:T(8,128)S(1)} fusion(bf16[384,640]{1,0:T(8,128)(2,1)} %get-tuple-element.36, bf16[640,640]{1,0:T(8,128)(2,1)} %get-tuple-element.40), kind=kOutput, calls=%fused_computation.15 | convolution fusion | flops 314572800 | bytes 2293760 | tf_op jit(solution)/shard_map/cond/branch_1_fun/dot_general | solution.py:244
  60.0 1.9 %fusion.4 = f32[384,640]{1,0:T(8,128)S(1)} fusion(bf16[384,640]{1,0:T(8,128)(2,1)} %get-tuple-element.36, bf16[640,640]{1,0:T(8,128)(2,1)} %get-tuple-element.37), kind=kOutput, calls=%fused_computation.14 | convolution fusion | flops 314572800 | bytes 2293760 | tf_op jit(solution)/shard_map/cond/branch_1_fun/dot_general | solution.py:244
  61.9 1.6 %fusion = bf16[384,640]{1,0:T(8,128)(2,1)S(1)} fusion(f32[384,640]{1,0:T(8,128)S(1)} %fusion.4, bf16[384,640]{1,0:T(8,128)(2,1)} %get-tuple-element.38, bf16[640,640]{1,0:T(8,128)(2,1)S(1)} %get-tuple-element.39), kind=kOutput, calls=%fused_computation.2 | convolution fusion | flops 315064320 | bytes 2785280 | tf_op jit(solution)/shard_map/cond/branch_1_fun/dot_general | solution.py:245
  63.5 2.4 %fusion.1 = bf16[384,640]{1,0:T(8,128)(2,1)} fusion(f32[384,640]{1,0:T(8,128)S(1)} %fusion.5, bf16[384,640]{1,0:T(8,128)(2,1)} %get-tuple-element.38, bf16[640,640]{1,0:T(8,128)(2,1)S(1)} %collective-permute-done), kind=kOutput, calls=%fused_computation.3 | convolution fusion | flops 315064320 | bytes 2785280 | tf_op jit(solution)/shard_map/cond/branch_1_fun/dot_general | solution.py:245
  65.9 1.7 %collective-permute-start.11 = (bf16[384,640]{1,0:T(8,128)(2,1)}, bf16[384,640]{1,0:T(8,128)(2,1)S(1)}, u32[]{:S(2)}, u32[]{:S(2)}) collective-permute-start(bf16[384,640]{1,0:T(8,128)(2,1)} %get-tuple-element.83), channel_id=1, source_target_pairs={{0,3},{2,1},{4,4},{6,6},{8,9},{10,11},{12,14},{14,12},{17,19},{19,... | collective-permute-start | bytes 1474568 | tf_op jit(solution)/shard_map/sums_1/ppermute | solution.py:162
  67.6 1.3 %collective-permute-start.12 = (bf16[384,640]{1,0:T(8,128)(2,1)}, bf16[384,640]{1,0:T(8,128)(2,1)S(1)}, u32[]{:S(2)}, u32[]{:S(2)}) collective-permute-start(bf16[384,640]{1,0:T(8,128)(2,1)} %get-tuple-element.83), channel_id=1, source_target_pairs={{1,19},{3,17},{5,20},{7,22},{9,25},{11,27},{13,30},{15,28},{16,3},... | collective-permute-start | bytes 1474568 | tf_op jit(solution)/shard_map/sums_cross_1/ppermute | solution.py:162
  69.0 8.3 %conditional.4 = (bf16[384,640]{1,0:T(8,128)(2,1)}, bf16[384,640]{1,0:T(8,128)(2,1)}) conditional(s32[]{:T(128)} %bitcast.1, () %tuple.40, (s32[]{:T(128)}, bf16[384,640]{1,0:T(8,128)(2,1)}, bf16[640,640]{1,0:T(8,128)(2,1)}, bf16[384,640]{1,0:T(8,128)(2,1)}, bf16[384,640]{1,0:T(8,128)(2,1)S(1)}) %tuple.41), branch_computations={%region_2.3_spmd, %region_3.4_spmd} | conditional | flops 630128640 | bytes 9338946 | solution.py:236
  69.0 3.0 %collective-permute-start.1 = (bf16[640,640]{1,0:T(8,128)(2,1)}, bf16[640,640]{1,0:T(8,128)(2,1)}, u32[]{:S(2)}, u32[]{:S(2)}) collective-permute-start(bf16[640,640]{1,0:T(8,128)(2,1)} %get-tuple-element.44), channel_id=1, source_target_pairs={{0,1},{1,0},{2,3},{3,2},{4,5},{5,4},{6,7},{7,6},{8,9},{9,8},{10,11... | collective-permute-start | bytes 2457608 | tf_op jit(solution)/shard_map/cond/branch_1_fun/core_swap/ppermute | solution.py:162
  72.0 1.9 %fusion.6 = f32[384,640]{1,0:T(8,128)S(1)} fusion(bf16[384,640]{1,0:T(8,128)(2,1)} %get-tuple-element.43, bf16[640,640]{1,0:T(8,128)(2,1)} %get-tuple-element.44), kind=kOutput, calls=%fused_computation.16 | convolution fusion | flops 314572800 | bytes 2293760 | tf_op jit(solution)/shard_map/cond/branch_1_fun/dot_general | solution.py:244
  73.9 0.4 collective-permute-done.1
  74.3 2.9 %broadcast_select_fusion = (bf16[384,640]{1,0:T(8,128)(2,1)}, bf16[384,640]{1,0:T(8,128)(2,1)}) fusion(bf16[384,640]{1,0:T(8,128)(2,1)S(1)} %get-tuple-element.42, pred[]{:T(512)S(6)} %eq.5, f32[384,640]{1,0:T(8,128)S(1)} %fusion.6, bf16[384,640]{1,0:T(8,128)(2,1)} %get-tuple-element.45, bf16[640,640]{1,0:T(8,128)(2,1)} %collective-permute-done.1), kind=kOutput, calls=%fused_computation.6 | convolution fusion | flops 315555840 | bytes 3768321 | tf_op jit(solution)/shard_map/cond/branch_1_fun/dot_general | solution.py:245
  77.2 1.4 %collective-permute-done.12.refs_3_ = bf16[384,640]{1,0:T(8,128)(2,1)S(1)} collective-permute-done((bf16[384,640]{1,0:T(8,128)(2,1)}, bf16[384,640]{1,0:T(8,128)(2,1)S(1)}, u32[]{:S(2)}, u32[]{:S(2)}) %collective-permute-start.12) | collective-permute-done | bytes 491552 | tf_op jit(solution)/shard_map/sums_cross_1/ppermute | solution.py:162
  78.6 1.3 %collective-permute-start.15 = (bf16[384,640]{1,0:T(8,128)(2,1)}, bf16[384,640]{1,0:T(8,128)(2,1)S(1)}, u32[]{:S(2)}, u32[]{:S(2)}) collective-permute-start(bf16[384,640]{1,0:T(8,128)(2,1)} %get-tuple-element.84), channel_id=1, source_target_pairs={{0,0},{2,2},{4,5},{6,7},{8,10},{10,8},{12,15},{14,13},{17,16},{19,... | collective-permute-start | bytes 1474568 | tf_op jit(solution)/shard_map/sums_02/ppermute | solution.py:162
  79.9 1.5 %collective-permute-start.17 = (bf16[384,640]{1,0:T(8,128)(2,1)}, bf16[384,640]{1,0:T(8,128)(2,1)}, u32[]{:S(2)}, u32[]{:S(2)}) collective-permute-start(bf16[384,640]{1,0:T(8,128)(2,1)} %get-tuple-element.84), channel_id=1, source_target_pairs={{1,16},{3,18},{5,21},{7,23},{9,26},{11,24},{13,31},{15,29},{16,0},... | collective-permute-start | bytes 1474568 | tf_op jit(solution)/shard_map/sums_cross_02/ppermute | solution.py:162
  81.4 5.1 %collective-permute-start.16 = (bf16[384,640]{1,0:T(8,128)(2,1)}, bf16[384,640]{1,0:T(8,128)(2,1)}, u32[]{:S(2)}, u32[]{:S(2)}) collective-permute-start(bf16[384,640]{1,0:T(8,128)(2,1)} %get-tuple-element.85), channel_id=1, source_target_pairs={{0,2},{2,0},{4,7},{6,5},{8,8},{10,10},{12,13},{14,15},{17,18},{19,... | collective-permute-start | bytes 1474568 | tf_op jit(solution)/shard_map/sums_20/ppermute | solution.py:162
  86.5 1.4 %collective-permute-start.18 = (bf16[384,640]{1,0:T(8,128)(2,1)}, bf16[384,640]{1,0:T(8,128)(2,1)}, u32[]{:S(2)}, u32[]{:S(2)}) collective-permute-start(bf16[384,640]{1,0:T(8,128)(2,1)} %get-tuple-element.85), channel_id=1, source_target_pairs={{1,18},{3,16},{5,23},{7,21},{9,24},{11,26},{13,29},{15,31},{16,2},... | collective-permute-start | bytes 1474568 | tf_op jit(solution)/shard_map/sums_cross_20/ppermute | solution.py:162
  87.9 6.9 %conditional.5 = (bf16[384,640]{1,0:T(8,128)(2,1)}) conditional(s32[]{:T(128)} %bitcast.1, () %tuple.36, (bf16[384,640]{1,0:T(8,128)(2,1)}, bf16[640,640]{1,0:T(8,128)(2,1)}, bf16[384,640]{1,0:T(8,128)(2,1)}) %tuple.44), branch_computations={%region_4.5_spmd, %region_5.6_spmd} | conditional | flops 629637120 | bytes 8355888 | solution.py:236
  87.9 2.3 %collective-permute-start.2 = (bf16[640,640]{1,0:T(8,128)(2,1)}, bf16[640,640]{1,0:T(8,128)(2,1)S(1)}, u32[]{:S(2)}, u32[]{:S(2)}) collective-permute-start(bf16[640,640]{1,0:T(8,128)(2,1)} %get-tuple-element.47), channel_id=1, source_target_pairs={{0,1},{1,0},{2,3},{3,2},{4,5},{5,4},{6,7},{7,6},{8,9},{9,8},{10,11... | collective-permute-start | bytes 2457608 | tf_op jit(solution)/shard_map/cond/branch_1_fun/core_swap/ppermute | solution.py:162
  90.2 1.9 %fusion.7 = f32[384,640]{1,0:T(8,128)S(1)} fusion(bf16[384,640]{1,0:T(8,128)(2,1)} %get-tuple-element.46, bf16[640,640]{1,0:T(8,128)(2,1)} %get-tuple-element.47), kind=kOutput, calls=%fused_computation.17 | convolution fusion | flops 314572800 | bytes 2293760 | tf_op jit(solution)/shard_map/cond/branch_1_fun/dot_general | solution.py:244
  92.4 2.4 %fusion.3 = bf16[384,640]{1,0:T(8,128)(2,1)} fusion(f32[384,640]{1,0:T(8,128)S(1)} %fusion.7, bf16[384,640]{1,0:T(8,128)(2,1)} %get-tuple-element.48, bf16[640,640]{1,0:T(8,128)(2,1)S(1)} %collective-permute-done.2), kind=kOutput, calls=%fused_computation.9 | convolution fusion | flops 315064320 | bytes 2785280 | tf_op jit(solution)/shard_map/cond/branch_1_fun/dot_general | solution.py:245
  94.8 2.3 %collective-permute-start.13 = (bf16[384,640]{1,0:T(8,128)(2,1)}, bf16[384,640]{1,0:T(8,128)(2,1)S(1)}, u32[]{:S(2)}, u32[]{:S(2)}) collective-permute-start(bf16[384,640]{1,0:T(8,128)(2,1)} %get-tuple-element.101), channel_id=1, source_target_pairs={{0,1},{2,3},{4,6},{6,4},{8,11},{10,9},{12,12},{14,14},{17,17},{19,... | collective-permute-start | bytes 1474568 | tf_op jit(solution)/shard_map/sums_3/ppermute | solution.py:162
  97.1 1.3 %collective-permute-start.14 = (bf16[384,640]{1,0:T(8,128)(2,1)}, bf16[384,640]{1,0:T(8,128)(2,1)S(1)}, u32[]{:S(2)}, u32[]{:S(2)}) collective-permute-start(bf16[384,640]{1,0:T(8,128)(2,1)} %get-tuple-element.101), channel_id=1, source_target_pairs={{1,17},{3,19},{5,22},{7,20},{9,27},{11,25},{13,28},{15,30},{16,1},... | collective-permute-start | bytes 1474568 | tf_op jit(solution)/shard_map/sums_cross_3/ppermute | solution.py:162
  98.5 1.5 %copy-done.1 = f32[384,1280]{1,0:T(8,128)S(1)} copy-done((f32[384,1280]{1,0:T(8,128)S(1)}, f32[384,1280]{1,0:T(8,128)}, u32[]{:S(2)}) %copy-start.1) | copy-done | bytes 1966104
  100.0 2.6 %finish.2.refs_2_ = f32[384,1280]{1,0:T(8,128)S(1)} custom-call(s32[1]{0:T(128)} %bitcast.spot, bf16[384,640]{1,0:T(8,128)(2,1)S(1)} %collective-permute-done.11.refs_0_, bf16[384,640]{1,0:T(8,128)(2,1)S(1)} %collective-permute-done.15.refs_1_, bf16[384,640]{1,0:T(8,128)(2,1)} %collective-permute-done.16.refs_2_, ...), custom_call_target="tpu_custom_call" | custom-call | tf_op jit(solution)/shard_map/finish/pallas_call | solution.py:186
  102.6 5.4 %collective-permute-done.13.refs_0_ = bf16[384,640]{1,0:T(8,128)(2,1)S(1)} collective-permute-done((bf16[384,640]{1,0:T(8,128)(2,1)}, bf16[384,640]{1,0:T(8,128)(2,1)S(1)}, u32[]{:S(2)}, u32[]{:S(2)}) %collective-permute-start.13) | collective-permute-done | bytes 491552 | tf_op jit(solution)/shard_map/sums_3/ppermute | solution.py:162
  108.0 4.5 %collective-permute-done.14.refs_1_ = bf16[384,640]{1,0:T(8,128)(2,1)S(1)} collective-permute-done((bf16[384,640]{1,0:T(8,128)(2,1)}, bf16[384,640]{1,0:T(8,128)(2,1)S(1)}, u32[]{:S(2)}, u32[]{:S(2)}) %collective-permute-start.14) | collective-permute-done | bytes 491552 | tf_op jit(solution)/shard_map/sums_cross_3/ppermute | solution.py:162
  112.6 1.9 %finish.3 = f32[384,1280]{1,0:T(8,128)} custom-call(s32[1]{0:T(128)} %bitcast.spot, bf16[384,640]{1,0:T(8,128)(2,1)S(1)} %collective-permute-done.13.refs_0_, bf16[384,640]{1,0:T(8,128)(2,1)S(1)} %collective-permute-done.14.refs_1_, f32[384,1280]{1,0:T(8,128)S(1)} %finish.2.refs_2_, f32[1,1280]{1,0:T(1,128)S(1)} %broadcast_in_dim.4.refs_7_.refs_3_), custom_call_target="tpu_custom_call" | custom-call | tf_op jit(solution)/shard_map/finish/pallas_call | solution.py:186
  (25 shorter events, 0.4 us)
Async XLA Ops:
  0.0 6.1 %copy-start = (bf16[640,1280]{1,0:T(8,128)(2,1)S(1)}, bf16[640,1280]{1,0:T(8,128)(2,1)}, u32[]{:S(2)}) copy-start(bf16[640,1280]{1,0:T(8,128)(2,1)} %param.17) | copy-start | bytes 4915204
  0.0 25.7 %collective-permute-start.4 = (bf16[2,384,640]{2,1,0:T(8,128)(2,1)}, bf16[2,384,640]{2,1,0:T(8,128)(2,1)S(1)}, u32[]{:S(2)}, u32[]{:S(2)}) collective-permute-start(bf16[2,384,640]{2,1,0:T(8,128)(2,1)} %own_ref.1), channel_id=1, source_target_pairs={{0,4},{4,8},{8,12},{1,5},{5,9},{9,13},{2,6},{6,10},{10,14},{3,7},{... | collective-permute-start | bytes 2949128 | tf_op jit(solution)/shard_map/ppermute | solution.py:119
  3.6 25.4 %collective-permute-start.5 = (bf16[2,384,640]{2,1,0:T(8,128)(2,1)}, bf16[2,384,640]{2,1,0:T(8,128)(2,1)}, u32[]{:S(2)}, u32[]{:S(2)}) collective-permute-start(bf16[2,384,640]{2,1,0:T(8,128)(2,1)} %own_ref.1), channel_id=1, source_target_pairs={{4,0},{8,4},{12,8},{5,1},{9,5},{13,9},{6,2},{10,6},{14,10},{7,3},{... | collective-permute-start | bytes 2949128 | tf_op jit(solution)/shard_map/ppermute | solution.py:119
  7.0 2.5 %collective-permute-start.3 = (bf16[640,640]{1,0:T(8,128)(2,1)}, bf16[640,640]{1,0:T(8,128)(2,1)S(1)}, u32[]{:S(2)}, u32[]{:S(2)}) collective-permute-start(bf16[640,640]{1,0:T(8,128)(2,1)} %constant_dynamic-slice_fusion), channel_id=1, source_target_pairs={{0,1},{1,0},{2,3},{3,2},{4,5},{5,4},{6,7},{7,6},{8,9},{9,8},{10,11... | collective-permute-start | bytes 2457608 | tf_op jit(solution)/shard_map/core_swap_0/ppermute | solution.py:162
  9.6 19.5 %copy-start.5 = (bf16[640,640]{1,0:T(8,128)(2,1)}, bf16[640,640]{1,0:T(8,128)(2,1)S(1)}, u32[]{:S(2)}) copy-start(bf16[640,640]{1,0:T(8,128)(2,1)S(1)} %collective-permute-done.3) | copy-start | bytes 2457604
  29.0 19.1 %collective-permute-start.8 = (bf16[640,640]{1,0:T(8,128)(2,1)}, bf16[640,640]{1,0:T(8,128)(2,1)}, u32[]{:S(2)}, u32[]{:S(2)}) collective-permute-start(bf16[640,640]{1,0:T(8,128)(2,1)} %constant_dynamic-slice_fusion), channel_id=1, source_target_pairs={{0,4},{1,5},{2,14},{3,15},{4,8},{5,9},{6,2},{7,3},{8,12},{9,13},{1... | collective-permute-start | bytes 2457608 | tf_op jit(solution)/shard_map/ring_1/ppermute | solution.py:162
  31.3 1.2 %copy-start.2 = (bf16[2,384,640]{2,1,0:T(8,128)(2,1)S(1)}, bf16[2,384,640]{2,1,0:T(8,128)(2,1)}, u32[]{:S(2)}) copy-start(bf16[2,384,640]{2,1,0:T(8,128)(2,1)} %own_ref.1) | copy-start | bytes 2949124
  32.5 1.0 copy-start.3
  33.5 0.7 copy-start.4
  41.9 11.8 %collective-permute-start.6 = (bf16[384,640]{1,0:T(8,128)(2,1)S(1)}, bf16[384,640]{1,0:T(8,128)(2,1)}, u32[]{:S(2)}, u32[]{:S(2)}) collective-permute-start(bf16[384,640]{1,0:T(8,128)(2,1)S(1)} %attend.1), channel_id=1, source_target_pairs={{0,16},{1,0},{2,18},{3,2},{4,20},{5,4},{6,22},{7,6},{8,24},{9,8},{... | collective-permute-start | bytes 1474568 | tf_op jit(solution)/shard_map/rows_1/ppermute | solution.py:162
  43.4 10.2 %collective-permute-start.7 = (bf16[384,640]{1,0:T(8,128)(2,1)S(1)}, bf16[384,640]{1,0:T(8,128)(2,1)}, u32[]{:S(2)}, u32[]{:S(2)}) collective-permute-start(bf16[384,640]{1,0:T(8,128)(2,1)S(1)} %attend.1), channel_id=1, source_target_pairs={{1,16},{3,18},{5,20},{7,22},{9,24},{11,26},{13,28},{15,30},{16,1},... | collective-permute-start | bytes 1474568 | tf_op jit(solution)/shard_map/rows_2/ppermute | solution.py:162
  48.2 20.7 %collective-permute-start.9 = (bf16[640,640]{1,0:T(8,128)(2,1)}, bf16[640,640]{1,0:T(8,128)(2,1)}, u32[]{:S(2)}, u32[]{:S(2)}) collective-permute-start(bf16[640,640]{1,0:T(8,128)(2,1)} %collective-permute-done.8), channel_id=1, source_target_pairs={{0,4},{1,5},{2,14},{3,15},{4,8},{5,9},{6,2},{7,3},{8,12},{9,13},{1... | collective-permute-start | bytes 2457608 | tf_op jit(solution)/shard_map/ring_2/ppermute | solution.py:162
  50.9 5.5 %copy-start.6 = (bf16[640,640]{1,0:T(8,128)(2,1)S(1)}, bf16[640,640]{1,0:T(8,128)(2,1)}, u32[]{:S(2)}) copy-start(bf16[640,640]{1,0:T(8,128)(2,1)} %copy-done.5) | copy-start | bytes 2457604
  56.4 7.1 %collective-permute-start = (bf16[640,640]{1,0:T(8,128)(2,1)}, bf16[640,640]{1,0:T(8,128)(2,1)S(1)}, u32[]{:S(2)}, u32[]{:S(2)}) collective-permute-start(bf16[640,640]{1,0:T(8,128)(2,1)} %get-tuple-element.40), channel_id=1, source_target_pairs={{0,1},{1,0},{2,3},{3,2},{4,5},{5,4},{6,7},{7,6},{8,9},{9,8},{10,11... | collective-permute-start | bytes 2457608 | tf_op jit(solution)/shard_map/cond/branch_1_fun/core_swap/ppermute | solution.py:162
  65.9 11.3 %collective-permute-start.11 = (bf16[384,640]{1,0:T(8,128)(2,1)}, bf16[384,640]{1,0:T(8,128)(2,1)S(1)}, u32[]{:S(2)}, u32[]{:S(2)}) collective-permute-start(bf16[384,640]{1,0:T(8,128)(2,1)} %get-tuple-element.83), channel_id=1, source_target_pairs={{0,3},{2,1},{4,4},{6,6},{8,9},{10,11},{12,14},{14,12},{17,19},{19,... | collective-permute-start | bytes 1474568 | tf_op jit(solution)/shard_map/sums_1/ppermute | solution.py:162
  67.6 11.0 %collective-permute-start.12 = (bf16[384,640]{1,0:T(8,128)(2,1)}, bf16[384,640]{1,0:T(8,128)(2,1)S(1)}, u32[]{:S(2)}, u32[]{:S(2)}) collective-permute-start(bf16[384,640]{1,0:T(8,128)(2,1)} %get-tuple-element.83), channel_id=1, source_target_pairs={{1,19},{3,17},{5,20},{7,22},{9,25},{11,27},{13,30},{15,28},{16,3},... | collective-permute-start | bytes 1474568 | tf_op jit(solution)/shard_map/sums_cross_1/ppermute | solution.py:162
  68.9 19.0 %collective-permute-start.10 = (bf16[640,640]{1,0:T(8,128)(2,1)}, bf16[640,640]{1,0:T(8,128)(2,1)}, u32[]{:S(2)}, u32[]{:S(2)}) collective-permute-start(bf16[640,640]{1,0:T(8,128)(2,1)} %collective-permute-done.9), channel_id=1, source_target_pairs={{0,4},{1,5},{2,14},{3,15},{4,8},{5,9},{6,2},{7,3},{8,12},{9,13},{1... | collective-permute-start | bytes 2457608 | tf_op jit(solution)/shard_map/ring_3/ppermute | solution.py:162
  69.0 5.3 %collective-permute-start.1 = (bf16[640,640]{1,0:T(8,128)(2,1)}, bf16[640,640]{1,0:T(8,128)(2,1)}, u32[]{:S(2)}, u32[]{:S(2)}) collective-permute-start(bf16[640,640]{1,0:T(8,128)(2,1)} %get-tuple-element.44), channel_id=1, source_target_pairs={{0,1},{1,0},{2,3},{3,2},{4,5},{5,4},{6,7},{7,6},{8,9},{9,8},{10,11... | collective-permute-start | bytes 2457608 | tf_op jit(solution)/shard_map/cond/branch_1_fun/core_swap/ppermute | solution.py:162
  78.6 18.5 %collective-permute-start.15 = (bf16[384,640]{1,0:T(8,128)(2,1)}, bf16[384,640]{1,0:T(8,128)(2,1)S(1)}, u32[]{:S(2)}, u32[]{:S(2)}) collective-permute-start(bf16[384,640]{1,0:T(8,128)(2,1)} %get-tuple-element.84), channel_id=1, source_target_pairs={{0,0},{2,2},{4,5},{6,7},{8,10},{10,8},{12,15},{14,13},{17,16},{19,... | collective-permute-start | bytes 1474568 | tf_op jit(solution)/shard_map/sums_02/ppermute | solution.py:162
  79.9 18.5 %collective-permute-start.17 = (bf16[384,640]{1,0:T(8,128)(2,1)}, bf16[384,640]{1,0:T(8,128)(2,1)}, u32[]{:S(2)}, u32[]{:S(2)}) collective-permute-start(bf16[384,640]{1,0:T(8,128)(2,1)} %get-tuple-element.84), channel_id=1, source_target_pairs={{1,16},{3,18},{5,21},{7,23},{9,26},{11,24},{13,31},{15,29},{16,0},... | collective-permute-start | bytes 1474568 | tf_op jit(solution)/shard_map/sums_cross_02/ppermute | solution.py:162
  81.4 17.1 %collective-permute-start.16 = (bf16[384,640]{1,0:T(8,128)(2,1)}, bf16[384,640]{1,0:T(8,128)(2,1)}, u32[]{:S(2)}, u32[]{:S(2)}) collective-permute-start(bf16[384,640]{1,0:T(8,128)(2,1)} %get-tuple-element.85), channel_id=1, source_target_pairs={{0,2},{2,0},{4,7},{6,5},{8,8},{10,10},{12,13},{14,15},{17,18},{19,... | collective-permute-start | bytes 1474568 | tf_op jit(solution)/shard_map/sums_20/ppermute | solution.py:162
  86.5 12.0 %collective-permute-start.18 = (bf16[384,640]{1,0:T(8,128)(2,1)}, bf16[384,640]{1,0:T(8,128)(2,1)}, u32[]{:S(2)}, u32[]{:S(2)}) collective-permute-start(bf16[384,640]{1,0:T(8,128)(2,1)} %get-tuple-element.85), channel_id=1, source_target_pairs={{1,18},{3,16},{5,23},{7,21},{9,24},{11,26},{13,29},{15,31},{16,2},... | collective-permute-start | bytes 1474568 | tf_op jit(solution)/shard_map/sums_cross_20/ppermute | solution.py:162
  87.9 10.5 %copy-start.7 = (f32[1280]{0:T(1024)S(1)}, f32[1280]{0:T(1024)}, u32[]{:S(2)}) copy-start(f32[1280]{0:T(1024)} %param.16) | copy-start | bytes 15364
  87.9 4.4 %collective-permute-start.2 = (bf16[640,640]{1,0:T(8,128)(2,1)}, bf16[640,640]{1,0:T(8,128)(2,1)S(1)}, u32[]{:S(2)}, u32[]{:S(2)}) collective-permute-start(bf16[640,640]{1,0:T(8,128)(2,1)} %get-tuple-element.47), channel_id=1, source_target_pairs={{0,1},{1,0},{2,3},{3,2},{4,5},{5,4},{6,7},{7,6},{8,9},{9,8},{10,11... | collective-permute-start | bytes 2457608 | tf_op jit(solution)/shard_map/cond/branch_1_fun/core_swap/ppermute | solution.py:162
  94.8 13.2 %collective-permute-start.13 = (bf16[384,640]{1,0:T(8,128)(2,1)}, bf16[384,640]{1,0:T(8,128)(2,1)S(1)}, u32[]{:S(2)}, u32[]{:S(2)}) collective-permute-start(bf16[384,640]{1,0:T(8,128)(2,1)} %get-tuple-element.101), channel_id=1, source_target_pairs={{0,1},{2,3},{4,6},{6,4},{8,11},{10,9},{12,12},{14,14},{17,17},{19,... | collective-permute-start | bytes 1474568 | tf_op jit(solution)/shard_map/sums_3/ppermute | solution.py:162
  97.1 15.4 %collective-permute-start.14 = (bf16[384,640]{1,0:T(8,128)(2,1)}, bf16[384,640]{1,0:T(8,128)(2,1)S(1)}, u32[]{:S(2)}, u32[]{:S(2)}) collective-permute-start(bf16[384,640]{1,0:T(8,128)(2,1)} %get-tuple-element.101), channel_id=1, source_target_pairs={{1,17},{3,19},{5,22},{7,20},{9,27},{11,25},{13,28},{15,30},{16,1},... | collective-permute-start | bytes 1474568 | tf_op jit(solution)/shard_map/sums_cross_3/ppermute | solution.py:162
  98.5 1.5 %copy-start.1 = (f32[384,1280]{1,0:T(8,128)S(1)}, f32[384,1280]{1,0:T(8,128)}, u32[]{:S(2)}) copy-start(f32[384,1280]{1,0:T(8,128)} %refs_6_.1) | copy-start | bytes 5898244

commit v5 on v4

--- a/solution.py
+++ b/solution.py
@@ -32,6 +32,7 @@
         out_shape=jax.ShapeDtypeStruct((1,), jnp.int32),
         in_specs=[scalar],
         out_specs=scalar,
+        compiler_params=pltpu.CompilerParams(vmem_limit_bytes=MIB),
         cost_estimate=weight(50),
         name="fence",
     )(token)
@@ -191,7 +192,7 @@
         + parts
         + [wide, pl.BlockSpec((1, width), lambda i: (0, 0))],
         out_specs=wide,
-        compiler_params=pltpu.CompilerParams(vmem_limit_bytes=32 * MIB),
+        compiler_params=pltpu.CompilerParams(vmem_limit_bytes=12 * MIB),
         name="finish",
     )(spot, *direct, *crossed, residual_in, gate[None, :])
 

time: 116 us -> 113 us (0.974)
  waiting for transfers between devices: 40 us -> 43.9 us
  starting transfers between devices: 35 us -> 32.4 us
  matrix products: 17 us -> 14.7 us
  other arithmetic: 2.78 us -> 1.56 us
    ppermute x17, waiting for transfers between devices: 20.6 us -> 23.6 us  [send(): return lax.ppermute(array, AXES, route)]
    ppermute x17, starting transfers between devices: 29 us -> 26.4 us  [send(): return lax.ppermute(array, AXES, route)]
    dot_general x4, matrix products: 9.39 us -> 7.32 us  [sums(): total = total + jnp.dot(rows_sib, sib, preferred_element_type=jnp.float32)]
    select_n x1, other arithmetic: 2.09 us -> 0.87 us  [ringed(): rows_sib = jnp.where(here, first, second)]
    unnamed x16 -> x20, local copies, waits for them, and re-layouts: 4.44 us -> 5.22 us
  transfers between devices with their start and end apart: 19 -> 19, of which waited for: 10 -> 11; matrix products, arithmetic and copies ran while one was open for 18% -> 15% of each run, Pallas kernels for 10% -> 10%
where the time goes in v5:
time: 113 us; the launch traced here: 111 us
  waiting for transfers between devices  43.9 us (39%)
  starting transfers between devices  32.4 us (29%)
  matrix products  14.7 us (13%)
  Pallas kernels  12.7 us (11%)
  local copies, waits for them, and re-layouts  5.31 us (5%)
  other arithmetic  1.56 us (1%)
    ppermute x17, starting transfers between devices, send(): return lax.ppermute(array, AXES, route)  26.4 us
    ppermute x17, waiting for transfers between devices, send(): return lax.ppermute(array, AXES, route)  23.6 us
    ppermute x1, waiting for transfers between devices, halos(): lax.ppermute(keyvals, 'frame', forward)  17 us
    pallas_call x1, Pallas kernels, attend(): pl.pallas_call(attend_kernel, out_shape=jax.ShapeDtypeStruct((rows, width...  7.67 us
    dot_general x4, matrix products, sums(): total = jnp.dot(rows_own, own, preferred_element_type=jnp.float32)  7.37 us
    dot_general x4, matrix products, sums(): total = total + jnp.dot(rows_sib, sib, preferred_element_type=jnp.float32)  7.32 us
    unnamed x20, local copies, waits for them, and re-layouts  5.22 us
    pallas_call x2, Pallas kernels, finish(): pl.pallas_call(finish_kernel, grid=(rows // step,), out_shape=jax.ShapeDt...  4.45 us
  transfers between devices with their start and end apart: 19, of which 11 were waited for; matrix products, arithmetic and copies ran while one was open for 15% of the time, Pallas kernels for 10%

profile of v5, /device:TPU:8, one launch (start us, length us, event | category | flops | bytes accessed | tf_op | source)
XLA Modules:
  0.0 111.5 jit_solution(3576821572589304683)
XLA Ops:
  0.0 3.6 %collective-permute-start.4 = (bf16[2,384,640]{2,1,0:T(8,128)(2,1)}, bf16[2,384,640]{2,1,0:T(8,128)(2,1)S(1)}, u32[]{:S(2)}, u32[]{:S(2)}) collective-permute-start(bf16[2,384,640]{2,1,0:T(8,128)(2,1)} %own_ref.1), channel_id=1, source_target_pairs={{0,4},{4,8},{8,12},{1,5},{5,9},{9,13},{2,6},{6,10},{10,14},{3,7},{... | collective-permute-start | bytes 2949128 | tf_op jit(solution)/shard_map/ppermute | solution.py:120
  3.6 2.4 %collective-permute-start.5 = (bf16[2,384,640]{2,1,0:T(8,128)(2,1)}, bf16[2,384,640]{2,1,0:T(8,128)(2,1)}, u32[]{:S(2)}, u32[]{:S(2)}) collective-permute-start(bf16[2,384,640]{2,1,0:T(8,128)(2,1)} %own_ref.1), channel_id=1, source_target_pairs={{4,0},{8,4},{12,8},{5,1},{9,5},{13,9},{6,2},{10,6},{14,10},{7,3},{... | collective-permute-start | bytes 2949128 | tf_op jit(solution)/shard_map/ppermute | solution.py:120
  6.2 2.4 %collective-permute-done.3 = bf16[640,640]{1,0:T(8,128)(2,1)} collective-permute-done((bf16[640,640]{1,0:T(8,128)(2,1)S(1)}, bf16[640,640]{1,0:T(8,128)(2,1)}, u32[]{:S(2)}, u32[]{:S(2)}) %collective-permute-start.3) | collective-permute-done | bytes 819232 | tf_op jit(solution)/shard_map/core_swap_0/ppermute | solution.py:163
  8.7 17.0 %collective-permute-done.4.low_ref = bf16[2,384,640]{2,1,0:T(8,128)(2,1)S(1)} collective-permute-done((bf16[2,384,640]{2,1,0:T(8,128)(2,1)}, bf16[2,384,640]{2,1,0:T(8,128)(2,1)S(1)}, u32[]{:S(2)}, u32[]{:S(2)}) %collective-permute-start.4) | collective-permute-done | bytes 983072 | tf_op jit(solution)/shard_map/ppermute | solution.py:120
  25.7 3.3 %collective-permute-done.5.high_ref = bf16[2,384,640]{2,1,0:T(8,128)(2,1)} collective-permute-done((bf16[2,384,640]{2,1,0:T(8,128)(2,1)}, bf16[2,384,640]{2,1,0:T(8,128)(2,1)}, u32[]{:S(2)}, u32[]{:S(2)}) %collective-permute-start.5) | collective-permute-done | bytes 983072 | tf_op jit(solution)/shard_map/ppermute | solution.py:120
  29.0 1.6 %collective-permute-start.8 = (bf16[640,640]{1,0:T(8,128)(2,1)S(1)}, bf16[640,640]{1,0:T(8,128)(2,1)}, u32[]{:S(2)}, u32[]{:S(2)}) collective-permute-start(bf16[640,640]{1,0:T(8,128)(2,1)S(1)} %constant_dynamic-slice_fusion), channel_id=1, source_target_pairs={{0,4},{1,5},{2,14},{3,15},{4,8},{5,9},{6,2},{7,3},{8,12},{9,13},{1... | collective-permute-start | bytes 2457608 | tf_op jit(solution)/shard_map/ring_1/ppermute | solution.py:163
  30.6 0.7 subtract_clamp_fusion.ids
  31.3 1.2 %copy-done.2 = bf16[2,384,640]{2,1,0:T(8,128)(2,1)S(1)} copy-done((bf16[2,384,640]{2,1,0:T(8,128)(2,1)S(1)}, bf16[2,384,640]{2,1,0:T(8,128)(2,1)}, u32[]{:S(2)}) %copy-start.2) | copy-done | bytes 983064
  32.5 1.0 copy-done.3
  33.5 0.7 copy-done.4
  34.2 7.7 %attend.1 = bf16[384,640]{1,0:T(8,128)(2,1)S(1)} custom-call(s32[6,8]{1,0:T(8,128)S(1)} %subtract_clamp_fusion.ids, s32[6]{0:T(128)S(1)} %copy-done.4, bf16[384,640]{1,0:T(8,128)(2,1)S(1)} %copy-done.3, bf16[2,384,640]{2,1,0:T(8,128)(2,1)S(1)} %copy-done.2, bf16[2,384,640]{2,1,0:T(8,128)(2,1)S(1)} %collective-permute-done.4.low_ref, ...), custom_call_target="tpu_custom_call" | custom-call | flops 8000000000 | bytes 24000000 | tf_op jit(solution)/shard_map/attend/pallas_call | solution.py:101
  41.9 1.5 %collective-permute-start.6 = (bf16[384,640]{1,0:T(8,128)(2,1)S(1)}, bf16[384,640]{1,0:T(8,128)(2,1)S(1)}, u32[]{:S(2)}, u32[]{:S(2)}) collective-permute-start(bf16[384,640]{1,0:T(8,128)(2,1)S(1)} %attend.1), channel_id=1, source_target_pairs={{0,16},{1,0},{2,18},{3,2},{4,20},{5,4},{6,22},{7,6},{8,24},{9,8},{... | collective-permute-start | bytes 1474568 | tf_op jit(solution)/shard_map/rows_1/ppermute | solution.py:163
  43.4 0.7 collective-permute-start.7
  44.1 3.8 %collective-permute-done.8 = bf16[640,640]{1,0:T(8,128)(2,1)} collective-permute-done((bf16[640,640]{1,0:T(8,128)(2,1)S(1)}, bf16[640,640]{1,0:T(8,128)(2,1)}, u32[]{:S(2)}, u32[]{:S(2)}) %collective-permute-start.8) | collective-permute-done | bytes 819232 | tf_op jit(solution)/shard_map/ring_1/ppermute | solution.py:163
  47.9 1.6 %collective-permute-start.9 = (bf16[640,640]{1,0:T(8,128)(2,1)}, bf16[640,640]{1,0:T(8,128)(2,1)}, u32[]{:S(2)}, u32[]{:S(2)}) collective-permute-start(bf16[640,640]{1,0:T(8,128)(2,1)} %collective-permute-done.8), channel_id=1, source_target_pairs={{0,4},{1,5},{2,14},{3,15},{4,8},{5,9},{6,2},{7,3},{8,12},{9,13},{1... | collective-permute-start | bytes 2457608 | tf_op jit(solution)/shard_map/ring_2/ppermute | solution.py:163
  50.1 3.6 %collective-permute-done.6 = bf16[384,640]{1,0:T(8,128)(2,1)S(1)} collective-permute-done((bf16[384,640]{1,0:T(8,128)(2,1)S(1)}, bf16[384,640]{1,0:T(8,128)(2,1)S(1)}, u32[]{:S(2)}, u32[]{:S(2)}) %collective-permute-start.6) | collective-permute-done | bytes 491552 | tf_op jit(solution)/shard_map/rows_1/ppermute | solution.py:163
  54.3 0.9 broadcast_select_fusion.2
  55.2 8.2 %conditional.3 = (bf16[384,640]{1,0:T(8,128)(2,1)S(1)}, bf16[384,640]{1,0:T(8,128)(2,1)}) conditional(s32[]{:T(128)} %bitcast.1, () %tuple.37, (bf16[384,640]{1,0:T(8,128)(2,1)}, bf16[640,640]{1,0:T(8,128)(2,1)S(1)}, bf16[384,640]{1,0:T(8,128)(2,1)S(1)}, bf16[640,640]{1,0:T(8,128)(2,1)}, bf16[640,640]{1,0:T(8,128)(2,1)}) %tuple.54), branch_computations={%region_0.1_spmd, %region_1.2_spmd} | conditional | flops 1259274240 | bytes 13434936 | solution.py:237
  55.2 1.5 %collective-permute-start = (bf16[640,640]{1,0:T(8,128)(2,1)}, bf16[640,640]{1,0:T(8,128)(2,1)S(1)}, u32[]{:S(2)}, u32[]{:S(2)}) collective-permute-start(bf16[640,640]{1,0:T(8,128)(2,1)} %get-tuple-element.40), channel_id=1, source_target_pairs={{0,1},{1,0},{2,3},{3,2},{4,5},{5,4},{6,7},{7,6},{8,9},{9,8},{10,11... | collective-permute-start | bytes 2457608 | tf_op jit(solution)/shard_map/cond/branch_1_fun/core_swap/ppermute | solution.py:163
  56.7 1.9 %fusion.5 = f32[384,640]{1,0:T(8,128)S(1)} fusion(bf16[384,640]{1,0:T(8,128)(2,1)} %get-tuple-element.36, bf16[640,640]{1,0:T(8,128)(2,1)} %get-tuple-element.40), kind=kOutput, calls=%fused_computation.15 | convolution fusion | flops 314572800 | bytes 2293760 | tf_op jit(solution)/shard_map/cond/branch_1_fun/dot_general | solution.py:245
  58.6 1.6 %fusion.4 = f32[384,640]{1,0:T(8,128)S(1)} fusion(bf16[384,640]{1,0:T(8,128)(2,1)} %get-tuple-element.36, bf16[640,640]{1,0:T(8,128)(2,1)S(1)} %get-tuple-element.37), kind=kOutput, calls=%fused_computation.14 | convolution fusion | flops 314572800 | bytes 2293760 | tf_op jit(solution)/shard_map/cond/branch_1_fun/dot_general | solution.py:245
  60.2 1.7 %fusion = bf16[384,640]{1,0:T(8,128)(2,1)S(1)} fusion(f32[384,640]{1,0:T(8,128)S(1)} %fusion.4, bf16[384,640]{1,0:T(8,128)(2,1)S(1)} %get-tuple-element.38, bf16[640,640]{1,0:T(8,128)(2,1)} %get-tuple-element.39), kind=kOutput, calls=%fused_computation.2 | convolution fusion | flops 315064320 | bytes 2785280 | tf_op jit(solution)/shard_map/cond/branch_1_fun/dot_general | solution.py:246
  62.0 1.4 %fusion.1 = bf16[384,640]{1,0:T(8,128)(2,1)} fusion(f32[384,640]{1,0:T(8,128)S(1)} %fusion.5, bf16[384,640]{1,0:T(8,128)(2,1)S(1)} %get-tuple-element.38, bf16[640,640]{1,0:T(8,128)(2,1)S(1)} %collective-permute-done), kind=kOutput, calls=%fused_computation.3 | convolution fusion | flops 315064320 | bytes 2785280 | tf_op jit(solution)/shard_map/cond/branch_1_fun/dot_general | solution.py:246
  63.4 0.8 copy-done.9
  64.1 1.7 %collective-permute-start.11 = (bf16[384,640]{1,0:T(8,128)(2,1)}, bf16[384,640]{1,0:T(8,128)(2,1)S(1)}, u32[]{:S(2)}, u32[]{:S(2)}) collective-permute-start(bf16[384,640]{1,0:T(8,128)(2,1)} %get-tuple-element.83), channel_id=1, source_target_pairs={{0,3},{2,1},{4,4},{6,6},{8,9},{10,11},{12,14},{14,12},{17,19},{19,... | collective-permute-start | bytes 1474568 | tf_op jit(solution)/shard_map/sums_1/ppermute | solution.py:163
  65.8 1.3 %collective-permute-start.12 = (bf16[384,640]{1,0:T(8,128)(2,1)}, bf16[384,640]{1,0:T(8,128)(2,1)S(1)}, u32[]{:S(2)}, u32[]{:S(2)}) collective-permute-start(bf16[384,640]{1,0:T(8,128)(2,1)} %get-tuple-element.83), channel_id=1, source_target_pairs={{1,19},{3,17},{5,20},{7,22},{9,25},{11,27},{13,30},{15,28},{16,3},... | collective-permute-start | bytes 1474568 | tf_op jit(solution)/shard_map/sums_cross_1/ppermute | solution.py:163
  67.1 0.6 collective-permute-start.10
  67.7 7.6 %conditional.4 = (bf16[384,640]{1,0:T(8,128)(2,1)}, bf16[384,640]{1,0:T(8,128)(2,1)}) conditional(s32[]{:T(128)} %bitcast.1, () %tuple.40, (s32[]{:T(128)}, bf16[384,640]{1,0:T(8,128)(2,1)}, bf16[640,640]{1,0:T(8,128)(2,1)}, bf16[384,640]{1,0:T(8,128)(2,1)S(1)}, bf16[384,640]{1,0:T(8,128)(2,1)}) %tuple.55), branch_computations={%region_2.3_spmd, %region_3.4_spmd} | conditional | flops 630128640 | bytes 11305054 | solution.py:237
  67.7 2.5 %collective-permute-start.1 = (bf16[640,640]{1,0:T(8,128)(2,1)}, bf16[640,640]{1,0:T(8,128)(2,1)}, u32[]{:S(2)}, u32[]{:S(2)}) collective-permute-start(bf16[640,640]{1,0:T(8,128)(2,1)} %get-tuple-element.44), channel_id=1, source_target_pairs={{0,1},{1,0},{2,3},{3,2},{4,5},{5,4},{6,7},{7,6},{8,9},{9,8},{10,11... | collective-permute-start | bytes 2457608 | tf_op jit(solution)/shard_map/cond/branch_1_fun/core_swap/ppermute | solution.py:163
  70.2 1.9 %fusion.6 = f32[384,640]{1,0:T(8,128)S(1)} fusion(bf16[384,640]{1,0:T(8,128)(2,1)} %get-tuple-element.43, bf16[640,640]{1,0:T(8,128)(2,1)} %get-tuple-element.44), kind=kOutput, calls=%fused_computation.16 | convolution fusion | flops 314572800 | bytes 2293760 | tf_op jit(solution)/shard_map/cond/branch_1_fun/dot_general | solution.py:245
  72.5 2.8 %broadcast_select_fusion = (bf16[384,640]{1,0:T(8,128)(2,1)}, bf16[384,640]{1,0:T(8,128)(2,1)}) fusion(bf16[384,640]{1,0:T(8,128)(2,1)S(1)} %copy-done.10, pred[]{:T(512)S(6)} %eq.5, f32[384,640]{1,0:T(8,128)S(1)} %fusion.6, bf16[384,640]{1,0:T(8,128)(2,1)S(1)} %get-tuple-element.45, bf16[640,640]{1,0:T(8,128)(2,1)} %collective-permute-done.1), kind=kOutput, calls=%fused_computation.6 | convolution fusion | flops 315555840 | bytes 3768321 | tf_op jit(solution)/shard_map/cond/branch_1_fun/dot_general | solution.py:246
  75.3 1.6 %collective-permute-done.12.refs_3_ = bf16[384,640]{1,0:T(8,128)(2,1)S(1)} collective-permute-done((bf16[384,640]{1,0:T(8,128)(2,1)}, bf16[384,640]{1,0:T(8,128)(2,1)S(1)}, u32[]{:S(2)}, u32[]{:S(2)}) %collective-permute-start.12) | collective-permute-done | bytes 491552 | tf_op jit(solution)/shard_map/sums_cross_1/ppermute | solution.py:163
  76.9 1.3 %collective-permute-start.15 = (bf16[384,640]{1,0:T(8,128)(2,1)}, bf16[384,640]{1,0:T(8,128)(2,1)S(1)}, u32[]{:S(2)}, u32[]{:S(2)}) collective-permute-start(bf16[384,640]{1,0:T(8,128)(2,1)} %get-tuple-element.84), channel_id=1, source_target_pairs={{0,0},{2,2},{4,5},{6,7},{8,10},{10,8},{12,15},{14,13},{17,16},{19,... | collective-permute-start | bytes 1474568 | tf_op jit(solution)/shard_map/sums_02/ppermute | solution.py:163
  78.2 1.5 %collective-permute-start.17 = (bf16[384,640]{1,0:T(8,128)(2,1)}, bf16[384,640]{1,0:T(8,128)(2,1)}, u32[]{:S(2)}, u32[]{:S(2)}) collective-permute-start(bf16[384,640]{1,0:T(8,128)(2,1)} %get-tuple-element.84), channel_id=1, source_target_pairs={{1,16},{3,18},{5,21},{7,23},{9,26},{11,24},{13,31},{15,29},{16,0},... | collective-permute-start | bytes 1474568 | tf_op jit(solution)/shard_map/sums_cross_02/ppermute | solution.py:163
  79.7 4.8 %collective-permute-start.16 = (bf16[384,640]{1,0:T(8,128)(2,1)}, bf16[384,640]{1,0:T(8,128)(2,1)}, u32[]{:S(2)}, u32[]{:S(2)}) collective-permute-start(bf16[384,640]{1,0:T(8,128)(2,1)} %get-tuple-element.85), channel_id=1, source_target_pairs={{0,2},{2,0},{4,7},{6,5},{8,8},{10,10},{12,13},{14,15},{17,18},{19,... | collective-permute-start | bytes 1474568 | tf_op jit(solution)/shard_map/sums_20/ppermute | solution.py:163
  84.5 1.4 %collective-permute-start.18 = (bf16[384,640]{1,0:T(8,128)(2,1)}, bf16[384,640]{1,0:T(8,128)(2,1)}, u32[]{:S(2)}, u32[]{:S(2)}) collective-permute-start(bf16[384,640]{1,0:T(8,128)(2,1)} %get-tuple-element.85), channel_id=1, source_target_pairs={{1,18},{3,16},{5,23},{7,21},{9,24},{11,26},{13,29},{15,31},{16,2},... | collective-permute-start | bytes 1474568 | tf_op jit(solution)/shard_map/sums_cross_20/ppermute | solution.py:163
  85.9 2.4 %collective-permute-done.10 = bf16[640,640]{1,0:T(8,128)(2,1)} collective-permute-done((bf16[640,640]{1,0:T(8,128)(2,1)}, bf16[640,640]{1,0:T(8,128)(2,1)}, u32[]{:S(2)}, u32[]{:S(2)}) %collective-permute-start.10) | collective-permute-done | bytes 819232 | tf_op jit(solution)/shard_map/ring_3/ppermute | solution.py:163
  88.3 4.7 %conditional.5 = (bf16[384,640]{1,0:T(8,128)(2,1)}) conditional(s32[]{:T(128)} %bitcast.1, () %tuple.36, (bf16[384,640]{1,0:T(8,128)(2,1)}, bf16[640,640]{1,0:T(8,128)(2,1)}, bf16[384,640]{1,0:T(8,128)(2,1)}) %tuple.53), branch_computations={%region_4.5_spmd, %region_5.6_spmd} | conditional | flops 629637120 | bytes 10321996 | solution.py:237
  88.3 1.2 %collective-permute-start.2 = (bf16[640,640]{1,0:T(8,128)(2,1)}, bf16[640,640]{1,0:T(8,128)(2,1)S(1)}, u32[]{:S(2)}, u32[]{:S(2)}) collective-permute-start(bf16[640,640]{1,0:T(8,128)(2,1)} %get-tuple-element.47), channel_id=1, source_target_pairs={{0,1},{1,0},{2,3},{3,2},{4,5},{5,4},{6,7},{7,6},{8,9},{9,8},{10,11... | collective-permute-start | bytes 2457608 | tf_op jit(solution)/shard_map/cond/branch_1_fun/core_swap/ppermute | solution.py:163
  89.5 1.9 %fusion.7 = f32[384,640]{1,0:T(8,128)S(1)} fusion(bf16[384,640]{1,0:T(8,128)(2,1)} %get-tuple-element.46, bf16[640,640]{1,0:T(8,128)(2,1)} %get-tuple-element.47), kind=kOutput, calls=%fused_computation.17 | convolution fusion | flops 314572800 | bytes 2293760 | tf_op jit(solution)/shard_map/cond/branch_1_fun/dot_general | solution.py:245
  91.6 1.4 %fusion.3 = bf16[384,640]{1,0:T(8,128)(2,1)} fusion(f32[384,640]{1,0:T(8,128)S(1)} %fusion.7, bf16[384,640]{1,0:T(8,128)(2,1)S(1)} %copy-done.6, bf16[640,640]{1,0:T(8,128)(2,1)S(1)} %collective-permute-done.2), kind=kOutput, calls=%fused_computation.9 | convolution fusion | flops 315064320 | bytes 2785280 | tf_op jit(solution)/shard_map/cond/branch_1_fun/dot_general | solution.py:246
  93.0 1.9 %collective-permute-start.13 = (bf16[384,640]{1,0:T(8,128)(2,1)}, bf16[384,640]{1,0:T(8,128)(2,1)S(1)}, u32[]{:S(2)}, u32[]{:S(2)}) collective-permute-start(bf16[384,640]{1,0:T(8,128)(2,1)} %get-tuple-element.101), channel_id=1, source_target_pairs={{0,1},{2,3},{4,6},{6,4},{8,11},{10,9},{12,12},{14,14},{17,17},{19,... | collective-permute-start | bytes 1474568 | tf_op jit(solution)/shard_map/sums_3/ppermute | solution.py:163
  95.0 1.3 %collective-permute-start.14 = (bf16[384,640]{1,0:T(8,128)(2,1)}, bf16[384,640]{1,0:T(8,128)(2,1)S(1)}, u32[]{:S(2)}, u32[]{:S(2)}) collective-permute-start(bf16[384,640]{1,0:T(8,128)(2,1)} %get-tuple-element.101), channel_id=1, source_target_pairs={{1,17},{3,19},{5,22},{7,20},{9,27},{11,25},{13,28},{15,30},{16,1},... | collective-permute-start | bytes 1474568 | tf_op jit(solution)/shard_map/sums_cross_3/ppermute | solution.py:163
  96.3 1.5 %copy-done.1 = f32[384,1280]{1,0:T(8,128)S(1)} copy-done((f32[384,1280]{1,0:T(8,128)S(1)}, f32[384,1280]{1,0:T(8,128)}, u32[]{:S(2)}) %copy-start.1) | copy-done | bytes 1966104
  97.9 2.6 %finish.2.refs_2_ = f32[384,1280]{1,0:T(8,128)S(1)} custom-call(s32[1]{0:T(128)} %bitcast.spot, bf16[384,640]{1,0:T(8,128)(2,1)S(1)} %collective-permute-done.11.refs_0_, bf16[384,640]{1,0:T(8,128)(2,1)S(1)} %collective-permute-done.15.refs_1_, bf16[384,640]{1,0:T(8,128)(2,1)} %collective-permute-done.16.refs_2_, ...), custom_call_target="tpu_custom_call" | custom-call | tf_op jit(solution)/shard_map/finish/pallas_call | solution.py:187
  100.5 7.0 %collective-permute-done.13.refs_0_ = bf16[384,640]{1,0:T(8,128)(2,1)S(1)} collective-permute-done((bf16[384,640]{1,0:T(8,128)(2,1)}, bf16[384,640]{1,0:T(8,128)(2,1)S(1)}, u32[]{:S(2)}, u32[]{:S(2)}) %collective-permute-start.13) | collective-permute-done | bytes 491552 | tf_op jit(solution)/shard_map/sums_3/ppermute | solution.py:163
  107.4 2.2 %collective-permute-done.14.refs_1_ = bf16[384,640]{1,0:T(8,128)(2,1)S(1)} collective-permute-done((bf16[384,640]{1,0:T(8,128)(2,1)}, bf16[384,640]{1,0:T(8,128)(2,1)S(1)}, u32[]{:S(2)}, u32[]{:S(2)}) %collective-permute-start.14) | collective-permute-done | bytes 491552 | tf_op jit(solution)/shard_map/sums_cross_3/ppermute | solution.py:163
  109.6 1.9 %finish.3 = f32[384,1280]{1,0:T(8,128)} custom-call(s32[1]{0:T(128)} %bitcast.spot, bf16[384,640]{1,0:T(8,128)(2,1)S(1)} %collective-permute-done.13.refs_0_, bf16[384,640]{1,0:T(8,128)(2,1)S(1)} %collective-permute-done.14.refs_1_, f32[384,1280]{1,0:T(8,128)S(1)} %finish.2.refs_2_, f32[1,1280]{1,0:T(1,128)S(1)} %broadcast_in_dim.4.refs_7_.refs_3_), custom_call_target="tpu_custom_call" | custom-call | tf_op jit(solution)/shard_map/finish/pallas_call | solution.py:187
  (33 shorter events, 1.4 us)
Async XLA Ops:
  0.0 6.1 %copy-start = (bf16[640,1280]{1,0:T(8,128)(2,1)S(1)}, bf16[640,1280]{1,0:T(8,128)(2,1)}, u32[]{:S(2)}) copy-start(bf16[640,1280]{1,0:T(8,128)(2,1)} %param.17) | copy-start | bytes 4915204
  0.0 25.7 %collective-permute-start.4 = (bf16[2,384,640]{2,1,0:T(8,128)(2,1)}, bf16[2,384,640]{2,1,0:T(8,128)(2,1)S(1)}, u32[]{:S(2)}, u32[]{:S(2)}) collective-permute-start(bf16[2,384,640]{2,1,0:T(8,128)(2,1)} %own_ref.1), channel_id=1, source_target_pairs={{0,4},{4,8},{8,12},{1,5},{5,9},{9,13},{2,6},{6,10},{10,14},{3,7},{... | collective-permute-start | bytes 2949128 | tf_op jit(solution)/shard_map/ppermute | solution.py:120
  3.6 25.4 %collective-permute-start.5 = (bf16[2,384,640]{2,1,0:T(8,128)(2,1)}, bf16[2,384,640]{2,1,0:T(8,128)(2,1)}, u32[]{:S(2)}, u32[]{:S(2)}) collective-permute-start(bf16[2,384,640]{2,1,0:T(8,128)(2,1)} %own_ref.1), channel_id=1, source_target_pairs={{4,0},{8,4},{12,8},{5,1},{9,5},{13,9},{6,2},{10,6},{14,10},{7,3},{... | collective-permute-start | bytes 2949128 | tf_op jit(solution)/shard_map/ppermute | solution.py:120
  6.1 35.7 %copy-start.7 = (bf16[640,640]{1,0:T(8,128)(2,1)}, bf16[640,640]{1,0:T(8,128)(2,1)S(1)}, u32[]{:S(2)}) copy-start(bf16[640,640]{1,0:T(8,128)(2,1)S(1)} %constant_dynamic-slice_fusion) | copy-start | bytes 2457604
  6.2 2.5 %collective-permute-start.3 = (bf16[640,640]{1,0:T(8,128)(2,1)S(1)}, bf16[640,640]{1,0:T(8,128)(2,1)}, u32[]{:S(2)}, u32[]{:S(2)}) collective-permute-start(bf16[640,640]{1,0:T(8,128)(2,1)S(1)} %constant_dynamic-slice_fusion), channel_id=1, source_target_pairs={{0,1},{1,0},{2,3},{3,2},{4,5},{5,4},{6,7},{7,6},{8,9},{9,8},{10,11... | collective-permute-start | bytes 2457608 | tf_op jit(solution)/shard_map/core_swap_0/ppermute | solution.py:163
  29.0 18.9 %collective-permute-start.8 = (bf16[640,640]{1,0:T(8,128)(2,1)S(1)}, bf16[640,640]{1,0:T(8,128)(2,1)}, u32[]{:S(2)}, u32[]{:S(2)}) collective-permute-start(bf16[640,640]{1,0:T(8,128)(2,1)S(1)} %constant_dynamic-slice_fusion), channel_id=1, source_target_pairs={{0,4},{1,5},{2,14},{3,15},{4,8},{5,9},{6,2},{7,3},{8,12},{9,13},{1... | collective-permute-start | bytes 2457608 | tf_op jit(solution)/shard_map/ring_1/ppermute | solution.py:163
  31.3 1.2 %copy-start.2 = (bf16[2,384,640]{2,1,0:T(8,128)(2,1)S(1)}, bf16[2,384,640]{2,1,0:T(8,128)(2,1)}, u32[]{:S(2)}) copy-start(bf16[2,384,640]{2,1,0:T(8,128)(2,1)} %own_ref.1) | copy-start | bytes 2949124
  32.5 1.0 copy-start.3
  33.5 0.7 copy-start.4
  41.9 11.8 %collective-permute-start.6 = (bf16[384,640]{1,0:T(8,128)(2,1)S(1)}, bf16[384,640]{1,0:T(8,128)(2,1)S(1)}, u32[]{:S(2)}, u32[]{:S(2)}) collective-permute-start(bf16[384,640]{1,0:T(8,128)(2,1)S(1)} %attend.1), channel_id=1, source_target_pairs={{0,16},{1,0},{2,18},{3,2},{4,20},{5,4},{6,22},{7,6},{8,24},{9,8},{... | collective-permute-start | bytes 1474568 | tf_op jit(solution)/shard_map/rows_1/ppermute | solution.py:163
  43.4 10.2 %collective-permute-start.7 = (bf16[384,640]{1,0:T(8,128)(2,1)S(1)}, bf16[384,640]{1,0:T(8,128)(2,1)S(1)}, u32[]{:S(2)}, u32[]{:S(2)}) collective-permute-start(bf16[384,640]{1,0:T(8,128)(2,1)S(1)} %attend.1), channel_id=1, source_target_pairs={{1,16},{3,18},{5,20},{7,22},{9,24},{11,26},{13,28},{15,30},{16,1},... | collective-permute-start | bytes 1474568 | tf_op jit(solution)/shard_map/rows_2/ppermute | solution.py:163
  47.9 19.2 %collective-permute-start.9 = (bf16[640,640]{1,0:T(8,128)(2,1)}, bf16[640,640]{1,0:T(8,128)(2,1)}, u32[]{:S(2)}, u32[]{:S(2)}) collective-permute-start(bf16[640,640]{1,0:T(8,128)(2,1)} %collective-permute-done.8), channel_id=1, source_target_pairs={{0,4},{1,5},{2,14},{3,15},{4,8},{5,9},{6,2},{7,3},{8,12},{9,13},{1... | collective-permute-start | bytes 2457608 | tf_op jit(solution)/shard_map/ring_2/ppermute | solution.py:163
  50.1 5.1 %copy-start.8 = (bf16[640,640]{1,0:T(8,128)(2,1)S(1)}, bf16[640,640]{1,0:T(8,128)(2,1)}, u32[]{:S(2)}) copy-start(bf16[640,640]{1,0:T(8,128)(2,1)} %copy-done.7) | copy-start | bytes 2457604
  55.2 12.5 %copy-start.5 = (bf16[384,640]{1,0:T(8,128)(2,1)}, bf16[384,640]{1,0:T(8,128)(2,1)S(1)}, u32[]{:S(2)}) copy-start(bf16[384,640]{1,0:T(8,128)(2,1)S(1)} %get-tuple-element.91) | copy-start | bytes 1474564
  55.2 6.8 %collective-permute-start = (bf16[640,640]{1,0:T(8,128)(2,1)}, bf16[640,640]{1,0:T(8,128)(2,1)S(1)}, u32[]{:S(2)}, u32[]{:S(2)}) collective-permute-start(bf16[640,640]{1,0:T(8,128)(2,1)} %get-tuple-element.40), channel_id=1, source_target_pairs={{0,1},{1,0},{2,3},{3,2},{4,5},{5,4},{6,7},{7,6},{8,9},{9,8},{10,11... | collective-permute-start | bytes 2457608 | tf_op jit(solution)/shard_map/cond/branch_1_fun/core_swap/ppermute | solution.py:163
  63.4 0.8 copy-start.9
  64.1 11.2 %collective-permute-start.11 = (bf16[384,640]{1,0:T(8,128)(2,1)}, bf16[384,640]{1,0:T(8,128)(2,1)S(1)}, u32[]{:S(2)}, u32[]{:S(2)}) collective-permute-start(bf16[384,640]{1,0:T(8,128)(2,1)} %get-tuple-element.83), channel_id=1, source_target_pairs={{0,3},{2,1},{4,4},{6,6},{8,9},{10,11},{12,14},{14,12},{17,19},{19,... | collective-permute-start | bytes 1474568 | tf_op jit(solution)/shard_map/sums_1/ppermute | solution.py:163
  65.8 11.1 %collective-permute-start.12 = (bf16[384,640]{1,0:T(8,128)(2,1)}, bf16[384,640]{1,0:T(8,128)(2,1)S(1)}, u32[]{:S(2)}, u32[]{:S(2)}) collective-permute-start(bf16[384,640]{1,0:T(8,128)(2,1)} %get-tuple-element.83), channel_id=1, source_target_pairs={{1,19},{3,17},{5,20},{7,22},{9,25},{11,27},{13,30},{15,28},{16,3},... | collective-permute-start | bytes 1474568 | tf_op jit(solution)/shard_map/sums_cross_1/ppermute | solution.py:163
  67.1 21.2 %collective-permute-start.10 = (bf16[640,640]{1,0:T(8,128)(2,1)}, bf16[640,640]{1,0:T(8,128)(2,1)}, u32[]{:S(2)}, u32[]{:S(2)}) collective-permute-start(bf16[640,640]{1,0:T(8,128)(2,1)} %collective-permute-done.9), channel_id=1, source_target_pairs={{0,4},{1,5},{2,14},{3,15},{4,8},{5,9},{6,2},{7,3},{8,12},{9,13},{1... | collective-permute-start | bytes 2457608 | tf_op jit(solution)/shard_map/ring_3/ppermute | solution.py:163
  67.7 4.8 %collective-permute-start.1 = (bf16[640,640]{1,0:T(8,128)(2,1)}, bf16[640,640]{1,0:T(8,128)(2,1)}, u32[]{:S(2)}, u32[]{:S(2)}) collective-permute-start(bf16[640,640]{1,0:T(8,128)(2,1)} %get-tuple-element.44), channel_id=1, source_target_pairs={{0,1},{1,0},{2,3},{3,2},{4,5},{5,4},{6,7},{7,6},{8,9},{9,8},{10,11... | collective-permute-start | bytes 2457608 | tf_op jit(solution)/shard_map/cond/branch_1_fun/core_swap/ppermute | solution.py:163
  70.2 2.3 %copy-start.10 = (bf16[384,640]{1,0:T(8,128)(2,1)S(1)}, bf16[384,640]{1,0:T(8,128)(2,1)}, u32[]{:S(2)}) copy-start(bf16[384,640]{1,0:T(8,128)(2,1)} %get-tuple-element.42) | copy-start | bytes 1474564 | tf_op jit(solution)/shard_map/cond
  76.9 18.1 %collective-permute-start.15 = (bf16[384,640]{1,0:T(8,128)(2,1)}, bf16[384,640]{1,0:T(8,128)(2,1)S(1)}, u32[]{:S(2)}, u32[]{:S(2)}) collective-permute-start(bf16[384,640]{1,0:T(8,128)(2,1)} %get-tuple-element.84), channel_id=1, source_target_pairs={{0,0},{2,2},{4,5},{6,7},{8,10},{10,8},{12,15},{14,13},{17,16},{19,... | collective-permute-start | bytes 1474568 | tf_op jit(solution)/shard_map/sums_02/ppermute | solution.py:163
  78.2 18.1 %collective-permute-start.17 = (bf16[384,640]{1,0:T(8,128)(2,1)}, bf16[384,640]{1,0:T(8,128)(2,1)}, u32[]{:S(2)}, u32[]{:S(2)}) collective-permute-start(bf16[384,640]{1,0:T(8,128)(2,1)} %get-tuple-element.84), channel_id=1, source_target_pairs={{1,16},{3,18},{5,21},{7,23},{9,26},{11,24},{13,31},{15,29},{16,0},... | collective-permute-start | bytes 1474568 | tf_op jit(solution)/shard_map/sums_cross_02/ppermute | solution.py:163
  79.7 16.6 %collective-permute-start.16 = (bf16[384,640]{1,0:T(8,128)(2,1)}, bf16[384,640]{1,0:T(8,128)(2,1)}, u32[]{:S(2)}, u32[]{:S(2)}) collective-permute-start(bf16[384,640]{1,0:T(8,128)(2,1)} %get-tuple-element.85), channel_id=1, source_target_pairs={{0,2},{2,0},{4,7},{6,5},{8,8},{10,10},{12,13},{14,15},{17,18},{19,... | collective-permute-start | bytes 1474568 | tf_op jit(solution)/shard_map/sums_20/ppermute | solution.py:163
  84.5 11.8 %collective-permute-start.18 = (bf16[384,640]{1,0:T(8,128)(2,1)}, bf16[384,640]{1,0:T(8,128)(2,1)}, u32[]{:S(2)}, u32[]{:S(2)}) collective-permute-start(bf16[384,640]{1,0:T(8,128)(2,1)} %get-tuple-element.85), channel_id=1, source_target_pairs={{1,18},{3,16},{5,23},{7,21},{9,24},{11,26},{13,29},{15,31},{16,2},... | collective-permute-start | bytes 1474568 | tf_op jit(solution)/shard_map/sums_cross_20/ppermute | solution.py:163
  88.3 8.0 %copy-start.11 = (f32[1280]{0:T(1024)S(1)}, f32[1280]{0:T(1024)}, u32[]{:S(2)}) copy-start(f32[1280]{0:T(1024)} %param.16) | copy-start | bytes 15364
  88.3 3.4 %copy-start.6 = (bf16[384,640]{1,0:T(8,128)(2,1)S(1)}, bf16[384,640]{1,0:T(8,128)(2,1)}, u32[]{:S(2)}) copy-start(bf16[384,640]{1,0:T(8,128)(2,1)} %get-tuple-element.48) | copy-start | bytes 1474564 | tf_op jit(solution)/shard_map/cond
  88.3 3.4 %collective-permute-start.2 = (bf16[640,640]{1,0:T(8,128)(2,1)}, bf16[640,640]{1,0:T(8,128)(2,1)S(1)}, u32[]{:S(2)}, u32[]{:S(2)}) collective-permute-start(bf16[640,640]{1,0:T(8,128)(2,1)} %get-tuple-element.47), channel_id=1, source_target_pairs={{0,1},{1,0},{2,3},{3,2},{4,5},{5,4},{6,7},{7,6},{8,9},{9,8},{10,11... | collective-permute-start | bytes 2457608 | tf_op jit(solution)/shard_map/cond/branch_1_fun/core_swap/ppermute | solution.py:163
  93.0 14.4 %collective-permute-start.13 = (bf16[384,640]{1,0:T(8,128)(2,1)}, bf16[384,640]{1,0:T(8,128)(2,1)S(1)}, u32[]{:S(2)}, u32[]{:S(2)}) collective-permute-start(bf16[384,640]{1,0:T(8,128)(2,1)} %get-tuple-element.101), channel_id=1, source_target_pairs={{0,1},{2,3},{4,6},{6,4},{8,11},{10,9},{12,12},{14,14},{17,17},{19,... | collective-permute-start | bytes 1474568 | tf_op jit(solution)/shard_map/sums_3/ppermute | solution.py:163
  95.0 14.7 %collective-permute-start.14 = (bf16[384,640]{1,0:T(8,128)(2,1)}, bf16[384,640]{1,0:T(8,128)(2,1)S(1)}, u32[]{:S(2)}, u32[]{:S(2)}) collective-permute-start(bf16[384,640]{1,0:T(8,128)(2,1)} %get-tuple-element.101), channel_id=1, source_target_pairs={{1,17},{3,19},{5,22},{7,20},{9,27},{11,25},{13,28},{15,30},{16,1},... | collective-permute-start | bytes 1474568 | tf_op jit(solution)/shard_map/sums_cross_3/ppermute | solution.py:163
  96.3 1.5 %copy-start.1 = (f32[384,1280]{1,0:T(8,128)S(1)}, f32[384,1280]{1,0:T(8,128)}, u32[]{:S(2)}) copy-start(f32[384,1280]{1,0:T(8,128)} %refs_6_.1) | copy-start | bytes 5898244

commit v6 on v3

--- a/solution.py
+++ b/solution.py
@@ -32,6 +32,7 @@
         out_shape=jax.ShapeDtypeStruct((1,), jnp.int32),
         in_specs=[scalar],
         out_specs=scalar,
+        compiler_params=pltpu.CompilerParams(vmem_limit_bytes=MIB),
         cost_estimate=weight(50),
         name="fence",
     )(token)
@@ -180,7 +181,7 @@
 
 def finish(direct, crossed, residual_in, gate, spot):
     rows, width = residual_in.shape
-    step = 128
+    step = rows // 2
     parts = [pl.BlockSpec((step, part.shape[1]), lambda i: (i, 0)) for part in direct + crossed]
     wide = pl.BlockSpec((step, width), lambda i: (i, 0))
     return pl.pallas_call(
@@ -191,7 +192,7 @@
         + parts
         + [wide, pl.BlockSpec((1, width), lambda i: (0, 0))],
         out_specs=wide,
-        compiler_params=pltpu.CompilerParams(vmem_limit_bytes=32 * MIB),
+        compiler_params=pltpu.CompilerParams(vmem_limit_bytes=24 * MIB),
         name="finish",
     )(spot, *direct, *crossed, residual_in, gate[None, :])
 
@@ -217,7 +218,7 @@
     low, high = halos(keyvals)
     w0 = lax.dynamic_slice_in_dim(out_weight, y * half, half, axis=1)
     v0 = send(w0, sibling, "core_swap_0")
-    w0, v0, low, high = tie((w0, v0, low, high))
+    w0, low = tie((w0, low))
     w1 = send(w0, ring, "ring_1")
     attended = attend(queries, keyvals, low, high, pattern, live)
     first = send(
@@ -268,12 +269,11 @@
     s0 = region(token, sums, rows_own, rows_sib, w0, v0)
     w2, s0 = tie((w2, s0))
     w3 = send(w2, ring, "ring_3")
-    w2, *middle = tie((w2, *middle))
     low_sum, high_sum = region(token, mix, rows_own, rows_sib, s0, w2)
+    low_sum, high_sum, *middle = tie((low_sum, high_sum, *middle))
     early = to_owners(low_sum, (0, 2), "02") + to_owners(high_sum, (2, 0), "20")
     w3, low_sum, high_sum = tie((w3, low_sum, high_sum))
     s3 = region(token, end, rows_own, rows_sib, w3)
-    s3, *early = tie((s3, *early))
     middle += early
     last = to_owners(s3, (3, 3), "3")
     spot = jnp.reshape(y, (1,))

time: 118 us -> 112 us (0.949)
  waiting for transfers between devices: 46.6 us -> 41.4 us
  starting transfers between devices: 31.7 us -> 34.4 us
  Pallas kernels: 13.3 us -> 11.5 us
  matrix products: 17.1 us -> 15.7 us
    ppermute x17, waiting for transfers between devices: 27.1 us -> 21.2 us  [send(): return lax.ppermute(array, AXES, route)]
    ppermute x17, starting transfers between devices: 25.6 us -> 28.3 us  [send(): return lax.ppermute(array, AXES, route)]
    ppermute x1, waiting for transfers between devices: 16.1 us -> 18.7 us  [halos(): lax.ppermute(keyvals, 'frame', forward)]
    ppermute x1, waiting for transfers between devices: 3.32 us -> 1.5 us  [halos(): lax.ppermute(keyvals, 'frame', backward)]
    dot_general x4, matrix products: 9.41 us -> 8.05 us  [sums(): total = total + jnp.dot(rows_sib, sib, preferred_element_type=jnp.float32)]
  transfers between devices with their start and end apart: 19 -> 19, of which waited for: 12 -> 11; matrix products, arithmetic and copies ran while one was open for 17% -> 16% of each run, Pallas kernels for 10% -> 9%
where the time goes in v6:
time: 112 us; the launch traced here: 111 us
  waiting for transfers between devices  41.4 us (37%)
  starting transfers between devices  34.4 us (31%)
  matrix products  15.7 us (14%)
  Pallas kernels  11.5 us (10%)
  local copies, waits for them, and re-layouts  5.42 us (5%)
  other arithmetic  1.57 us (1%)
    ppermute x17, starting transfers between devices, send(): return lax.ppermute(array, AXES, route)  28.3 us
    ppermute x17, waiting for transfers between devices, send(): return lax.ppermute(array, AXES, route)  21.2 us
    ppermute x1, waiting for transfers between devices, halos(): lax.ppermute(keyvals, 'frame', forward)  18.7 us
    dot_general x4, matrix products, sums(): total = total + jnp.dot(rows_sib, sib, preferred_element_type=jnp.float32)  8.05 us
    pallas_call x1, Pallas kernels, attend(): pl.pallas_call(attend_kernel, out_shape=jax.ShapeDtypeStruct((rows, width...  7.66 us
    dot_general x4, matrix products, sums(): total = jnp.dot(rows_own, own, preferred_element_type=jnp.float32)  7.64 us
    unnamed x14, local copies, waits for them, and re-layouts  4.44 us
    ppermute x1, starting transfers between devices, halos(): lax.ppermute(keyvals, 'frame', forward)  3.61 us
  transfers between devices with their start and end apart: 19, of which 11 were waited for; matrix products, arithmetic and copies ran while one was open for 16% of the time, Pallas kernels for 9%

profile of v6, /device:TPU:8, one launch (start us, length us, event | category | flops | bytes accessed | tf_op | source)
XLA Modules:
  0.0 110.9 jit_solution(866146435684055726)
XLA Ops:
  0.0 3.6 %collective-permute-start.3 = (bf16[2,384,640]{2,1,0:T(8,128)(2,1)}, bf16[2,384,640]{2,1,0:T(8,128)(2,1)S(1)}, u32[]{:S(2)}, u32[]{:S(2)}) collective-permute-start(bf16[2,384,640]{2,1,0:T(8,128)(2,1)} %own_ref.1), channel_id=1, source_target_pairs={{0,4},{4,8},{8,12},{1,5},{5,9},{9,13},{2,6},{6,10},{10,14},{3,7},{... | collective-permute-start | bytes 2949128 | tf_op jit(solution)/shard_map/ppermute | solution.py:120
  3.6 2.4 %collective-permute-start.4 = (bf16[2,384,640]{2,1,0:T(8,128)(2,1)}, bf16[2,384,640]{2,1,0:T(8,128)(2,1)}, u32[]{:S(2)}, u32[]{:S(2)}) collective-permute-start(bf16[2,384,640]{2,1,0:T(8,128)(2,1)} %own_ref.1), channel_id=1, source_target_pairs={{4,0},{8,4},{12,8},{5,1},{9,5},{13,9},{6,2},{10,6},{14,10},{7,3},{... | collective-permute-start | bytes 2949128 | tf_op jit(solution)/shard_map/ppermute | solution.py:120
  6.1 1.0 constant_dynamic-slice_fusion
  7.0 18.7 %collective-permute-done.3.low_ref = bf16[2,384,640]{2,1,0:T(8,128)(2,1)S(1)} collective-permute-done((bf16[2,384,640]{2,1,0:T(8,128)(2,1)}, bf16[2,384,640]{2,1,0:T(8,128)(2,1)S(1)}, u32[]{:S(2)}, u32[]{:S(2)}) %collective-permute-start.3) | collective-permute-done | bytes 983072 | tf_op jit(solution)/shard_map/ppermute | solution.py:120
  25.7 1.6 %collective-permute-start.7 = (bf16[640,640]{1,0:T(8,128)(2,1)}, bf16[640,640]{1,0:T(8,128)(2,1)}, u32[]{:S(2)}, u32[]{:S(2)}) collective-permute-start(bf16[640,640]{1,0:T(8,128)(2,1)} %constant_dynamic-slice_fusion), channel_id=1, source_target_pairs={{0,4},{1,5},{2,14},{3,15},{4,8},{5,9},{6,2},{7,3},{8,12},{9,13},{1... | collective-permute-start | bytes 2457608 | tf_op jit(solution)/shard_map/ring_1/ppermute | solution.py:163
  27.3 0.7 subtract_clamp_fusion.ids
  28.0 1.5 %collective-permute-done.4.high_ref = bf16[2,384,640]{2,1,0:T(8,128)(2,1)} collective-permute-done((bf16[2,384,640]{2,1,0:T(8,128)(2,1)}, bf16[2,384,640]{2,1,0:T(8,128)(2,1)}, u32[]{:S(2)}, u32[]{:S(2)}) %collective-permute-start.4) | collective-permute-done | bytes 983072 | tf_op jit(solution)/shard_map/ppermute | solution.py:120
  29.5 1.2 %copy-done.2 = bf16[2,384,640]{2,1,0:T(8,128)(2,1)S(1)} copy-done((bf16[2,384,640]{2,1,0:T(8,128)(2,1)S(1)}, bf16[2,384,640]{2,1,0:T(8,128)(2,1)}, u32[]{:S(2)}) %copy-start.2) | copy-done | bytes 983064
  30.7 1.0 copy-done.3
  31.7 0.7 copy-done.4
  32.4 7.7 %attend.1 = bf16[384,640]{1,0:T(8,128)(2,1)S(1)} custom-call(s32[6,8]{1,0:T(8,128)S(1)} %subtract_clamp_fusion.ids, s32[6]{0:T(128)S(1)} %copy-done.4, bf16[384,640]{1,0:T(8,128)(2,1)S(1)} %copy-done.3, bf16[2,384,640]{2,1,0:T(8,128)(2,1)S(1)} %copy-done.2, bf16[2,384,640]{2,1,0:T(8,128)(2,1)S(1)} %collective-permute-done.3.low_ref, ...), custom_call_target="tpu_custom_call" | custom-call | flops 8000000000 | bytes 24000000 | tf_op jit(solution)/shard_map/attend/pallas_call | solution.py:101
  40.0 1.5 %collective-permute-start.5 = (bf16[384,640]{1,0:T(8,128)(2,1)S(1)}, bf16[384,640]{1,0:T(8,128)(2,1)S(1)}, u32[]{:S(2)}, u32[]{:S(2)}) collective-permute-start(bf16[384,640]{1,0:T(8,128)(2,1)S(1)} %attend.1), channel_id=1, source_target_pairs={{0,16},{1,0},{2,18},{3,2},{4,20},{5,4},{6,22},{7,6},{8,24},{9,8},{... | collective-permute-start | bytes 1474568 | tf_op jit(solution)/shard_map/rows_1/ppermute | solution.py:163
  41.6 0.7 collective-permute-start.6
  42.3 3.0 %collective-permute-done.7 = bf16[640,640]{1,0:T(8,128)(2,1)} collective-permute-done((bf16[640,640]{1,0:T(8,128)(2,1)}, bf16[640,640]{1,0:T(8,128)(2,1)}, u32[]{:S(2)}, u32[]{:S(2)}) %collective-permute-start.7) | collective-permute-done | bytes 819232 | tf_op jit(solution)/shard_map/ring_1/ppermute | solution.py:163
  45.3 1.6 %collective-permute-start.8 = (bf16[640,640]{1,0:T(8,128)(2,1)}, bf16[640,640]{1,0:T(8,128)(2,1)}, u32[]{:S(2)}, u32[]{:S(2)}) collective-permute-start(bf16[640,640]{1,0:T(8,128)(2,1)} %collective-permute-done.7), channel_id=1, source_target_pairs={{0,4},{1,5},{2,14},{3,15},{4,8},{5,9},{6,2},{7,3},{8,12},{9,13},{1... | collective-permute-start | bytes 2457608 | tf_op jit(solution)/shard_map/ring_2/ppermute | solution.py:163
  47.4 4.4 %collective-permute-done.5 = bf16[384,640]{1,0:T(8,128)(2,1)S(1)} collective-permute-done((bf16[384,640]{1,0:T(8,128)(2,1)S(1)}, bf16[384,640]{1,0:T(8,128)(2,1)S(1)}, u32[]{:S(2)}, u32[]{:S(2)}) %collective-permute-start.5) | collective-permute-done | bytes 491552 | tf_op jit(solution)/shard_map/rows_1/ppermute | solution.py:163
  52.5 0.9 broadcast_select_fusion.2
  53.4 5.0 %conditional.6 = (bf16[384,640]{1,0:T(8,128)(2,1)}) conditional(s32[]{:T(128)} %bitcast.1, () %tuple.46, (bf16[384,640]{1,0:T(8,128)(2,1)}, bf16[640,640]{1,0:T(8,128)(2,1)}, bf16[384,640]{1,0:T(8,128)(2,1)S(1)}) %tuple.47), branch_computations={%region_4.5_spmd, %region_5.6_spmd} | conditional | flops 629637120 | bytes 8355888 | solution.py:237
  53.4 1.5 %collective-permute-start.1 = (bf16[640,640]{1,0:T(8,128)(2,1)}, bf16[640,640]{1,0:T(8,128)(2,1)S(1)}, u32[]{:S(2)}, u32[]{:S(2)}) collective-permute-start(bf16[640,640]{1,0:T(8,128)(2,1)} %get-tuple-element.56), channel_id=1, source_target_pairs={{0,1},{1,0},{2,3},{3,2},{4,5},{5,4},{6,7},{7,6},{8,9},{9,8},{10,11... | collective-permute-start | bytes 2457608 | tf_op jit(solution)/shard_map/cond/branch_1_fun/core_swap/ppermute | solution.py:163
  54.8 1.9 %fusion.6 = f32[384,640]{1,0:T(8,128)S(1)} fusion(bf16[384,640]{1,0:T(8,128)(2,1)} %get-tuple-element.55, bf16[640,640]{1,0:T(8,128)(2,1)} %get-tuple-element.56), kind=kOutput, calls=%fused_computation.16 | convolution fusion | flops 314572800 | bytes 2293760 | tf_op jit(solution)/shard_map/cond/branch_1_fun/dot_general | solution.py:245
  57.0 1.4 %fusion.2 = bf16[384,640]{1,0:T(8,128)(2,1)} fusion(f32[384,640]{1,0:T(8,128)S(1)} %fusion.6, bf16[384,640]{1,0:T(8,128)(2,1)S(1)} %get-tuple-element.57, bf16[640,640]{1,0:T(8,128)(2,1)S(1)} %collective-permute-done.1), kind=kOutput, calls=%fused_computation.7 | convolution fusion | flops 315064320 | bytes 2785280 | tf_op jit(solution)/shard_map/cond/branch_1_fun/dot_general | solution.py:246
  58.4 1.7 %collective-permute-start.11 = (bf16[384,640]{1,0:T(8,128)(2,1)}, bf16[384,640]{1,0:T(8,128)(2,1)S(1)}, u32[]{:S(2)}, u32[]{:S(2)}) collective-permute-start(bf16[384,640]{1,0:T(8,128)(2,1)} %get-tuple-element.102), channel_id=1, source_target_pairs={{0,3},{2,1},{4,4},{6,6},{8,9},{10,11},{12,14},{14,12},{17,19},{19,... | collective-permute-start | bytes 1474568 | tf_op jit(solution)/shard_map/sums_1/ppermute | solution.py:163
  60.1 1.3 %collective-permute-start.12 = (bf16[384,640]{1,0:T(8,128)(2,1)}, bf16[384,640]{1,0:T(8,128)(2,1)S(1)}, u32[]{:S(2)}, u32[]{:S(2)}) collective-permute-start(bf16[384,640]{1,0:T(8,128)(2,1)} %get-tuple-element.102), channel_id=1, source_target_pairs={{1,19},{3,17},{5,20},{7,22},{9,25},{11,27},{13,30},{15,28},{16,3},... | collective-permute-start | bytes 1474568 | tf_op jit(solution)/shard_map/sums_cross_1/ppermute | solution.py:163
  61.4 4.5 %conditional.4 = (bf16[384,640]{1,0:T(8,128)(2,1)}) conditional(s32[]{:T(128)} %bitcast.1, () %tuple.41, (bf16[384,640]{1,0:T(8,128)(2,1)}, bf16[640,640]{1,0:T(8,128)(2,1)}, bf16[384,640]{1,0:T(8,128)(2,1)S(1)}, bf16[640,640]{1,0:T(8,128)(2,1)}) %tuple.42), branch_computations={%region_0.1_spmd, %region_1.2_spmd} | conditional | flops 629637120 | bytes 5079048 | solution.py:237
  61.4 1.9 %fusion.4 = f32[384,640]{1,0:T(8,128)S(1)} fusion(bf16[384,640]{1,0:T(8,128)(2,1)} %get-tuple-element.46, bf16[640,640]{1,0:T(8,128)(2,1)} %get-tuple-element.47), kind=kOutput, calls=%fused_computation.14 | convolution fusion | flops 314572800 | bytes 2293760 | tf_op jit(solution)/shard_map/cond/branch_1_fun/dot_general | solution.py:245
  63.3 2.6 %fusion = bf16[384,640]{1,0:T(8,128)(2,1)} fusion(f32[384,640]{1,0:T(8,128)S(1)} %fusion.4, bf16[384,640]{1,0:T(8,128)(2,1)S(1)} %get-tuple-element.48, bf16[640,640]{1,0:T(8,128)(2,1)} %get-tuple-element.49), kind=kOutput, calls=%fused_computation.1 | convolution fusion | flops 315064320 | bytes 2785280 | tf_op jit(solution)/shard_map/cond/branch_1_fun/dot_general | solution.py:246
  65.9 0.6 collective-permute-done.8
  66.4 2.0 %collective-permute-start.10 = (bf16[640,640]{1,0:T(8,128)(2,1)}, bf16[640,640]{1,0:T(8,128)(2,1)}, u32[]{:S(2)}, u32[]{:S(2)}) collective-permute-start(bf16[640,640]{1,0:T(8,128)(2,1)} %collective-permute-done.8), channel_id=1, source_target_pairs={{0,4},{1,5},{2,14},{3,15},{4,8},{5,9},{6,2},{7,3},{8,12},{9,13},{1... | collective-permute-start | bytes 2457608 | tf_op jit(solution)/shard_map/ring_3/ppermute | solution.py:163
  68.5 7.9 %conditional.5 = (bf16[384,640]{1,0:T(8,128)(2,1)}, bf16[384,640]{1,0:T(8,128)(2,1)}) conditional(s32[]{:T(128)} %bitcast.1, () %tuple.44, (s32[]{:T(128)}, bf16[384,640]{1,0:T(8,128)(2,1)}, bf16[640,640]{1,0:T(8,128)(2,1)}, bf16[384,640]{1,0:T(8,128)(2,1)S(1)}, bf16[384,640]{1,0:T(8,128)(2,1)}) %tuple.45), branch_computations={%region_2.3_spmd, %region_3.4_spmd} | conditional | flops 630128640 | bytes 11305054 | solution.py:237
  68.5 2.9 %collective-permute-start = (bf16[640,640]{1,0:T(8,128)(2,1)}, bf16[640,640]{1,0:T(8,128)(2,1)}, u32[]{:S(2)}, u32[]{:S(2)}) collective-permute-start(bf16[640,640]{1,0:T(8,128)(2,1)} %get-tuple-element.53), channel_id=1, source_target_pairs={{0,1},{1,0},{2,3},{3,2},{4,5},{5,4},{6,7},{7,6},{8,9},{9,8},{10,11... | collective-permute-start | bytes 2457608 | tf_op jit(solution)/shard_map/cond/branch_1_fun/core_swap/ppermute | solution.py:163
  71.4 1.9 %fusion.5 = f32[384,640]{1,0:T(8,128)S(1)} fusion(bf16[384,640]{1,0:T(8,128)(2,1)} %get-tuple-element.52, bf16[640,640]{1,0:T(8,128)(2,1)} %get-tuple-element.53), kind=kOutput, calls=%fused_computation.15 | convolution fusion | flops 314572800 | bytes 2293760 | tf_op jit(solution)/shard_map/cond/branch_1_fun/dot_general | solution.py:245
  73.7 2.7 %broadcast_select_fusion = (bf16[384,640]{1,0:T(8,128)(2,1)}, bf16[384,640]{1,0:T(8,128)(2,1)}) fusion(bf16[384,640]{1,0:T(8,128)(2,1)S(1)} %copy-done.7, pred[]{:T(512)S(6)} %eq.5, f32[384,640]{1,0:T(8,128)S(1)} %fusion.5, bf16[384,640]{1,0:T(8,128)(2,1)S(1)} %get-tuple-element.54, bf16[640,640]{1,0:T(8,128)(2,1)} %collective-permute-done), kind=kOutput, calls=%fused_computation.4 | convolution fusion | flops 315555840 | bytes 3768321 | tf_op jit(solution)/shard_map/cond/branch_1_fun/dot_general | solution.py:246
  76.4 2.3 %collective-permute-start.15 = (bf16[384,640]{1,0:T(8,128)(2,1)}, bf16[384,640]{1,0:T(8,128)(2,1)S(1)}, u32[]{:S(2)}, u32[]{:S(2)}) collective-permute-start(bf16[384,640]{1,0:T(8,128)(2,1)} %get-tuple-element.88), channel_id=1, source_target_pairs={{0,0},{2,2},{4,5},{6,7},{8,10},{10,8},{12,15},{14,13},{17,16},{19,... | collective-permute-start | bytes 1474568 | tf_op jit(solution)/shard_map/sums_02/ppermute | solution.py:163
  78.7 1.5 %collective-permute-start.17 = (bf16[384,640]{1,0:T(8,128)(2,1)}, bf16[384,640]{1,0:T(8,128)(2,1)}, u32[]{:S(2)}, u32[]{:S(2)}) collective-permute-start(bf16[384,640]{1,0:T(8,128)(2,1)} %get-tuple-element.88), channel_id=1, source_target_pairs={{1,16},{3,18},{5,21},{7,23},{9,26},{11,24},{13,31},{15,29},{16,0},... | collective-permute-start | bytes 1474568 | tf_op jit(solution)/shard_map/sums_cross_02/ppermute | solution.py:163
  80.2 4.0 %collective-permute-start.16 = (bf16[384,640]{1,0:T(8,128)(2,1)}, bf16[384,640]{1,0:T(8,128)(2,1)}, u32[]{:S(2)}, u32[]{:S(2)}) collective-permute-start(bf16[384,640]{1,0:T(8,128)(2,1)} %get-tuple-element.89), channel_id=1, source_target_pairs={{0,2},{2,0},{4,7},{6,5},{8,8},{10,10},{12,13},{14,15},{17,18},{19,... | collective-permute-start | bytes 1474568 | tf_op jit(solution)/shard_map/sums_20/ppermute | solution.py:163
  84.2 1.4 %collective-permute-start.18 = (bf16[384,640]{1,0:T(8,128)(2,1)}, bf16[384,640]{1,0:T(8,128)(2,1)}, u32[]{:S(2)}, u32[]{:S(2)}) collective-permute-start(bf16[384,640]{1,0:T(8,128)(2,1)} %get-tuple-element.89), channel_id=1, source_target_pairs={{1,18},{3,16},{5,23},{7,21},{9,24},{11,26},{13,29},{15,31},{16,2},... | collective-permute-start | bytes 1474568 | tf_op jit(solution)/shard_map/sums_cross_20/ppermute | solution.py:163
  85.6 2.6 %collective-permute-done.10 = bf16[640,640]{1,0:T(8,128)(2,1)} collective-permute-done((bf16[640,640]{1,0:T(8,128)(2,1)}, bf16[640,640]{1,0:T(8,128)(2,1)}, u32[]{:S(2)}, u32[]{:S(2)}) %collective-permute-start.10) | collective-permute-done | bytes 819232 | tf_op jit(solution)/shard_map/ring_3/ppermute | solution.py:163
  88.3 4.5 %conditional.7 = (bf16[384,640]{1,0:T(8,128)(2,1)}) conditional(s32[]{:T(128)} %bitcast.1, () %tuple.40, (bf16[384,640]{1,0:T(8,128)(2,1)}, bf16[640,640]{1,0:T(8,128)(2,1)}, bf16[384,640]{1,0:T(8,128)(2,1)}) %tuple.61), branch_computations={%region_6.7_spmd, %region_7.8_spmd} | conditional | flops 629637120 | bytes 10321996 | solution.py:237
  88.3 1.0 collective-permute-start.2
  89.2 1.9 %fusion.7 = f32[384,640]{1,0:T(8,128)S(1)} fusion(bf16[384,640]{1,0:T(8,128)(2,1)} %get-tuple-element.58, bf16[640,640]{1,0:T(8,128)(2,1)} %get-tuple-element.59), kind=kOutput, calls=%fused_computation.17 | convolution fusion | flops 314572800 | bytes 2293760 | tf_op jit(solution)/shard_map/cond/branch_1_fun/dot_general | solution.py:245
  91.4 1.4 %fusion.3 = bf16[384,640]{1,0:T(8,128)(2,1)} fusion(f32[384,640]{1,0:T(8,128)S(1)} %fusion.7, bf16[384,640]{1,0:T(8,128)(2,1)S(1)} %copy-done.6, bf16[640,640]{1,0:T(8,128)(2,1)S(1)} %collective-permute-done.2), kind=kOutput, calls=%fused_computation.9 | convolution fusion | flops 315064320 | bytes 2785280 | tf_op jit(solution)/shard_map/cond/branch_1_fun/dot_general | solution.py:246
  92.8 2.1 %collective-permute-start.13 = (bf16[384,640]{1,0:T(8,128)(2,1)}, bf16[384,640]{1,0:T(8,128)(2,1)S(1)}, u32[]{:S(2)}, u32[]{:S(2)}) collective-permute-start(bf16[384,640]{1,0:T(8,128)(2,1)} %get-tuple-element.103), channel_id=1, source_target_pairs={{0,1},{2,3},{4,6},{6,4},{8,11},{10,9},{12,12},{14,14},{17,17},{19,... | collective-permute-start | bytes 1474568 | tf_op jit(solution)/shard_map/sums_3/ppermute | solution.py:163
  94.9 1.3 %collective-permute-start.14 = (bf16[384,640]{1,0:T(8,128)(2,1)}, bf16[384,640]{1,0:T(8,128)(2,1)S(1)}, u32[]{:S(2)}, u32[]{:S(2)}) collective-permute-start(bf16[384,640]{1,0:T(8,128)(2,1)} %get-tuple-element.103), channel_id=1, source_target_pairs={{1,17},{3,19},{5,22},{7,20},{9,27},{11,25},{13,28},{15,30},{16,1},... | collective-permute-start | bytes 1474568 | tf_op jit(solution)/shard_map/sums_cross_3/ppermute | solution.py:163
  96.3 1.5 %copy-done.1 = f32[384,1280]{1,0:T(8,128)S(1)} copy-done((f32[384,1280]{1,0:T(8,128)S(1)}, f32[384,1280]{1,0:T(8,128)}, u32[]{:S(2)}) %copy-start.1) | copy-done | bytes 1966104
  97.8 1.9 %finish.2.refs_2_ = f32[384,1280]{1,0:T(8,128)S(1)} custom-call(s32[1]{0:T(128)} %bitcast.spot, bf16[384,640]{1,0:T(8,128)(2,1)S(1)} %collective-permute-done.11.refs_0_, bf16[384,640]{1,0:T(8,128)(2,1)S(1)} %collective-permute-done.15.refs_1_, bf16[384,640]{1,0:T(8,128)(2,1)} %collective-permute-done.16.refs_2_, ...), custom_call_target="tpu_custom_call" | custom-call | tf_op jit(solution)/shard_map/finish/pallas_call | solution.py:187
  99.7 7.4 %collective-permute-done.13.refs_0_ = bf16[384,640]{1,0:T(8,128)(2,1)S(1)} collective-permute-done((bf16[384,640]{1,0:T(8,128)(2,1)}, bf16[384,640]{1,0:T(8,128)(2,1)S(1)}, u32[]{:S(2)}, u32[]{:S(2)}) %collective-permute-start.13) | collective-permute-done | bytes 491552 | tf_op jit(solution)/shard_map/sums_3/ppermute | solution.py:163
  107.1 2.3 %collective-permute-done.14.refs_1_ = bf16[384,640]{1,0:T(8,128)(2,1)S(1)} collective-permute-done((bf16[384,640]{1,0:T(8,128)(2,1)}, bf16[384,640]{1,0:T(8,128)(2,1)S(1)}, u32[]{:S(2)}, u32[]{:S(2)}) %collective-permute-start.14) | collective-permute-done | bytes 491552 | tf_op jit(solution)/shard_map/sums_cross_3/ppermute | solution.py:163
  109.4 1.4 %finish.3 = f32[384,1280]{1,0:T(8,128)} custom-call(s32[1]{0:T(128)} %bitcast.spot, bf16[384,640]{1,0:T(8,128)(2,1)S(1)} %collective-permute-done.13.refs_0_, bf16[384,640]{1,0:T(8,128)(2,1)S(1)} %collective-permute-done.14.refs_1_, f32[384,1280]{1,0:T(8,128)S(1)} %finish.2.refs_2_, f32[1,1280]{1,0:T(1,128)S(1)} %broadcast_in_dim.4.refs_7_.refs_3_), custom_call_target="tpu_custom_call" | custom-call | tf_op jit(solution)/shard_map/finish/pallas_call | solution.py:187
  (28 shorter events, 1.5 us)
Async XLA Ops:
  0.0 6.1 %copy-start = (bf16[640,1280]{1,0:T(8,128)(2,1)S(1)}, bf16[640,1280]{1,0:T(8,128)(2,1)}, u32[]{:S(2)}) copy-start(bf16[640,1280]{1,0:T(8,128)(2,1)} %param.19) | copy-start | bytes 4915204
  0.0 25.7 %collective-permute-start.3 = (bf16[2,384,640]{2,1,0:T(8,128)(2,1)}, bf16[2,384,640]{2,1,0:T(8,128)(2,1)S(1)}, u32[]{:S(2)}, u32[]{:S(2)}) collective-permute-start(bf16[2,384,640]{2,1,0:T(8,128)(2,1)} %own_ref.1), channel_id=1, source_target_pairs={{0,4},{4,8},{8,12},{1,5},{5,9},{9,13},{2,6},{6,10},{10,14},{3,7},{... | collective-permute-start | bytes 2949128 | tf_op jit(solution)/shard_map/ppermute | solution.py:120
  3.6 25.9 %collective-permute-start.4 = (bf16[2,384,640]{2,1,0:T(8,128)(2,1)}, bf16[2,384,640]{2,1,0:T(8,128)(2,1)}, u32[]{:S(2)}, u32[]{:S(2)}) collective-permute-start(bf16[2,384,640]{2,1,0:T(8,128)(2,1)} %own_ref.1), channel_id=1, source_target_pairs={{4,0},{8,4},{12,8},{5,1},{9,5},{13,9},{6,2},{10,6},{14,10},{7,3},{... | collective-permute-start | bytes 2949128 | tf_op jit(solution)/shard_map/ppermute | solution.py:120
  7.0 54.3 %collective-permute-start.9 = (bf16[640,640]{1,0:T(8,128)(2,1)}, bf16[640,640]{1,0:T(8,128)(2,1)}, u32[]{:S(2)}, u32[]{:S(2)}) collective-permute-start(bf16[640,640]{1,0:T(8,128)(2,1)} %constant_dynamic-slice_fusion), channel_id=1, source_target_pairs={{0,1},{1,0},{2,3},{3,2},{4,5},{5,4},{6,7},{7,6},{8,9},{9,8},{10,11... | collective-permute-start | bytes 2457608 | tf_op jit(solution)/shard_map/core_swap_0/ppermute | solution.py:163
  25.7 19.5 %collective-permute-start.7 = (bf16[640,640]{1,0:T(8,128)(2,1)}, bf16[640,640]{1,0:T(8,128)(2,1)}, u32[]{:S(2)}, u32[]{:S(2)}) collective-permute-start(bf16[640,640]{1,0:T(8,128)(2,1)} %constant_dynamic-slice_fusion), channel_id=1, source_target_pairs={{0,4},{1,5},{2,14},{3,15},{4,8},{5,9},{6,2},{7,3},{8,12},{9,13},{1... | collective-permute-start | bytes 2457608 | tf_op jit(solution)/shard_map/ring_1/ppermute | solution.py:163
  29.5 1.2 %copy-start.2 = (bf16[2,384,640]{2,1,0:T(8,128)(2,1)S(1)}, bf16[2,384,640]{2,1,0:T(8,128)(2,1)}, u32[]{:S(2)}) copy-start(bf16[2,384,640]{2,1,0:T(8,128)(2,1)} %own_ref.1) | copy-start | bytes 2949124
  30.7 1.0 copy-start.3
  31.7 0.7 copy-start.4
  40.0 11.8 %collective-permute-start.5 = (bf16[384,640]{1,0:T(8,128)(2,1)S(1)}, bf16[384,640]{1,0:T(8,128)(2,1)S(1)}, u32[]{:S(2)}, u32[]{:S(2)}) collective-permute-start(bf16[384,640]{1,0:T(8,128)(2,1)S(1)} %attend.1), channel_id=1, source_target_pairs={{0,16},{1,0},{2,18},{3,2},{4,20},{5,4},{6,22},{7,6},{8,24},{9,8},{... | collective-permute-start | bytes 1474568 | tf_op jit(solution)/shard_map/rows_1/ppermute | solution.py:163
  41.6 10.2 %collective-permute-start.6 = (bf16[384,640]{1,0:T(8,128)(2,1)S(1)}, bf16[384,640]{1,0:T(8,128)(2,1)S(1)}, u32[]{:S(2)}, u32[]{:S(2)}) collective-permute-start(bf16[384,640]{1,0:T(8,128)(2,1)S(1)} %attend.1), channel_id=1, source_target_pairs={{1,16},{3,18},{5,20},{7,22},{9,24},{11,26},{13,28},{15,30},{16,1},... | collective-permute-start | bytes 1474568 | tf_op jit(solution)/shard_map/rows_2/ppermute | solution.py:163
  45.3 21.2 %collective-permute-start.8 = (bf16[640,640]{1,0:T(8,128)(2,1)}, bf16[640,640]{1,0:T(8,128)(2,1)}, u32[]{:S(2)}, u32[]{:S(2)}) collective-permute-start(bf16[640,640]{1,0:T(8,128)(2,1)} %collective-permute-done.7), channel_id=1, source_target_pairs={{0,4},{1,5},{2,14},{3,15},{4,8},{5,9},{6,2},{7,3},{8,12},{9,13},{1... | collective-permute-start | bytes 2457608 | tf_op jit(solution)/shard_map/ring_2/ppermute | solution.py:163
  53.3 15.1 %copy-start.5 = (bf16[384,640]{1,0:T(8,128)(2,1)}, bf16[384,640]{1,0:T(8,128)(2,1)S(1)}, u32[]{:S(2)}) copy-start(bf16[384,640]{1,0:T(8,128)(2,1)S(1)} %get-tuple-element.95) | copy-start | bytes 1474564
  53.4 3.7 %collective-permute-start.1 = (bf16[640,640]{1,0:T(8,128)(2,1)}, bf16[640,640]{1,0:T(8,128)(2,1)S(1)}, u32[]{:S(2)}, u32[]{:S(2)}) collective-permute-start(bf16[640,640]{1,0:T(8,128)(2,1)} %get-tuple-element.56), channel_id=1, source_target_pairs={{0,1},{1,0},{2,3},{3,2},{4,5},{5,4},{6,7},{7,6},{8,9},{9,8},{10,11... | collective-permute-start | bytes 2457608 | tf_op jit(solution)/shard_map/cond/branch_1_fun/core_swap/ppermute | solution.py:163
  58.4 18.0 %collective-permute-start.11 = (bf16[384,640]{1,0:T(8,128)(2,1)}, bf16[384,640]{1,0:T(8,128)(2,1)S(1)}, u32[]{:S(2)}, u32[]{:S(2)}) collective-permute-start(bf16[384,640]{1,0:T(8,128)(2,1)} %get-tuple-element.102), channel_id=1, source_target_pairs={{0,3},{2,1},{4,4},{6,6},{8,9},{10,11},{12,14},{14,12},{17,19},{19,... | collective-permute-start | bytes 1474568 | tf_op jit(solution)/shard_map/sums_1/ppermute | solution.py:163
  60.1 16.3 %collective-permute-start.12 = (bf16[384,640]{1,0:T(8,128)(2,1)}, bf16[384,640]{1,0:T(8,128)(2,1)S(1)}, u32[]{:S(2)}, u32[]{:S(2)}) collective-permute-start(bf16[384,640]{1,0:T(8,128)(2,1)} %get-tuple-element.102), channel_id=1, source_target_pairs={{1,19},{3,17},{5,20},{7,22},{9,25},{11,27},{13,30},{15,28},{16,3},... | collective-permute-start | bytes 1474568 | tf_op jit(solution)/shard_map/sums_cross_1/ppermute | solution.py:163
  66.4 21.8 %collective-permute-start.10 = (bf16[640,640]{1,0:T(8,128)(2,1)}, bf16[640,640]{1,0:T(8,128)(2,1)}, u32[]{:S(2)}, u32[]{:S(2)}) collective-permute-start(bf16[640,640]{1,0:T(8,128)(2,1)} %collective-permute-done.8), channel_id=1, source_target_pairs={{0,4},{1,5},{2,14},{3,15},{4,8},{5,9},{6,2},{7,3},{8,12},{9,13},{1... | collective-permute-start | bytes 2457608 | tf_op jit(solution)/shard_map/ring_3/ppermute | solution.py:163
  68.5 5.2 %collective-permute-start = (bf16[640,640]{1,0:T(8,128)(2,1)}, bf16[640,640]{1,0:T(8,128)(2,1)}, u32[]{:S(2)}, u32[]{:S(2)}) collective-permute-start(bf16[640,640]{1,0:T(8,128)(2,1)} %get-tuple-element.53), channel_id=1, source_target_pairs={{0,1},{1,0},{2,3},{3,2},{4,5},{5,4},{6,7},{7,6},{8,9},{9,8},{10,11... | collective-permute-start | bytes 2457608 | tf_op jit(solution)/shard_map/cond/branch_1_fun/core_swap/ppermute | solution.py:163
  71.4 2.3 %copy-start.7 = (bf16[384,640]{1,0:T(8,128)(2,1)S(1)}, bf16[384,640]{1,0:T(8,128)(2,1)}, u32[]{:S(2)}) copy-start(bf16[384,640]{1,0:T(8,128)(2,1)} %get-tuple-element.51) | copy-start | bytes 1474564 | tf_op jit(solution)/shard_map/cond
  76.4 18.5 %collective-permute-start.15 = (bf16[384,640]{1,0:T(8,128)(2,1)}, bf16[384,640]{1,0:T(8,128)(2,1)S(1)}, u32[]{:S(2)}, u32[]{:S(2)}) collective-permute-start(bf16[384,640]{1,0:T(8,128)(2,1)} %get-tuple-element.88), channel_id=1, source_target_pairs={{0,0},{2,2},{4,5},{6,7},{8,10},{10,8},{12,15},{14,13},{17,16},{19,... | collective-permute-start | bytes 1474568 | tf_op jit(solution)/shard_map/sums_02/ppermute | solution.py:163
  78.7 17.5 %collective-permute-start.17 = (bf16[384,640]{1,0:T(8,128)(2,1)}, bf16[384,640]{1,0:T(8,128)(2,1)}, u32[]{:S(2)}, u32[]{:S(2)}) collective-permute-start(bf16[384,640]{1,0:T(8,128)(2,1)} %get-tuple-element.88), channel_id=1, source_target_pairs={{1,16},{3,18},{5,21},{7,23},{9,26},{11,24},{13,31},{15,29},{16,0},... | collective-permute-start | bytes 1474568 | tf_op jit(solution)/shard_map/sums_cross_02/ppermute | solution.py:163
  80.2 16.0 %collective-permute-start.16 = (bf16[384,640]{1,0:T(8,128)(2,1)}, bf16[384,640]{1,0:T(8,128)(2,1)}, u32[]{:S(2)}, u32[]{:S(2)}) collective-permute-start(bf16[384,640]{1,0:T(8,128)(2,1)} %get-tuple-element.89), channel_id=1, source_target_pairs={{0,2},{2,0},{4,7},{6,5},{8,8},{10,10},{12,13},{14,15},{17,18},{19,... | collective-permute-start | bytes 1474568 | tf_op jit(solution)/shard_map/sums_20/ppermute | solution.py:163
  84.2 12.1 %collective-permute-start.18 = (bf16[384,640]{1,0:T(8,128)(2,1)}, bf16[384,640]{1,0:T(8,128)(2,1)}, u32[]{:S(2)}, u32[]{:S(2)}) collective-permute-start(bf16[384,640]{1,0:T(8,128)(2,1)} %get-tuple-element.89), channel_id=1, source_target_pairs={{1,18},{3,16},{5,23},{7,21},{9,24},{11,26},{13,29},{15,31},{16,2},... | collective-permute-start | bytes 1474568 | tf_op jit(solution)/shard_map/sums_cross_20/ppermute | solution.py:163
  88.3 8.0 %copy-start.8 = (f32[1280]{0:T(1024)S(1)}, f32[1280]{0:T(1024)}, u32[]{:S(2)}) copy-start(f32[1280]{0:T(1024)} %param.18) | copy-start | bytes 15364
  88.3 3.1 %copy-start.6 = (bf16[384,640]{1,0:T(8,128)(2,1)S(1)}, bf16[384,640]{1,0:T(8,128)(2,1)}, u32[]{:S(2)}) copy-start(bf16[384,640]{1,0:T(8,128)(2,1)} %get-tuple-element.60) | copy-start | bytes 1474564 | tf_op jit(solution)/shard_map/cond
  88.3 3.1 %collective-permute-start.2 = (bf16[640,640]{1,0:T(8,128)(2,1)}, bf16[640,640]{1,0:T(8,128)(2,1)S(1)}, u32[]{:S(2)}, u32[]{:S(2)}) collective-permute-start(bf16[640,640]{1,0:T(8,128)(2,1)} %get-tuple-element.59), channel_id=1, source_target_pairs={{0,1},{1,0},{2,3},{3,2},{4,5},{5,4},{6,7},{7,6},{8,9},{9,8},{10,11... | collective-permute-start | bytes 2457608 | tf_op jit(solution)/shard_map/cond/branch_1_fun/core_swap/ppermute | solution.py:163
  92.8 14.3 %collective-permute-start.13 = (bf16[384,640]{1,0:T(8,128)(2,1)}, bf16[384,640]{1,0:T(8,128)(2,1)S(1)}, u32[]{:S(2)}, u32[]{:S(2)}) collective-permute-start(bf16[384,640]{1,0:T(8,128)(2,1)} %get-tuple-element.103), channel_id=1, source_target_pairs={{0,1},{2,3},{4,6},{6,4},{8,11},{10,9},{12,12},{14,14},{17,17},{19,... | collective-permute-start | bytes 1474568 | tf_op jit(solution)/shard_map/sums_3/ppermute | solution.py:163
  94.9 14.5 %collective-permute-start.14 = (bf16[384,640]{1,0:T(8,128)(2,1)}, bf16[384,640]{1,0:T(8,128)(2,1)S(1)}, u32[]{:S(2)}, u32[]{:S(2)}) collective-permute-start(bf16[384,640]{1,0:T(8,128)(2,1)} %get-tuple-element.103), channel_id=1, source_target_pairs={{1,17},{3,19},{5,22},{7,20},{9,27},{11,25},{13,28},{15,30},{16,1},... | collective-permute-start | bytes 1474568 | tf_op jit(solution)/shard_map/sums_cross_3/ppermute | solution.py:163
  96.3 1.5 %copy-start.1 = (f32[384,1280]{1,0:T(8,128)S(1)}, f32[384,1280]{1,0:T(8,128)}, u32[]{:S(2)}) copy-start(f32[384,1280]{1,0:T(8,128)} %refs_6_.1) | copy-start | bytes 5898244

commit v7 on v6

--- a/solution.py
+++ b/solution.py
@@ -205,6 +205,7 @@
     tie = lax.optimization_barrier
 
     ring = pairs(lambda y, f, x, c: (y, (f + 1) % 4 if x == 0 else (f - 1) % 4, x, c))
+    back = [(target, source) for source, target in ring]
     sibling = pairs(lambda y, f, x, c: (y, f, x, 1 - c))
     here = y == c
     left = x == 0
@@ -268,7 +269,7 @@
     middle = to_owners(s1, (1, 1), "1")
     s0 = region(token, sums, rows_own, rows_sib, w0, v0)
     w2, s0 = tie((w2, s0))
-    w3 = send(w2, ring, "ring_3")
+    w3 = send(w0, back, "ring_after")
     low_sum, high_sum = region(token, mix, rows_own, rows_sib, s0, w2)
     low_sum, high_sum, *middle = tie((low_sum, high_sum, *middle))
     early = to_owners(low_sum, (0, 2), "02") + to_owners(high_sum, (2, 0), "20")

time: 112 us -> 110 us (0.982)
  waiting for transfers between devices: 41.4 us -> 39.4 us
    ppermute x17, waiting for transfers between devices: 21.2 us -> 19.3 us  [send(): return lax.ppermute(array, AXES, route)]
  transfers between devices with their start and end apart: 19 -> 19, of which waited for: 11 -> 11; matrix products, arithmetic and copies ran while one was open for 16% -> 17% of each run, Pallas kernels for 9% -> 9%
where the time goes in v7:
time: 110 us; the launch traced here: 108 us
  waiting for transfers between devices  39.4 us (36%)
  starting transfers between devices  33.4 us (30%)
  matrix products  15.7 us (14%)
  Pallas kernels  11.5 us (10%)
  local copies, waits for them, and re-layouts  5.42 us (5%)
  other arithmetic  1.58 us (1%)
    ppermute x17, starting transfers between devices, send(): return lax.ppermute(array, AXES, route)  27.4 us
    ppermute x17, waiting for transfers between devices, send(): return lax.ppermute(array, AXES, route)  19.3 us
    ppermute x1, waiting for transfers between devices, halos(): lax.ppermute(keyvals, 'frame', forward)  18.7 us
    dot_general x4, matrix products, sums(): total = total + jnp.dot(rows_sib, sib, preferred_element_type=jnp.float32)  8.06 us
    dot_general x4, matrix products, sums(): total = jnp.dot(rows_own, own, preferred_element_type=jnp.float32)  7.67 us
    pallas_call x1, Pallas kernels, attend(): pl.pallas_call(attend_kernel, out_shape=jax.ShapeDtypeStruct((rows, width...  7.66 us
    unnamed x14, local copies, waits for them, and re-layouts  4.44 us
    ppermute x1, starting transfers between devices, halos(): lax.ppermute(keyvals, 'frame', forward)  3.61 us
  transfers between devices with their start and end apart: 19, of which 11 were waited for; matrix products, arithmetic and copies ran while one was open for 17% of the time, Pallas kernels for 9%

profile of v7, /device:TPU:8, one launch (start us, length us, event | category | flops | bytes accessed | tf_op | source)
XLA Modules:
  0.0 108.0 jit_solution(16273803139030031181)
XLA Ops:
  0.0 3.6 %collective-permute-start.3 = (bf16[2,384,640]{2,1,0:T(8,128)(2,1)}, bf16[2,384,640]{2,1,0:T(8,128)(2,1)S(1)}, u32[]{:S(2)}, u32[]{:S(2)}) collective-permute-start(bf16[2,384,640]{2,1,0:T(8,128)(2,1)} %own_ref.1), channel_id=1, source_target_pairs={{0,4},{4,8},{8,12},{1,5},{5,9},{9,13},{2,6},{6,10},{10,14},{3,7},{... | collective-permute-start | bytes 2949128 | tf_op jit(solution)/shard_map/ppermute | solution.py:120
  3.6 2.4 %collective-permute-start.4 = (bf16[2,384,640]{2,1,0:T(8,128)(2,1)}, bf16[2,384,640]{2,1,0:T(8,128)(2,1)}, u32[]{:S(2)}, u32[]{:S(2)}) collective-permute-start(bf16[2,384,640]{2,1,0:T(8,128)(2,1)} %own_ref.1), channel_id=1, source_target_pairs={{4,0},{8,4},{12,8},{5,1},{9,5},{13,9},{6,2},{10,6},{14,10},{7,3},{... | collective-permute-start | bytes 2949128 | tf_op jit(solution)/shard_map/ppermute | solution.py:120
  6.1 1.0 constant_dynamic-slice_fusion
  7.0 18.7 %collective-permute-done.3.low_ref = bf16[2,384,640]{2,1,0:T(8,128)(2,1)S(1)} collective-permute-done((bf16[2,384,640]{2,1,0:T(8,128)(2,1)}, bf16[2,384,640]{2,1,0:T(8,128)(2,1)S(1)}, u32[]{:S(2)}, u32[]{:S(2)}) %collective-permute-start.3) | collective-permute-done | bytes 983072 | tf_op jit(solution)/shard_map/ppermute | solution.py:120
  25.7 1.6 %collective-permute-start.7 = (bf16[640,640]{1,0:T(8,128)(2,1)}, bf16[640,640]{1,0:T(8,128)(2,1)}, u32[]{:S(2)}, u32[]{:S(2)}) collective-permute-start(bf16[640,640]{1,0:T(8,128)(2,1)} %constant_dynamic-slice_fusion), channel_id=1, source_target_pairs={{0,4},{1,5},{2,14},{3,15},{4,8},{5,9},{6,2},{7,3},{8,12},{9,13},{1... | collective-permute-start | bytes 2457608 | tf_op jit(solution)/shard_map/ring_1/ppermute | solution.py:163
  27.3 0.7 subtract_clamp_fusion.ids
  28.0 1.5 %collective-permute-done.4.high_ref = bf16[2,384,640]{2,1,0:T(8,128)(2,1)} collective-permute-done((bf16[2,384,640]{2,1,0:T(8,128)(2,1)}, bf16[2,384,640]{2,1,0:T(8,128)(2,1)}, u32[]{:S(2)}, u32[]{:S(2)}) %collective-permute-start.4) | collective-permute-done | bytes 983072 | tf_op jit(solution)/shard_map/ppermute | solution.py:120
  29.5 1.2 %copy-done.2 = bf16[2,384,640]{2,1,0:T(8,128)(2,1)S(1)} copy-done((bf16[2,384,640]{2,1,0:T(8,128)(2,1)S(1)}, bf16[2,384,640]{2,1,0:T(8,128)(2,1)}, u32[]{:S(2)}) %copy-start.2) | copy-done | bytes 983064
  30.7 1.0 copy-done.3
  31.7 0.7 copy-done.4
  32.4 7.7 %attend.1 = bf16[384,640]{1,0:T(8,128)(2,1)S(1)} custom-call(s32[6,8]{1,0:T(8,128)S(1)} %subtract_clamp_fusion.ids, s32[6]{0:T(128)S(1)} %copy-done.4, bf16[384,640]{1,0:T(8,128)(2,1)S(1)} %copy-done.3, bf16[2,384,640]{2,1,0:T(8,128)(2,1)S(1)} %copy-done.2, bf16[2,384,640]{2,1,0:T(8,128)(2,1)S(1)} %collective-permute-done.3.low_ref, ...), custom_call_target="tpu_custom_call" | custom-call | flops 8000000000 | bytes 24000000 | tf_op jit(solution)/shard_map/attend/pallas_call | solution.py:101
  40.0 1.5 %collective-permute-start.5 = (bf16[384,640]{1,0:T(8,128)(2,1)S(1)}, bf16[384,640]{1,0:T(8,128)(2,1)S(1)}, u32[]{:S(2)}, u32[]{:S(2)}) collective-permute-start(bf16[384,640]{1,0:T(8,128)(2,1)S(1)} %attend.1), channel_id=1, source_target_pairs={{0,16},{1,0},{2,18},{3,2},{4,20},{5,4},{6,22},{7,6},{8,24},{9,8},{... | collective-permute-start | bytes 1474568 | tf_op jit(solution)/shard_map/rows_1/ppermute | solution.py:163
  41.6 0.7 collective-permute-start.6
  42.3 3.0 %collective-permute-done.7 = bf16[640,640]{1,0:T(8,128)(2,1)} collective-permute-done((bf16[640,640]{1,0:T(8,128)(2,1)}, bf16[640,640]{1,0:T(8,128)(2,1)}, u32[]{:S(2)}, u32[]{:S(2)}) %collective-permute-start.7) | collective-permute-done | bytes 819232 | tf_op jit(solution)/shard_map/ring_1/ppermute | solution.py:163
  45.3 1.6 %collective-permute-start.9 = (bf16[640,640]{1,0:T(8,128)(2,1)}, bf16[640,640]{1,0:T(8,128)(2,1)}, u32[]{:S(2)}, u32[]{:S(2)}) collective-permute-start(bf16[640,640]{1,0:T(8,128)(2,1)} %collective-permute-done.7), channel_id=1, source_target_pairs={{0,4},{1,5},{2,14},{3,15},{4,8},{5,9},{6,2},{7,3},{8,12},{9,13},{1... | collective-permute-start | bytes 2457608 | tf_op jit(solution)/shard_map/ring_2/ppermute | solution.py:163
  46.8 0.6 fence.1
  47.4 4.4 %collective-permute-done.5 = bf16[384,640]{1,0:T(8,128)(2,1)S(1)} collective-permute-done((bf16[384,640]{1,0:T(8,128)(2,1)S(1)}, bf16[384,640]{1,0:T(8,128)(2,1)S(1)}, u32[]{:S(2)}, u32[]{:S(2)}) %collective-permute-start.5) | collective-permute-done | bytes 491552 | tf_op jit(solution)/shard_map/rows_1/ppermute | solution.py:163
  52.5 0.9 broadcast_select_fusion.2
  53.4 5.0 %conditional.6 = (bf16[384,640]{1,0:T(8,128)(2,1)}) conditional(s32[]{:T(128)} %bitcast.1, () %tuple.46, (bf16[384,640]{1,0:T(8,128)(2,1)}, bf16[640,640]{1,0:T(8,128)(2,1)}, bf16[384,640]{1,0:T(8,128)(2,1)S(1)}) %tuple.47), branch_computations={%region_4.5_spmd, %region_5.6_spmd} | conditional | flops 629637120 | bytes 8355888 | solution.py:238
  53.4 1.5 %collective-permute-start.1 = (bf16[640,640]{1,0:T(8,128)(2,1)}, bf16[640,640]{1,0:T(8,128)(2,1)S(1)}, u32[]{:S(2)}, u32[]{:S(2)}) collective-permute-start(bf16[640,640]{1,0:T(8,128)(2,1)} %get-tuple-element.56), channel_id=1, source_target_pairs={{0,1},{1,0},{2,3},{3,2},{4,5},{5,4},{6,7},{7,6},{8,9},{9,8},{10,11... | collective-permute-start | bytes 2457608 | tf_op jit(solution)/shard_map/cond/branch_1_fun/core_swap/ppermute | solution.py:163
  54.9 1.9 %fusion.6 = f32[384,640]{1,0:T(8,128)S(1)} fusion(bf16[384,640]{1,0:T(8,128)(2,1)} %get-tuple-element.55, bf16[640,640]{1,0:T(8,128)(2,1)} %get-tuple-element.56), kind=kOutput, calls=%fused_computation.16 | convolution fusion | flops 314572800 | bytes 2293760 | tf_op jit(solution)/shard_map/cond/branch_1_fun/dot_general | solution.py:246
  57.1 1.4 %fusion.2 = bf16[384,640]{1,0:T(8,128)(2,1)} fusion(f32[384,640]{1,0:T(8,128)S(1)} %fusion.6, bf16[384,640]{1,0:T(8,128)(2,1)S(1)} %get-tuple-element.57, bf16[640,640]{1,0:T(8,128)(2,1)S(1)} %collective-permute-done.1), kind=kOutput, calls=%fused_computation.7 | convolution fusion | flops 315064320 | bytes 2785280 | tf_op jit(solution)/shard_map/cond/branch_1_fun/dot_general | solution.py:247
  58.4 1.7 %collective-permute-start.11 = (bf16[384,640]{1,0:T(8,128)(2,1)}, bf16[384,640]{1,0:T(8,128)(2,1)S(1)}, u32[]{:S(2)}, u32[]{:S(2)}) collective-permute-start(bf16[384,640]{1,0:T(8,128)(2,1)} %get-tuple-element.102), channel_id=1, source_target_pairs={{0,3},{2,1},{4,4},{6,6},{8,9},{10,11},{12,14},{14,12},{17,19},{19,... | collective-permute-start | bytes 1474568 | tf_op jit(solution)/shard_map/sums_1/ppermute | solution.py:163
  60.1 1.3 %collective-permute-start.12 = (bf16[384,640]{1,0:T(8,128)(2,1)}, bf16[384,640]{1,0:T(8,128)(2,1)S(1)}, u32[]{:S(2)}, u32[]{:S(2)}) collective-permute-start(bf16[384,640]{1,0:T(8,128)(2,1)} %get-tuple-element.102), channel_id=1, source_target_pairs={{1,19},{3,17},{5,20},{7,22},{9,25},{11,27},{13,30},{15,28},{16,3},... | collective-permute-start | bytes 1474568 | tf_op jit(solution)/shard_map/sums_cross_1/ppermute | solution.py:163
  61.4 2.7 %collective-permute-start.8 = (bf16[640,640]{1,0:T(8,128)(2,1)}, bf16[640,640]{1,0:T(8,128)(2,1)}, u32[]{:S(2)}, u32[]{:S(2)}) collective-permute-start(bf16[640,640]{1,0:T(8,128)(2,1)} %constant_dynamic-slice_fusion), channel_id=1, source_target_pairs={{4,0},{5,1},{14,2},{15,3},{8,4},{9,5},{2,6},{3,7},{12,8},{13,9},{6... | collective-permute-start | bytes 2457608 | tf_op jit(solution)/shard_map/ring_after/ppermute | solution.py:163
  64.1 4.5 %conditional.4 = (bf16[384,640]{1,0:T(8,128)(2,1)}) conditional(s32[]{:T(128)} %bitcast.1, () %tuple.42, (bf16[384,640]{1,0:T(8,128)(2,1)}, bf16[640,640]{1,0:T(8,128)(2,1)}, bf16[384,640]{1,0:T(8,128)(2,1)S(1)}, bf16[640,640]{1,0:T(8,128)(2,1)}) %tuple.43), branch_computations={%region_0.1_spmd, %region_1.2_spmd} | conditional | flops 629637120 | bytes 5079048 | solution.py:238
  64.1 1.9 %fusion.4 = f32[384,640]{1,0:T(8,128)S(1)} fusion(bf16[384,640]{1,0:T(8,128)(2,1)} %get-tuple-element.46, bf16[640,640]{1,0:T(8,128)(2,1)} %get-tuple-element.47), kind=kOutput, calls=%fused_computation.14 | convolution fusion | flops 314572800 | bytes 2293760 | tf_op jit(solution)/shard_map/cond/branch_1_fun/dot_general | solution.py:246
  66.0 2.5 %fusion = bf16[384,640]{1,0:T(8,128)(2,1)} fusion(f32[384,640]{1,0:T(8,128)S(1)} %fusion.4, bf16[384,640]{1,0:T(8,128)(2,1)S(1)} %get-tuple-element.48, bf16[640,640]{1,0:T(8,128)(2,1)} %get-tuple-element.49), kind=kOutput, calls=%fused_computation.1 | convolution fusion | flops 315064320 | bytes 2785280 | tf_op jit(solution)/shard_map/cond/branch_1_fun/dot_general | solution.py:247
  68.6 8.0 %conditional.5 = (bf16[384,640]{1,0:T(8,128)(2,1)}, bf16[384,640]{1,0:T(8,128)(2,1)}) conditional(s32[]{:T(128)} %bitcast.1, () %tuple.41, (s32[]{:T(128)}, bf16[384,640]{1,0:T(8,128)(2,1)}, bf16[640,640]{1,0:T(8,128)(2,1)}, bf16[384,640]{1,0:T(8,128)(2,1)S(1)}, bf16[384,640]{1,0:T(8,128)(2,1)}) %tuple.45), branch_computations={%region_2.3_spmd, %region_3.4_spmd} | conditional | flops 630128640 | bytes 11305054 | solution.py:238
  68.6 3.0 %collective-permute-start = (bf16[640,640]{1,0:T(8,128)(2,1)}, bf16[640,640]{1,0:T(8,128)(2,1)}, u32[]{:S(2)}, u32[]{:S(2)}) collective-permute-start(bf16[640,640]{1,0:T(8,128)(2,1)} %get-tuple-element.53), channel_id=1, source_target_pairs={{0,1},{1,0},{2,3},{3,2},{4,5},{5,4},{6,7},{7,6},{8,9},{9,8},{10,11... | collective-permute-start | bytes 2457608 | tf_op jit(solution)/shard_map/cond/branch_1_fun/core_swap/ppermute | solution.py:163
  71.6 1.9 %fusion.5 = f32[384,640]{1,0:T(8,128)S(1)} fusion(bf16[384,640]{1,0:T(8,128)(2,1)} %get-tuple-element.52, bf16[640,640]{1,0:T(8,128)(2,1)} %get-tuple-element.53), kind=kOutput, calls=%fused_computation.15 | convolution fusion | flops 314572800 | bytes 2293760 | tf_op jit(solution)/shard_map/cond/branch_1_fun/dot_general | solution.py:246
  73.9 2.7 %broadcast_select_fusion = (bf16[384,640]{1,0:T(8,128)(2,1)}, bf16[384,640]{1,0:T(8,128)(2,1)}) fusion(bf16[384,640]{1,0:T(8,128)(2,1)S(1)} %copy-done.7, pred[]{:T(512)S(6)} %eq.5, f32[384,640]{1,0:T(8,128)S(1)} %fusion.5, bf16[384,640]{1,0:T(8,128)(2,1)S(1)} %get-tuple-element.54, bf16[640,640]{1,0:T(8,128)(2,1)} %collective-permute-done), kind=kOutput, calls=%fused_computation.4 | convolution fusion | flops 315555840 | bytes 3768321 | tf_op jit(solution)/shard_map/cond/branch_1_fun/dot_general | solution.py:247
  76.6 2.3 %collective-permute-start.15 = (bf16[384,640]{1,0:T(8,128)(2,1)}, bf16[384,640]{1,0:T(8,128)(2,1)S(1)}, u32[]{:S(2)}, u32[]{:S(2)}) collective-permute-start(bf16[384,640]{1,0:T(8,128)(2,1)} %get-tuple-element.88), channel_id=1, source_target_pairs={{0,0},{2,2},{4,5},{6,7},{8,10},{10,8},{12,15},{14,13},{17,16},{19,... | collective-permute-start | bytes 1474568 | tf_op jit(solution)/shard_map/sums_02/ppermute | solution.py:163
  78.9 1.5 %collective-permute-start.17 = (bf16[384,640]{1,0:T(8,128)(2,1)}, bf16[384,640]{1,0:T(8,128)(2,1)}, u32[]{:S(2)}, u32[]{:S(2)}) collective-permute-start(bf16[384,640]{1,0:T(8,128)(2,1)} %get-tuple-element.88), channel_id=1, source_target_pairs={{1,16},{3,18},{5,21},{7,23},{9,26},{11,24},{13,31},{15,29},{16,0},... | collective-permute-start | bytes 1474568 | tf_op jit(solution)/shard_map/sums_cross_02/ppermute | solution.py:163
  80.4 3.3 %collective-permute-start.16 = (bf16[384,640]{1,0:T(8,128)(2,1)}, bf16[384,640]{1,0:T(8,128)(2,1)}, u32[]{:S(2)}, u32[]{:S(2)}) collective-permute-start(bf16[384,640]{1,0:T(8,128)(2,1)} %get-tuple-element.89), channel_id=1, source_target_pairs={{0,2},{2,0},{4,7},{6,5},{8,8},{10,10},{12,13},{14,15},{17,18},{19,... | collective-permute-start | bytes 1474568 | tf_op jit(solution)/shard_map/sums_20/ppermute | solution.py:163
  83.7 1.5 %collective-permute-start.18 = (bf16[384,640]{1,0:T(8,128)(2,1)}, bf16[384,640]{1,0:T(8,128)(2,1)}, u32[]{:S(2)}, u32[]{:S(2)}) collective-permute-start(bf16[384,640]{1,0:T(8,128)(2,1)} %get-tuple-element.89), channel_id=1, source_target_pairs={{1,18},{3,16},{5,23},{7,21},{9,24},{11,26},{13,29},{15,31},{16,2},... | collective-permute-start | bytes 1474568 | tf_op jit(solution)/shard_map/sums_cross_20/ppermute | solution.py:163
  85.2 0.8 collective-permute-done.8
  86.0 3.9 %conditional.7 = (bf16[384,640]{1,0:T(8,128)(2,1)}) conditional(s32[]{:T(128)} %bitcast.1, () %tuple.40, (bf16[384,640]{1,0:T(8,128)(2,1)}, bf16[640,640]{1,0:T(8,128)(2,1)}, bf16[384,640]{1,0:T(8,128)(2,1)}) %tuple.61), branch_computations={%region_6.7_spmd, %region_7.8_spmd} | conditional | flops 629637120 | bytes 10321996 | solution.py:238
  86.1 1.9 %fusion.7 = f32[384,640]{1,0:T(8,128)S(1)} fusion(bf16[384,640]{1,0:T(8,128)(2,1)} %get-tuple-element.58, bf16[640,640]{1,0:T(8,128)(2,1)} %get-tuple-element.59), kind=kOutput, calls=%fused_computation.17 | convolution fusion | flops 314572800 | bytes 2293760 | tf_op jit(solution)/shard_map/cond/branch_1_fun/dot_general | solution.py:246
  88.5 1.4 %fusion.3 = bf16[384,640]{1,0:T(8,128)(2,1)} fusion(f32[384,640]{1,0:T(8,128)S(1)} %fusion.7, bf16[384,640]{1,0:T(8,128)(2,1)S(1)} %copy-done.6, bf16[640,640]{1,0:T(8,128)(2,1)S(1)} %collective-permute-done.2), kind=kOutput, calls=%fused_computation.9 | convolution fusion | flops 315064320 | bytes 2785280 | tf_op jit(solution)/shard_map/cond/branch_1_fun/dot_general | solution.py:247
  89.9 2.0 %collective-permute-start.13 = (bf16[384,640]{1,0:T(8,128)(2,1)}, bf16[384,640]{1,0:T(8,128)(2,1)S(1)}, u32[]{:S(2)}, u32[]{:S(2)}) collective-permute-start(bf16[384,640]{1,0:T(8,128)(2,1)} %get-tuple-element.103), channel_id=1, source_target_pairs={{0,1},{2,3},{4,6},{6,4},{8,11},{10,9},{12,12},{14,14},{17,17},{19,... | collective-permute-start | bytes 1474568 | tf_op jit(solution)/shard_map/sums_3/ppermute | solution.py:163
  91.9 1.3 %collective-permute-start.14 = (bf16[384,640]{1,0:T(8,128)(2,1)}, bf16[384,640]{1,0:T(8,128)(2,1)S(1)}, u32[]{:S(2)}, u32[]{:S(2)}) collective-permute-start(bf16[384,640]{1,0:T(8,128)(2,1)} %get-tuple-element.103), channel_id=1, source_target_pairs={{1,17},{3,19},{5,22},{7,20},{9,27},{11,25},{13,28},{15,30},{16,1},... | collective-permute-start | bytes 1474568 | tf_op jit(solution)/shard_map/sums_cross_3/ppermute | solution.py:163
  93.2 0.6 collective-permute-done.16.refs_2_
  93.8 1.5 %copy-done.1 = f32[384,1280]{1,0:T(8,128)S(1)} copy-done((f32[384,1280]{1,0:T(8,128)S(1)}, f32[384,1280]{1,0:T(8,128)}, u32[]{:S(2)}) %copy-start.1) | copy-done | bytes 1966104
  95.3 1.9 %finish.2.refs_2_ = f32[384,1280]{1,0:T(8,128)S(1)} custom-call(s32[1]{0:T(128)} %bitcast.spot, bf16[384,640]{1,0:T(8,128)(2,1)S(1)} %collective-permute-done.11.refs_0_, bf16[384,640]{1,0:T(8,128)(2,1)S(1)} %collective-permute-done.15.refs_1_, bf16[384,640]{1,0:T(8,128)(2,1)} %collective-permute-done.16.refs_2_, ...), custom_call_target="tpu_custom_call" | custom-call | tf_op jit(solution)/shard_map/finish/pallas_call | solution.py:187
  97.2 8.0 %collective-permute-done.13.refs_0_ = bf16[384,640]{1,0:T(8,128)(2,1)S(1)} collective-permute-done((bf16[384,640]{1,0:T(8,128)(2,1)}, bf16[384,640]{1,0:T(8,128)(2,1)S(1)}, u32[]{:S(2)}, u32[]{:S(2)}) %collective-permute-start.13) | collective-permute-done | bytes 491552 | tf_op jit(solution)/shard_map/sums_3/ppermute | solution.py:163
  105.2 1.4 %collective-permute-done.14.refs_1_ = bf16[384,640]{1,0:T(8,128)(2,1)S(1)} collective-permute-done((bf16[384,640]{1,0:T(8,128)(2,1)}, bf16[384,640]{1,0:T(8,128)(2,1)S(1)}, u32[]{:S(2)}, u32[]{:S(2)}) %collective-permute-start.14) | collective-permute-done | bytes 491552 | tf_op jit(solution)/shard_map/sums_cross_3/ppermute | solution.py:163
  106.6 1.4 %finish.3 = f32[384,1280]{1,0:T(8,128)} custom-call(s32[1]{0:T(128)} %bitcast.spot, bf16[384,640]{1,0:T(8,128)(2,1)S(1)} %collective-permute-done.13.refs_0_, bf16[384,640]{1,0:T(8,128)(2,1)S(1)} %collective-permute-done.14.refs_1_, f32[384,1280]{1,0:T(8,128)S(1)} %finish.2.refs_2_, f32[1,1280]{1,0:T(1,128)S(1)} %broadcast_in_dim.4.refs_7_.refs_3_), custom_call_target="tpu_custom_call" | custom-call | tf_op jit(solution)/shard_map/finish/pallas_call | solution.py:187
  (28 shorter events, 1.3 us)
Async XLA Ops:
  0.0 6.1 %copy-start = (bf16[640,1280]{1,0:T(8,128)(2,1)S(1)}, bf16[640,1280]{1,0:T(8,128)(2,1)}, u32[]{:S(2)}) copy-start(bf16[640,1280]{1,0:T(8,128)(2,1)} %param.19) | copy-start | bytes 4915204
  0.0 25.7 %collective-permute-start.3 = (bf16[2,384,640]{2,1,0:T(8,128)(2,1)}, bf16[2,384,640]{2,1,0:T(8,128)(2,1)S(1)}, u32[]{:S(2)}, u32[]{:S(2)}) collective-permute-start(bf16[2,384,640]{2,1,0:T(8,128)(2,1)} %own_ref.1), channel_id=1, source_target_pairs={{0,4},{4,8},{8,12},{1,5},{5,9},{9,13},{2,6},{6,10},{10,14},{3,7},{... | collective-permute-start | bytes 2949128 | tf_op jit(solution)/shard_map/ppermute | solution.py:120
  3.6 25.9 %collective-permute-start.4 = (bf16[2,384,640]{2,1,0:T(8,128)(2,1)}, bf16[2,384,640]{2,1,0:T(8,128)(2,1)}, u32[]{:S(2)}, u32[]{:S(2)}) collective-permute-start(bf16[2,384,640]{2,1,0:T(8,128)(2,1)} %own_ref.1), channel_id=1, source_target_pairs={{4,0},{8,4},{12,8},{5,1},{9,5},{13,9},{6,2},{10,6},{14,10},{7,3},{... | collective-permute-start | bytes 2949128 | tf_op jit(solution)/shard_map/ppermute | solution.py:120
  7.0 57.1 %collective-permute-start.10 = (bf16[640,640]{1,0:T(8,128)(2,1)}, bf16[640,640]{1,0:T(8,128)(2,1)}, u32[]{:S(2)}, u32[]{:S(2)}) collective-permute-start(bf16[640,640]{1,0:T(8,128)(2,1)} %constant_dynamic-slice_fusion), channel_id=1, source_target_pairs={{0,1},{1,0},{2,3},{3,2},{4,5},{5,4},{6,7},{7,6},{8,9},{9,8},{10,11... | collective-permute-start | bytes 2457608 | tf_op jit(solution)/shard_map/core_swap_0/ppermute | solution.py:163
  25.7 19.5 %collective-permute-start.7 = (bf16[640,640]{1,0:T(8,128)(2,1)}, bf16[640,640]{1,0:T(8,128)(2,1)}, u32[]{:S(2)}, u32[]{:S(2)}) collective-permute-start(bf16[640,640]{1,0:T(8,128)(2,1)} %constant_dynamic-slice_fusion), channel_id=1, source_target_pairs={{0,4},{1,5},{2,14},{3,15},{4,8},{5,9},{6,2},{7,3},{8,12},{9,13},{1... | collective-permute-start | bytes 2457608 | tf_op jit(solution)/shard_map/ring_1/ppermute | solution.py:163
  29.5 1.2 %copy-start.2 = (bf16[2,384,640]{2,1,0:T(8,128)(2,1)S(1)}, bf16[2,384,640]{2,1,0:T(8,128)(2,1)}, u32[]{:S(2)}) copy-start(bf16[2,384,640]{2,1,0:T(8,128)(2,1)} %own_ref.1) | copy-start | bytes 2949124
  30.7 1.0 copy-start.3
  31.7 0.7 copy-start.4
  40.0 11.8 %collective-permute-start.5 = (bf16[384,640]{1,0:T(8,128)(2,1)S(1)}, bf16[384,640]{1,0:T(8,128)(2,1)S(1)}, u32[]{:S(2)}, u32[]{:S(2)}) collective-permute-start(bf16[384,640]{1,0:T(8,128)(2,1)S(1)} %attend.1), channel_id=1, source_target_pairs={{0,16},{1,0},{2,18},{3,2},{4,20},{5,4},{6,22},{7,6},{8,24},{9,8},{... | collective-permute-start | bytes 1474568 | tf_op jit(solution)/shard_map/rows_1/ppermute | solution.py:163
  41.6 10.2 %collective-permute-start.6 = (bf16[384,640]{1,0:T(8,128)(2,1)S(1)}, bf16[384,640]{1,0:T(8,128)(2,1)S(1)}, u32[]{:S(2)}, u32[]{:S(2)}) collective-permute-start(bf16[384,640]{1,0:T(8,128)(2,1)S(1)} %attend.1), channel_id=1, source_target_pairs={{1,16},{3,18},{5,20},{7,22},{9,24},{11,26},{13,28},{15,30},{16,1},... | collective-permute-start | bytes 1474568 | tf_op jit(solution)/shard_map/rows_2/ppermute | solution.py:163
  45.3 23.3 %collective-permute-start.9 = (bf16[640,640]{1,0:T(8,128)(2,1)}, bf16[640,640]{1,0:T(8,128)(2,1)}, u32[]{:S(2)}, u32[]{:S(2)}) collective-permute-start(bf16[640,640]{1,0:T(8,128)(2,1)} %collective-permute-done.7), channel_id=1, source_target_pairs={{0,4},{1,5},{2,14},{3,15},{4,8},{5,9},{6,2},{7,3},{8,12},{9,13},{1... | collective-permute-start | bytes 2457608 | tf_op jit(solution)/shard_map/ring_2/ppermute | solution.py:163
  53.4 15.2 %copy-start.5 = (bf16[384,640]{1,0:T(8,128)(2,1)}, bf16[384,640]{1,0:T(8,128)(2,1)S(1)}, u32[]{:S(2)}) copy-start(bf16[384,640]{1,0:T(8,128)(2,1)S(1)} %get-tuple-element.95) | copy-start | bytes 1474564
  53.4 3.7 %collective-permute-start.1 = (bf16[640,640]{1,0:T(8,128)(2,1)}, bf16[640,640]{1,0:T(8,128)(2,1)S(1)}, u32[]{:S(2)}, u32[]{:S(2)}) collective-permute-start(bf16[640,640]{1,0:T(8,128)(2,1)} %get-tuple-element.56), channel_id=1, source_target_pairs={{0,1},{1,0},{2,3},{3,2},{4,5},{5,4},{6,7},{7,6},{8,9},{9,8},{10,11... | collective-permute-start | bytes 2457608 | tf_op jit(solution)/shard_map/cond/branch_1_fun/core_swap/ppermute | solution.py:163
  58.4 18.2 %collective-permute-start.11 = (bf16[384,640]{1,0:T(8,128)(2,1)}, bf16[384,640]{1,0:T(8,128)(2,1)S(1)}, u32[]{:S(2)}, u32[]{:S(2)}) collective-permute-start(bf16[384,640]{1,0:T(8,128)(2,1)} %get-tuple-element.102), channel_id=1, source_target_pairs={{0,3},{2,1},{4,4},{6,6},{8,9},{10,11},{12,14},{14,12},{17,19},{19,... | collective-permute-start | bytes 1474568 | tf_op jit(solution)/shard_map/sums_1/ppermute | solution.py:163
  60.1 16.5 %collective-permute-start.12 = (bf16[384,640]{1,0:T(8,128)(2,1)}, bf16[384,640]{1,0:T(8,128)(2,1)S(1)}, u32[]{:S(2)}, u32[]{:S(2)}) collective-permute-start(bf16[384,640]{1,0:T(8,128)(2,1)} %get-tuple-element.102), channel_id=1, source_target_pairs={{1,19},{3,17},{5,20},{7,22},{9,25},{11,27},{13,30},{15,28},{16,3},... | collective-permute-start | bytes 1474568 | tf_op jit(solution)/shard_map/sums_cross_1/ppermute | solution.py:163
  61.4 24.6 %collective-permute-start.8 = (bf16[640,640]{1,0:T(8,128)(2,1)}, bf16[640,640]{1,0:T(8,128)(2,1)}, u32[]{:S(2)}, u32[]{:S(2)}) collective-permute-start(bf16[640,640]{1,0:T(8,128)(2,1)} %constant_dynamic-slice_fusion), channel_id=1, source_target_pairs={{4,0},{5,1},{14,2},{15,3},{8,4},{9,5},{2,6},{3,7},{12,8},{13,9},{6... | collective-permute-start | bytes 2457608 | tf_op jit(solution)/shard_map/ring_after/ppermute | solution.py:163
  68.6 5.3 %collective-permute-start = (bf16[640,640]{1,0:T(8,128)(2,1)}, bf16[640,640]{1,0:T(8,128)(2,1)}, u32[]{:S(2)}, u32[]{:S(2)}) collective-permute-start(bf16[640,640]{1,0:T(8,128)(2,1)} %get-tuple-element.53), channel_id=1, source_target_pairs={{0,1},{1,0},{2,3},{3,2},{4,5},{5,4},{6,7},{7,6},{8,9},{9,8},{10,11... | collective-permute-start | bytes 2457608 | tf_op jit(solution)/shard_map/cond/branch_1_fun/core_swap/ppermute | solution.py:163
  71.6 2.3 %copy-start.7 = (bf16[384,640]{1,0:T(8,128)(2,1)S(1)}, bf16[384,640]{1,0:T(8,128)(2,1)}, u32[]{:S(2)}) copy-start(bf16[384,640]{1,0:T(8,128)(2,1)} %get-tuple-element.51) | copy-start | bytes 1474564 | tf_op jit(solution)/shard_map/cond
  76.6 15.2 %collective-permute-start.15 = (bf16[384,640]{1,0:T(8,128)(2,1)}, bf16[384,640]{1,0:T(8,128)(2,1)S(1)}, u32[]{:S(2)}, u32[]{:S(2)}) collective-permute-start(bf16[384,640]{1,0:T(8,128)(2,1)} %get-tuple-element.88), channel_id=1, source_target_pairs={{0,0},{2,2},{4,5},{6,7},{8,10},{10,8},{12,15},{14,13},{17,16},{19,... | collective-permute-start | bytes 1474568 | tf_op jit(solution)/shard_map/sums_02/ppermute | solution.py:163
  78.9 14.8 %collective-permute-start.17 = (bf16[384,640]{1,0:T(8,128)(2,1)}, bf16[384,640]{1,0:T(8,128)(2,1)}, u32[]{:S(2)}, u32[]{:S(2)}) collective-permute-start(bf16[384,640]{1,0:T(8,128)(2,1)} %get-tuple-element.88), channel_id=1, source_target_pairs={{1,16},{3,18},{5,21},{7,23},{9,26},{11,24},{13,31},{15,29},{16,0},... | collective-permute-start | bytes 1474568 | tf_op jit(solution)/shard_map/sums_cross_02/ppermute | solution.py:163
  80.4 13.4 %collective-permute-start.16 = (bf16[384,640]{1,0:T(8,128)(2,1)}, bf16[384,640]{1,0:T(8,128)(2,1)}, u32[]{:S(2)}, u32[]{:S(2)}) collective-permute-start(bf16[384,640]{1,0:T(8,128)(2,1)} %get-tuple-element.89), channel_id=1, source_target_pairs={{0,2},{2,0},{4,7},{6,5},{8,8},{10,10},{12,13},{14,15},{17,18},{19,... | collective-permute-start | bytes 1474568 | tf_op jit(solution)/shard_map/sums_20/ppermute | solution.py:163
  83.7 10.1 %collective-permute-start.18 = (bf16[384,640]{1,0:T(8,128)(2,1)}, bf16[384,640]{1,0:T(8,128)(2,1)}, u32[]{:S(2)}, u32[]{:S(2)}) collective-permute-start(bf16[384,640]{1,0:T(8,128)(2,1)} %get-tuple-element.89), channel_id=1, source_target_pairs={{1,18},{3,16},{5,23},{7,21},{9,24},{11,26},{13,29},{15,31},{16,2},... | collective-permute-start | bytes 1474568 | tf_op jit(solution)/shard_map/sums_cross_20/ppermute | solution.py:163
  86.0 7.2 %copy-start.8 = (f32[1280]{0:T(1024)S(1)}, f32[1280]{0:T(1024)}, u32[]{:S(2)}) copy-start(f32[1280]{0:T(1024)} %param.18) | copy-start | bytes 15364
  86.0 2.5 %copy-start.6 = (bf16[384,640]{1,0:T(8,128)(2,1)S(1)}, bf16[384,640]{1,0:T(8,128)(2,1)}, u32[]{:S(2)}) copy-start(bf16[384,640]{1,0:T(8,128)(2,1)} %get-tuple-element.60) | copy-start | bytes 1474564 | tf_op jit(solution)/shard_map/cond
  86.0 2.5 %collective-permute-start.2 = (bf16[640,640]{1,0:T(8,128)(2,1)}, bf16[640,640]{1,0:T(8,128)(2,1)S(1)}, u32[]{:S(2)}, u32[]{:S(2)}) collective-permute-start(bf16[640,640]{1,0:T(8,128)(2,1)} %get-tuple-element.59), channel_id=1, source_target_pairs={{0,1},{1,0},{2,3},{3,2},{4,5},{5,4},{6,7},{7,6},{8,9},{9,8},{10,11... | collective-permute-start | bytes 2457608 | tf_op jit(solution)/shard_map/cond/branch_1_fun/core_swap/ppermute | solution.py:163
  89.9 15.3 %collective-permute-start.13 = (bf16[384,640]{1,0:T(8,128)(2,1)}, bf16[384,640]{1,0:T(8,128)(2,1)S(1)}, u32[]{:S(2)}, u32[]{:S(2)}) collective-permute-start(bf16[384,640]{1,0:T(8,128)(2,1)} %get-tuple-element.103), channel_id=1, source_target_pairs={{0,1},{2,3},{4,6},{6,4},{8,11},{10,9},{12,12},{14,14},{17,17},{19,... | collective-permute-start | bytes 1474568 | tf_op jit(solution)/shard_map/sums_3/ppermute | solution.py:163
  91.9 14.7 %collective-permute-start.14 = (bf16[384,640]{1,0:T(8,128)(2,1)}, bf16[384,640]{1,0:T(8,128)(2,1)S(1)}, u32[]{:S(2)}, u32[]{:S(2)}) collective-permute-start(bf16[384,640]{1,0:T(8,128)(2,1)} %get-tuple-element.103), channel_id=1, source_target_pairs={{1,17},{3,19},{5,22},{7,20},{9,27},{11,25},{13,28},{15,30},{16,1},... | collective-permute-start | bytes 1474568 | tf_op jit(solution)/shard_map/sums_cross_3/ppermute | solution.py:163
  93.8 1.5 %copy-start.1 = (f32[384,1280]{1,0:T(8,128)S(1)}, f32[384,1280]{1,0:T(8,128)}, u32[]{:S(2)}) copy-start(f32[384,1280]{1,0:T(8,128)} %refs_6_.1) | copy-start | bytes 5898244

commit v8 on v7

--- a/solution.py
+++ b/solution.py
@@ -253,8 +253,10 @@
     def begin(rows_own, rows_sib, w1):
         return sums(rows_own, rows_sib, w1, swapped(w1))
 
-    def mix(rows_own, rows_sib, s0, w2):
-        s2 = sums(rows_own, rows_sib, w2, swapped(w2))
+    def mix(rows_own, rows_sib, w0, v0, w2):
+        v2 = swapped(w2)
+        s0 = sums(rows_own, rows_sib, w0, v0)
+        s2 = sums(rows_own, rows_sib, w2, v2)
         return jnp.where(left, s0, s2), jnp.where(left, s2, s0)
 
     def end(rows_own, rows_sib, w3):
@@ -267,10 +269,9 @@
     rows_sib = jnp.where(here, first, second)
     s1 = region(token, begin, rows_own, rows_sib, w1)
     middle = to_owners(s1, (1, 1), "1")
-    s0 = region(token, sums, rows_own, rows_sib, w0, v0)
-    w2, s0 = tie((w2, s0))
+    w2, s1 = tie((w2, s1))
     w3 = send(w0, back, "ring_after")
-    low_sum, high_sum = region(token, mix, rows_own, rows_sib, s0, w2)
+    low_sum, high_sum = region(token, mix, rows_own, rows_sib, w0, v0, w2)
     low_sum, high_sum, *middle = tie((low_sum, high_sum, *middle))
     early = to_owners(low_sum, (0, 2), "02") + to_owners(high_sum, (2, 0), "20")
     w3, low_sum, high_sum = tie((w3, low_sum, high_sum))

time: 110 us -> 109 us (level)
  waiting for transfers between devices: 39.4 us -> 41.8 us
  starting transfers between devices: 33.4 us -> 31.9 us
    ppermute x17, waiting for transfers between devices: 19.3 us -> 21.6 us  [send(): return lax.ppermute(array, AXES, route)]
    ppermute x17, starting transfers between devices: 27.4 us -> 25.9 us  [send(): return lax.ppermute(array, AXES, route)]
  transfers between devices with their start and end apart: 19 -> 19, of which waited for: 11 -> 11; matrix products, arithmetic and copies ran while one was open for 17% -> 16% of each run, Pallas kernels for 9% -> 9%
where the time goes in v8:
time: 109 us; the launch traced here: 108 us
  waiting for transfers between devices  41.8 us (38%)
  starting transfers between devices  31.9 us (29%)
  matrix products  14.9 us (14%)
  Pallas kernels  11.5 us (11%)
  local copies, waits for them, and re-layouts  5.42 us (5%)
  other arithmetic  1.57 us (1%)
    ppermute x17, starting transfers between devices, send(): return lax.ppermute(array, AXES, route)  25.9 us
    ppermute x17, waiting for transfers between devices, send(): return lax.ppermute(array, AXES, route)  21.6 us
    ppermute x1, waiting for transfers between devices, halos(): lax.ppermute(keyvals, 'frame', forward)  18.7 us
    pallas_call x1, Pallas kernels, attend(): pl.pallas_call(attend_kernel, out_shape=jax.ShapeDtypeStruct((rows, width...  7.66 us
    dot_general x4, matrix products, sums(): total = jnp.dot(rows_own, own, preferred_element_type=jnp.float32)  7.62 us
    dot_general x4, matrix products, sums(): total = total + jnp.dot(rows_sib, sib, preferred_element_type=jnp.float32)  7.27 us
    unnamed x14, local copies, waits for them, and re-layouts  4.44 us
    ppermute x1, starting transfers between devices, halos(): lax.ppermute(keyvals, 'frame', forward)  3.61 us
  transfers between devices with their start and end apart: 19, of which 11 were waited for; matrix products, arithmetic and copies ran while one was open for 16% of the time, Pallas kernels for 9%

profile of v8, /device:TPU:8, one launch (start us, length us, event | category | flops | bytes accessed | tf_op | source)
XLA Modules:
  0.0 108.0 jit_solution(11167455747812093069)
XLA Ops:
  0.0 3.6 %collective-permute-start.3 = (bf16[2,384,640]{2,1,0:T(8,128)(2,1)}, bf16[2,384,640]{2,1,0:T(8,128)(2,1)S(1)}, u32[]{:S(2)}, u32[]{:S(2)}) collective-permute-start(bf16[2,384,640]{2,1,0:T(8,128)(2,1)} %own_ref.1), channel_id=1, source_target_pairs={{0,4},{4,8},{8,12},{1,5},{5,9},{9,13},{2,6},{6,10},{10,14},{3,7},{... | collective-permute-start | bytes 2949128 | tf_op jit(solution)/shard_map/ppermute | solution.py:120
  3.6 2.4 %collective-permute-start.4 = (bf16[2,384,640]{2,1,0:T(8,128)(2,1)}, bf16[2,384,640]{2,1,0:T(8,128)(2,1)}, u32[]{:S(2)}, u32[]{:S(2)}) collective-permute-start(bf16[2,384,640]{2,1,0:T(8,128)(2,1)} %own_ref.1), channel_id=1, source_target_pairs={{4,0},{8,4},{12,8},{5,1},{9,5},{13,9},{6,2},{10,6},{14,10},{7,3},{... | collective-permute-start | bytes 2949128 | tf_op jit(solution)/shard_map/ppermute | solution.py:120
  6.1 1.0 constant_dynamic-slice_fusion
  7.0 18.7 %collective-permute-done.3.low_ref = bf16[2,384,640]{2,1,0:T(8,128)(2,1)S(1)} collective-permute-done((bf16[2,384,640]{2,1,0:T(8,128)(2,1)}, bf16[2,384,640]{2,1,0:T(8,128)(2,1)S(1)}, u32[]{:S(2)}, u32[]{:S(2)}) %collective-permute-start.3) | collective-permute-done | bytes 983072 | tf_op jit(solution)/shard_map/ppermute | solution.py:120
  25.7 1.6 %collective-permute-start.7 = (bf16[640,640]{1,0:T(8,128)(2,1)}, bf16[640,640]{1,0:T(8,128)(2,1)}, u32[]{:S(2)}, u32[]{:S(2)}) collective-permute-start(bf16[640,640]{1,0:T(8,128)(2,1)} %constant_dynamic-slice_fusion), channel_id=1, source_target_pairs={{0,4},{1,5},{2,14},{3,15},{4,8},{5,9},{6,2},{7,3},{8,12},{9,13},{1... | collective-permute-start | bytes 2457608 | tf_op jit(solution)/shard_map/ring_1/ppermute | solution.py:163
  27.3 0.7 subtract_clamp_fusion.ids
  28.0 1.5 %collective-permute-done.4.high_ref = bf16[2,384,640]{2,1,0:T(8,128)(2,1)} collective-permute-done((bf16[2,384,640]{2,1,0:T(8,128)(2,1)}, bf16[2,384,640]{2,1,0:T(8,128)(2,1)}, u32[]{:S(2)}, u32[]{:S(2)}) %collective-permute-start.4) | collective-permute-done | bytes 983072 | tf_op jit(solution)/shard_map/ppermute | solution.py:120
  29.5 1.2 %copy-done.2 = bf16[2,384,640]{2,1,0:T(8,128)(2,1)S(1)} copy-done((bf16[2,384,640]{2,1,0:T(8,128)(2,1)S(1)}, bf16[2,384,640]{2,1,0:T(8,128)(2,1)}, u32[]{:S(2)}) %copy-start.2) | copy-done | bytes 983064
  30.7 1.0 copy-done.3
  31.7 0.7 copy-done.4
  32.4 7.7 %attend.1 = bf16[384,640]{1,0:T(8,128)(2,1)S(1)} custom-call(s32[6,8]{1,0:T(8,128)S(1)} %subtract_clamp_fusion.ids, s32[6]{0:T(128)S(1)} %copy-done.4, bf16[384,640]{1,0:T(8,128)(2,1)S(1)} %copy-done.3, bf16[2,384,640]{2,1,0:T(8,128)(2,1)S(1)} %copy-done.2, bf16[2,384,640]{2,1,0:T(8,128)(2,1)S(1)} %collective-permute-done.3.low_ref, ...), custom_call_target="tpu_custom_call" | custom-call | flops 8000000000 | bytes 24000000 | tf_op jit(solution)/shard_map/attend/pallas_call | solution.py:101
  40.0 1.5 %collective-permute-start.5 = (bf16[384,640]{1,0:T(8,128)(2,1)S(1)}, bf16[384,640]{1,0:T(8,128)(2,1)S(1)}, u32[]{:S(2)}, u32[]{:S(2)}) collective-permute-start(bf16[384,640]{1,0:T(8,128)(2,1)S(1)} %attend.1), channel_id=1, source_target_pairs={{0,16},{1,0},{2,18},{3,2},{4,20},{5,4},{6,22},{7,6},{8,24},{9,8},{... | collective-permute-start | bytes 1474568 | tf_op jit(solution)/shard_map/rows_1/ppermute | solution.py:163
  41.6 0.7 collective-permute-start.6
  42.3 3.0 %collective-permute-done.7 = bf16[640,640]{1,0:T(8,128)(2,1)} collective-permute-done((bf16[640,640]{1,0:T(8,128)(2,1)}, bf16[640,640]{1,0:T(8,128)(2,1)}, u32[]{:S(2)}, u32[]{:S(2)}) %collective-permute-start.7) | collective-permute-done | bytes 819232 | tf_op jit(solution)/shard_map/ring_1/ppermute | solution.py:163
  45.3 1.6 %collective-permute-start.10 = (bf16[640,640]{1,0:T(8,128)(2,1)}, bf16[640,640]{1,0:T(8,128)(2,1)}, u32[]{:S(2)}, u32[]{:S(2)}) collective-permute-start(bf16[640,640]{1,0:T(8,128)(2,1)} %collective-permute-done.7), channel_id=1, source_target_pairs={{0,4},{1,5},{2,14},{3,15},{4,8},{5,9},{6,2},{7,3},{8,12},{9,13},{1... | collective-permute-start | bytes 2457608 | tf_op jit(solution)/shard_map/ring_2/ppermute | solution.py:163
  46.8 0.6 fence.1
  47.4 4.4 %collective-permute-done.5 = bf16[384,640]{1,0:T(8,128)(2,1)S(1)} collective-permute-done((bf16[384,640]{1,0:T(8,128)(2,1)S(1)}, bf16[384,640]{1,0:T(8,128)(2,1)S(1)}, u32[]{:S(2)}, u32[]{:S(2)}) %collective-permute-start.5) | collective-permute-done | bytes 491552 | tf_op jit(solution)/shard_map/rows_1/ppermute | solution.py:163
  52.5 0.9 broadcast_select_fusion.2
  53.3 5.0 %conditional.3 = (bf16[384,640]{1,0:T(8,128)(2,1)}) conditional(s32[]{:T(128)} %bitcast.1, () %tuple.36, (bf16[384,640]{1,0:T(8,128)(2,1)}, bf16[640,640]{1,0:T(8,128)(2,1)}, bf16[384,640]{1,0:T(8,128)(2,1)S(1)}) %tuple.37), branch_computations={%region_0.1_spmd, %region_1.2_spmd} | conditional | flops 629637120 | bytes 8355888 | solution.py:238
  53.3 1.5 %collective-permute-start = (bf16[640,640]{1,0:T(8,128)(2,1)}, bf16[640,640]{1,0:T(8,128)(2,1)S(1)}, u32[]{:S(2)}, u32[]{:S(2)}) collective-permute-start(bf16[640,640]{1,0:T(8,128)(2,1)} %get-tuple-element.38), channel_id=1, source_target_pairs={{0,1},{1,0},{2,3},{3,2},{4,5},{5,4},{6,7},{7,6},{8,9},{9,8},{10,11... | collective-permute-start | bytes 2457608 | tf_op jit(solution)/shard_map/cond/branch_1_fun/core_swap/ppermute | solution.py:163
  54.8 1.9 %fusion.4 = f32[384,640]{1,0:T(8,128)S(1)} fusion(bf16[384,640]{1,0:T(8,128)(2,1)} %get-tuple-element.37, bf16[640,640]{1,0:T(8,128)(2,1)} %get-tuple-element.38), kind=kOutput, calls=%fused_computation.14 | convolution fusion | flops 314572800 | bytes 2293760 | tf_op jit(solution)/shard_map/cond/branch_1_fun/dot_general | solution.py:246
  57.0 1.4 %fusion = bf16[384,640]{1,0:T(8,128)(2,1)} fusion(f32[384,640]{1,0:T(8,128)S(1)} %fusion.4, bf16[384,640]{1,0:T(8,128)(2,1)S(1)} %get-tuple-element.39, bf16[640,640]{1,0:T(8,128)(2,1)S(1)} %collective-permute-done), kind=kOutput, calls=%fused_computation.1 | convolution fusion | flops 315064320 | bytes 2785280 | tf_op jit(solution)/shard_map/cond/branch_1_fun/dot_general | solution.py:247
  58.4 1.7 %collective-permute-start.11 = (bf16[384,640]{1,0:T(8,128)(2,1)}, bf16[384,640]{1,0:T(8,128)(2,1)S(1)}, u32[]{:S(2)}, u32[]{:S(2)}) collective-permute-start(bf16[384,640]{1,0:T(8,128)(2,1)} %get-tuple-element.87), channel_id=1, source_target_pairs={{0,3},{2,1},{4,4},{6,6},{8,9},{10,11},{12,14},{14,12},{17,19},{19,... | collective-permute-start | bytes 1474568 | tf_op jit(solution)/shard_map/sums_1/ppermute | solution.py:163
  60.1 1.3 %collective-permute-start.12 = (bf16[384,640]{1,0:T(8,128)(2,1)}, bf16[384,640]{1,0:T(8,128)(2,1)S(1)}, u32[]{:S(2)}, u32[]{:S(2)}) collective-permute-start(bf16[384,640]{1,0:T(8,128)(2,1)} %get-tuple-element.87), channel_id=1, source_target_pairs={{1,19},{3,17},{5,20},{7,22},{9,25},{11,27},{13,30},{15,28},{16,3},... | collective-permute-start | bytes 1474568 | tf_op jit(solution)/shard_map/sums_cross_1/ppermute | solution.py:163
  61.3 2.7 %collective-permute-start.8 = (bf16[640,640]{1,0:T(8,128)(2,1)}, bf16[640,640]{1,0:T(8,128)(2,1)}, u32[]{:S(2)}, u32[]{:S(2)}) collective-permute-start(bf16[640,640]{1,0:T(8,128)(2,1)} %constant_dynamic-slice_fusion), channel_id=1, source_target_pairs={{4,0},{5,1},{14,2},{15,3},{8,4},{9,5},{2,6},{3,7},{12,8},{13,9},{6... | collective-permute-start | bytes 2457608 | tf_op jit(solution)/shard_map/ring_after/ppermute | solution.py:163
  64.1 2.4 %collective-permute-done.10 = bf16[640,640]{1,0:T(8,128)(2,1)} collective-permute-done((bf16[640,640]{1,0:T(8,128)(2,1)}, bf16[640,640]{1,0:T(8,128)(2,1)}, u32[]{:S(2)}, u32[]{:S(2)}) %collective-permute-start.10) | collective-permute-done | bytes 819232 | tf_op jit(solution)/shard_map/ring_2/ppermute | solution.py:163
  66.4 9.0 %conditional.4 = (bf16[384,640]{1,0:T(8,128)(2,1)}, bf16[384,640]{1,0:T(8,128)(2,1)}) conditional(s32[]{:T(128)} %bitcast.1, () %tuple.35, (s32[]{:T(128)}, bf16[384,640]{1,0:T(8,128)(2,1)}, bf16[640,640]{1,0:T(8,128)(2,1)}, bf16[384,640]{1,0:T(8,128)(2,1)S(1)}, bf16[640,640]{1,0:T(8,128)(2,1)}, /*index=5*/bf16[640,640]{1,0:T(8,128)(2,1)}) %tuple.39), branch_computations={%region_2.3_spmd, %region_3.4_spmd} | conditional | flops 1259765760 | bytes 14417986 | solution.py:238
  66.4 0.7 collective-permute-start.1
  67.1 1.9 %fusion.6 = f32[384,640]{1,0:T(8,128)S(1)} fusion(bf16[384,640]{1,0:T(8,128)(2,1)} %get-tuple-element.41, bf16[640,640]{1,0:T(8,128)(2,1)} %get-tuple-element.45), kind=kOutput, calls=%fused_computation.16 | convolution fusion | flops 314572800 | bytes 2293760 | tf_op jit(solution)/shard_map/cond/branch_1_fun/dot_general | solution.py:246
  69.0 1.9 %fusion.5 = f32[384,640]{1,0:T(8,128)S(1)} fusion(bf16[384,640]{1,0:T(8,128)(2,1)} %get-tuple-element.41, bf16[640,640]{1,0:T(8,128)(2,1)} %get-tuple-element.42), kind=kOutput, calls=%fused_computation.15 | convolution fusion | flops 314572800 | bytes 2293760 | tf_op jit(solution)/shard_map/cond/branch_1_fun/dot_general | solution.py:246
  71.0 1.7 %fusion.1 = bf16[384,640]{1,0:T(8,128)(2,1)S(1)} fusion(f32[384,640]{1,0:T(8,128)S(1)} %fusion.5, bf16[384,640]{1,0:T(8,128)(2,1)S(1)} %get-tuple-element.43, bf16[640,640]{1,0:T(8,128)(2,1)} %get-tuple-element.44), kind=kOutput, calls=%fused_computation.4 | convolution fusion | flops 315064320 | bytes 2785280 | tf_op jit(solution)/shard_map/cond/branch_1_fun/dot_general | solution.py:247
  72.7 2.8 %broadcast_select_fusion = (bf16[384,640]{1,0:T(8,128)(2,1)}, bf16[384,640]{1,0:T(8,128)(2,1)}) fusion(bf16[384,640]{1,0:T(8,128)(2,1)S(1)} %fusion.1, pred[]{:T(512)S(6)} %eq.5, f32[384,640]{1,0:T(8,128)S(1)} %fusion.6, bf16[384,640]{1,0:T(8,128)(2,1)S(1)} %get-tuple-element.43, bf16[640,640]{1,0:T(8,128)(2,1)} %collective-permute-done.1), kind=kOutput, calls=%fused_computation.6 | convolution fusion | flops 315555840 | bytes 3768321 | tf_op jit(solution)/shard_map/cond/branch_1_fun/dot_general | solution.py:247
  75.5 2.0 %collective-permute-start.15 = (bf16[384,640]{1,0:T(8,128)(2,1)}, bf16[384,640]{1,0:T(8,128)(2,1)S(1)}, u32[]{:S(2)}, u32[]{:S(2)}) collective-permute-start(bf16[384,640]{1,0:T(8,128)(2,1)} %get-tuple-element.74), channel_id=1, source_target_pairs={{0,0},{2,2},{4,5},{6,7},{8,10},{10,8},{12,15},{14,13},{17,16},{19,... | collective-permute-start | bytes 1474568 | tf_op jit(solution)/shard_map/sums_02/ppermute | solution.py:163
  77.4 1.5 %collective-permute-start.17 = (bf16[384,640]{1,0:T(8,128)(2,1)}, bf16[384,640]{1,0:T(8,128)(2,1)}, u32[]{:S(2)}, u32[]{:S(2)}) collective-permute-start(bf16[384,640]{1,0:T(8,128)(2,1)} %get-tuple-element.74), channel_id=1, source_target_pairs={{1,16},{3,18},{5,21},{7,23},{9,26},{11,24},{13,31},{15,29},{16,0},... | collective-permute-start | bytes 1474568 | tf_op jit(solution)/shard_map/sums_cross_02/ppermute | solution.py:163
  78.9 4.5 %collective-permute-start.16 = (bf16[384,640]{1,0:T(8,128)(2,1)}, bf16[384,640]{1,0:T(8,128)(2,1)}, u32[]{:S(2)}, u32[]{:S(2)}) collective-permute-start(bf16[384,640]{1,0:T(8,128)(2,1)} %get-tuple-element.75), channel_id=1, source_target_pairs={{0,2},{2,0},{4,7},{6,5},{8,8},{10,10},{12,13},{14,15},{17,18},{19,... | collective-permute-start | bytes 1474568 | tf_op jit(solution)/shard_map/sums_20/ppermute | solution.py:163
  83.4 1.5 %collective-permute-start.18 = (bf16[384,640]{1,0:T(8,128)(2,1)}, bf16[384,640]{1,0:T(8,128)(2,1)}, u32[]{:S(2)}, u32[]{:S(2)}) collective-permute-start(bf16[384,640]{1,0:T(8,128)(2,1)} %get-tuple-element.75), channel_id=1, source_target_pairs={{1,18},{3,16},{5,23},{7,21},{9,24},{11,26},{13,29},{15,31},{16,2},... | collective-permute-start | bytes 1474568 | tf_op jit(solution)/shard_map/sums_cross_20/ppermute | solution.py:163
  84.9 1.1 %collective-permute-done.8 = bf16[640,640]{1,0:T(8,128)(2,1)} collective-permute-done((bf16[640,640]{1,0:T(8,128)(2,1)}, bf16[640,640]{1,0:T(8,128)(2,1)}, u32[]{:S(2)}, u32[]{:S(2)}) %collective-permute-start.8) | collective-permute-done | bytes 819232 | tf_op jit(solution)/shard_map/ring_after/ppermute | solution.py:163
  86.0 3.9 %conditional.5 = (bf16[384,640]{1,0:T(8,128)(2,1)}) conditional(s32[]{:T(128)} %bitcast.1, () %tuple.34, (bf16[384,640]{1,0:T(8,128)(2,1)}, bf16[640,640]{1,0:T(8,128)(2,1)}, bf16[384,640]{1,0:T(8,128)(2,1)}) %tuple.51), branch_computations={%region_4.5_spmd, %region_5.6_spmd} | conditional | flops 629637120 | bytes 10321996 | solution.py:238
  86.1 1.9 %fusion.7 = f32[384,640]{1,0:T(8,128)S(1)} fusion(bf16[384,640]{1,0:T(8,128)(2,1)} %get-tuple-element.46, bf16[640,640]{1,0:T(8,128)(2,1)} %get-tuple-element.47), kind=kOutput, calls=%fused_computation.17 | convolution fusion | flops 314572800 | bytes 2293760 | tf_op jit(solution)/shard_map/cond/branch_1_fun/dot_general | solution.py:246
  88.0 0.5 collective-permute-done.2
  88.5 1.4 %fusion.3 = bf16[384,640]{1,0:T(8,128)(2,1)} fusion(f32[384,640]{1,0:T(8,128)S(1)} %fusion.7, bf16[384,640]{1,0:T(8,128)(2,1)S(1)} %copy-done.6, bf16[640,640]{1,0:T(8,128)(2,1)S(1)} %collective-permute-done.2), kind=kOutput, calls=%fused_computation.9 | convolution fusion | flops 315064320 | bytes 2785280 | tf_op jit(solution)/shard_map/cond/branch_1_fun/dot_general | solution.py:247
  89.9 1.9 %collective-permute-start.13 = (bf16[384,640]{1,0:T(8,128)(2,1)}, bf16[384,640]{1,0:T(8,128)(2,1)S(1)}, u32[]{:S(2)}, u32[]{:S(2)}) collective-permute-start(bf16[384,640]{1,0:T(8,128)(2,1)} %get-tuple-element.88), channel_id=1, source_target_pairs={{0,1},{2,3},{4,6},{6,4},{8,11},{10,9},{12,12},{14,14},{17,17},{19,... | collective-permute-start | bytes 1474568 | tf_op jit(solution)/shard_map/sums_3/ppermute | solution.py:163
  91.8 1.3 %collective-permute-start.14 = (bf16[384,640]{1,0:T(8,128)(2,1)}, bf16[384,640]{1,0:T(8,128)(2,1)S(1)}, u32[]{:S(2)}, u32[]{:S(2)}) collective-permute-start(bf16[384,640]{1,0:T(8,128)(2,1)} %get-tuple-element.88), channel_id=1, source_target_pairs={{1,17},{3,19},{5,22},{7,20},{9,27},{11,25},{13,28},{15,30},{16,1},... | collective-permute-start | bytes 1474568 | tf_op jit(solution)/shard_map/sums_cross_3/ppermute | solution.py:163
  93.2 1.5 %copy-done.1 = f32[384,1280]{1,0:T(8,128)S(1)} copy-done((f32[384,1280]{1,0:T(8,128)S(1)}, f32[384,1280]{1,0:T(8,128)}, u32[]{:S(2)}) %copy-start.1) | copy-done | bytes 1966104
  94.8 1.9 %finish.2.refs_2_ = f32[384,1280]{1,0:T(8,128)S(1)} custom-call(s32[1]{0:T(128)} %bitcast.spot, bf16[384,640]{1,0:T(8,128)(2,1)S(1)} %collective-permute-done.11.refs_0_, bf16[384,640]{1,0:T(8,128)(2,1)S(1)} %collective-permute-done.15.refs_1_, bf16[384,640]{1,0:T(8,128)(2,1)} %collective-permute-done.16.refs_2_, ...), custom_call_target="tpu_custom_call" | custom-call | tf_op jit(solution)/shard_map/finish/pallas_call | solution.py:187
  96.7 8.3 %collective-permute-done.13.refs_0_ = bf16[384,640]{1,0:T(8,128)(2,1)S(1)} collective-permute-done((bf16[384,640]{1,0:T(8,128)(2,1)}, bf16[384,640]{1,0:T(8,128)(2,1)S(1)}, u32[]{:S(2)}, u32[]{:S(2)}) %collective-permute-start.13) | collective-permute-done | bytes 491552 | tf_op jit(solution)/shard_map/sums_3/ppermute | solution.py:163
  105.0 1.6 %collective-permute-done.14.refs_1_ = bf16[384,640]{1,0:T(8,128)(2,1)S(1)} collective-permute-done((bf16[384,640]{1,0:T(8,128)(2,1)}, bf16[384,640]{1,0:T(8,128)(2,1)S(1)}, u32[]{:S(2)}, u32[]{:S(2)}) %collective-permute-start.14) | collective-permute-done | bytes 491552 | tf_op jit(solution)/shard_map/sums_cross_3/ppermute | solution.py:163
  106.6 1.4 %finish.3 = f32[384,1280]{1,0:T(8,128)} custom-call(s32[1]{0:T(128)} %bitcast.spot, bf16[384,640]{1,0:T(8,128)(2,1)S(1)} %collective-permute-done.13.refs_0_, bf16[384,640]{1,0:T(8,128)(2,1)S(1)} %collective-permute-done.14.refs_1_, f32[384,1280]{1,0:T(8,128)S(1)} %finish.2.refs_2_, f32[1,1280]{1,0:T(1,128)S(1)} %broadcast_in_dim.4.refs_7_.refs_3_), custom_call_target="tpu_custom_call" | custom-call | tf_op jit(solution)/shard_map/finish/pallas_call | solution.py:187
  (25 shorter events, 0.5 us)
Async XLA Ops:
  0.0 6.1 %copy-start = (bf16[640,1280]{1,0:T(8,128)(2,1)S(1)}, bf16[640,1280]{1,0:T(8,128)(2,1)}, u32[]{:S(2)}) copy-start(bf16[640,1280]{1,0:T(8,128)(2,1)} %param.17) | copy-start | bytes 4915204
  0.0 25.7 %collective-permute-start.3 = (bf16[2,384,640]{2,1,0:T(8,128)(2,1)}, bf16[2,384,640]{2,1,0:T(8,128)(2,1)S(1)}, u32[]{:S(2)}, u32[]{:S(2)}) collective-permute-start(bf16[2,384,640]{2,1,0:T(8,128)(2,1)} %own_ref.1), channel_id=1, source_target_pairs={{0,4},{4,8},{8,12},{1,5},{5,9},{9,13},{2,6},{6,10},{10,14},{3,7},{... | collective-permute-start | bytes 2949128 | tf_op jit(solution)/shard_map/ppermute | solution.py:120
  3.6 25.9 %collective-permute-start.4 = (bf16[2,384,640]{2,1,0:T(8,128)(2,1)}, bf16[2,384,640]{2,1,0:T(8,128)(2,1)}, u32[]{:S(2)}, u32[]{:S(2)}) collective-permute-start(bf16[2,384,640]{2,1,0:T(8,128)(2,1)} %own_ref.1), channel_id=1, source_target_pairs={{4,0},{8,4},{12,8},{5,1},{9,5},{13,9},{6,2},{10,6},{14,10},{7,3},{... | collective-permute-start | bytes 2949128 | tf_op jit(solution)/shard_map/ppermute | solution.py:120
  7.0 59.4 %collective-permute-start.9 = (bf16[640,640]{1,0:T(8,128)(2,1)}, bf16[640,640]{1,0:T(8,128)(2,1)}, u32[]{:S(2)}, u32[]{:S(2)}) collective-permute-start(bf16[640,640]{1,0:T(8,128)(2,1)} %constant_dynamic-slice_fusion), channel_id=1, source_target_pairs={{0,1},{1,0},{2,3},{3,2},{4,5},{5,4},{6,7},{7,6},{8,9},{9,8},{10,11... | collective-permute-start | bytes 2457608 | tf_op jit(solution)/shard_map/core_swap_0/ppermute | solution.py:163
  25.7 19.5 %collective-permute-start.7 = (bf16[640,640]{1,0:T(8,128)(2,1)}, bf16[640,640]{1,0:T(8,128)(2,1)}, u32[]{:S(2)}, u32[]{:S(2)}) collective-permute-start(bf16[640,640]{1,0:T(8,128)(2,1)} %constant_dynamic-slice_fusion), channel_id=1, source_target_pairs={{0,4},{1,5},{2,14},{3,15},{4,8},{5,9},{6,2},{7,3},{8,12},{9,13},{1... | collective-permute-start | bytes 2457608 | tf_op jit(solution)/shard_map/ring_1/ppermute | solution.py:163
  29.5 1.2 %copy-start.2 = (bf16[2,384,640]{2,1,0:T(8,128)(2,1)S(1)}, bf16[2,384,640]{2,1,0:T(8,128)(2,1)}, u32[]{:S(2)}) copy-start(bf16[2,384,640]{2,1,0:T(8,128)(2,1)} %own_ref.1) | copy-start | bytes 2949124
  30.7 1.0 copy-start.3
  31.7 0.7 copy-start.4
  40.0 11.8 %collective-permute-start.5 = (bf16[384,640]{1,0:T(8,128)(2,1)S(1)}, bf16[384,640]{1,0:T(8,128)(2,1)S(1)}, u32[]{:S(2)}, u32[]{:S(2)}) collective-permute-start(bf16[384,640]{1,0:T(8,128)(2,1)S(1)} %attend.1), channel_id=1, source_target_pairs={{0,16},{1,0},{2,18},{3,2},{4,20},{5,4},{6,22},{7,6},{8,24},{9,8},{... | collective-permute-start | bytes 1474568 | tf_op jit(solution)/shard_map/rows_1/ppermute | solution.py:163
  41.6 10.2 %collective-permute-start.6 = (bf16[384,640]{1,0:T(8,128)(2,1)S(1)}, bf16[384,640]{1,0:T(8,128)(2,1)S(1)}, u32[]{:S(2)}, u32[]{:S(2)}) collective-permute-start(bf16[384,640]{1,0:T(8,128)(2,1)S(1)} %attend.1), channel_id=1, source_target_pairs={{1,16},{3,18},{5,20},{7,22},{9,24},{11,26},{13,28},{15,30},{16,1},... | collective-permute-start | bytes 1474568 | tf_op jit(solution)/shard_map/rows_2/ppermute | solution.py:163
  45.3 21.2 %collective-permute-start.10 = (bf16[640,640]{1,0:T(8,128)(2,1)}, bf16[640,640]{1,0:T(8,128)(2,1)}, u32[]{:S(2)}, u32[]{:S(2)}) collective-permute-start(bf16[640,640]{1,0:T(8,128)(2,1)} %collective-permute-done.7), channel_id=1, source_target_pairs={{0,4},{1,5},{2,14},{3,15},{4,8},{5,9},{6,2},{7,3},{8,12},{9,13},{1... | collective-permute-start | bytes 2457608 | tf_op jit(solution)/shard_map/ring_2/ppermute | solution.py:163
  53.3 13.1 %copy-start.5 = (bf16[384,640]{1,0:T(8,128)(2,1)}, bf16[384,640]{1,0:T(8,128)(2,1)S(1)}, u32[]{:S(2)}) copy-start(bf16[384,640]{1,0:T(8,128)(2,1)S(1)} %get-tuple-element.81) | copy-start | bytes 1474564
  53.3 3.7 %collective-permute-start = (bf16[640,640]{1,0:T(8,128)(2,1)}, bf16[640,640]{1,0:T(8,128)(2,1)S(1)}, u32[]{:S(2)}, u32[]{:S(2)}) collective-permute-start(bf16[640,640]{1,0:T(8,128)(2,1)} %get-tuple-element.38), channel_id=1, source_target_pairs={{0,1},{1,0},{2,3},{3,2},{4,5},{5,4},{6,7},{7,6},{8,9},{9,8},{10,11... | collective-permute-start | bytes 2457608 | tf_op jit(solution)/shard_map/cond/branch_1_fun/core_swap/ppermute | solution.py:163
  58.4 17.1 %collective-permute-start.11 = (bf16[384,640]{1,0:T(8,128)(2,1)}, bf16[384,640]{1,0:T(8,128)(2,1)S(1)}, u32[]{:S(2)}, u32[]{:S(2)}) collective-permute-start(bf16[384,640]{1,0:T(8,128)(2,1)} %get-tuple-element.87), channel_id=1, source_target_pairs={{0,3},{2,1},{4,4},{6,6},{8,9},{10,11},{12,14},{14,12},{17,19},{19,... | collective-permute-start | bytes 1474568 | tf_op jit(solution)/shard_map/sums_1/ppermute | solution.py:163
  60.1 15.4 %collective-permute-start.12 = (bf16[384,640]{1,0:T(8,128)(2,1)}, bf16[384,640]{1,0:T(8,128)(2,1)S(1)}, u32[]{:S(2)}, u32[]{:S(2)}) collective-permute-start(bf16[384,640]{1,0:T(8,128)(2,1)} %get-tuple-element.87), channel_id=1, source_target_pairs={{1,19},{3,17},{5,20},{7,22},{9,25},{11,27},{13,30},{15,28},{16,3},... | collective-permute-start | bytes 1474568 | tf_op jit(solution)/shard_map/sums_cross_1/ppermute | solution.py:163
  61.3 24.6 %collective-permute-start.8 = (bf16[640,640]{1,0:T(8,128)(2,1)}, bf16[640,640]{1,0:T(8,128)(2,1)}, u32[]{:S(2)}, u32[]{:S(2)}) collective-permute-start(bf16[640,640]{1,0:T(8,128)(2,1)} %constant_dynamic-slice_fusion), channel_id=1, source_target_pairs={{4,0},{5,1},{14,2},{15,3},{8,4},{9,5},{2,6},{3,7},{12,8},{13,9},{6... | collective-permute-start | bytes 2457608 | tf_op jit(solution)/shard_map/ring_after/ppermute | solution.py:163
  66.4 6.3 %collective-permute-start.1 = (bf16[640,640]{1,0:T(8,128)(2,1)}, bf16[640,640]{1,0:T(8,128)(2,1)}, u32[]{:S(2)}, u32[]{:S(2)}) collective-permute-start(bf16[640,640]{1,0:T(8,128)(2,1)} %get-tuple-element.45), channel_id=1, source_target_pairs={{0,1},{1,0},{2,3},{3,2},{4,5},{5,4},{6,7},{7,6},{8,9},{9,8},{10,11... | collective-permute-start | bytes 2457608 | tf_op jit(solution)/shard_map/cond/branch_1_fun/core_swap/ppermute | solution.py:163
  75.5 16.3 %collective-permute-start.15 = (bf16[384,640]{1,0:T(8,128)(2,1)}, bf16[384,640]{1,0:T(8,128)(2,1)S(1)}, u32[]{:S(2)}, u32[]{:S(2)}) collective-permute-start(bf16[384,640]{1,0:T(8,128)(2,1)} %get-tuple-element.74), channel_id=1, source_target_pairs={{0,0},{2,2},{4,5},{6,7},{8,10},{10,8},{12,15},{14,13},{17,16},{19,... | collective-permute-start | bytes 1474568 | tf_op jit(solution)/shard_map/sums_02/ppermute | solution.py:163
  77.4 15.8 %collective-permute-start.17 = (bf16[384,640]{1,0:T(8,128)(2,1)}, bf16[384,640]{1,0:T(8,128)(2,1)}, u32[]{:S(2)}, u32[]{:S(2)}) collective-permute-start(bf16[384,640]{1,0:T(8,128)(2,1)} %get-tuple-element.74), channel_id=1, source_target_pairs={{1,16},{3,18},{5,21},{7,23},{9,26},{11,24},{13,31},{15,29},{16,0},... | collective-permute-start | bytes 1474568 | tf_op jit(solution)/shard_map/sums_cross_02/ppermute | solution.py:163
  78.9 14.3 %collective-permute-start.16 = (bf16[384,640]{1,0:T(8,128)(2,1)}, bf16[384,640]{1,0:T(8,128)(2,1)}, u32[]{:S(2)}, u32[]{:S(2)}) collective-permute-start(bf16[384,640]{1,0:T(8,128)(2,1)} %get-tuple-element.75), channel_id=1, source_target_pairs={{0,2},{2,0},{4,7},{6,5},{8,8},{10,10},{12,13},{14,15},{17,18},{19,... | collective-permute-start | bytes 1474568 | tf_op jit(solution)/shard_map/sums_20/ppermute | solution.py:163
  83.4 9.8 %collective-permute-start.18 = (bf16[384,640]{1,0:T(8,128)(2,1)}, bf16[384,640]{1,0:T(8,128)(2,1)}, u32[]{:S(2)}, u32[]{:S(2)}) collective-permute-start(bf16[384,640]{1,0:T(8,128)(2,1)} %get-tuple-element.75), channel_id=1, source_target_pairs={{1,18},{3,16},{5,23},{7,21},{9,24},{11,26},{13,29},{15,31},{16,2},... | collective-permute-start | bytes 1474568 | tf_op jit(solution)/shard_map/sums_cross_20/ppermute | solution.py:163
  86.0 7.2 %copy-start.7 = (f32[1280]{0:T(1024)S(1)}, f32[1280]{0:T(1024)}, u32[]{:S(2)}) copy-start(f32[1280]{0:T(1024)} %param.16) | copy-start | bytes 15364
  86.0 2.5 %copy-start.6 = (bf16[384,640]{1,0:T(8,128)(2,1)S(1)}, bf16[384,640]{1,0:T(8,128)(2,1)}, u32[]{:S(2)}) copy-start(bf16[384,640]{1,0:T(8,128)(2,1)} %get-tuple-element.48) | copy-start | bytes 1474564 | tf_op jit(solution)/shard_map/cond
  86.0 2.5 %collective-permute-start.2 = (bf16[640,640]{1,0:T(8,128)(2,1)}, bf16[640,640]{1,0:T(8,128)(2,1)S(1)}, u32[]{:S(2)}, u32[]{:S(2)}) collective-permute-start(bf16[640,640]{1,0:T(8,128)(2,1)} %get-tuple-element.47), channel_id=1, source_target_pairs={{0,1},{1,0},{2,3},{3,2},{4,5},{5,4},{6,7},{7,6},{8,9},{9,8},{10,11... | collective-permute-start | bytes 2457608 | tf_op jit(solution)/shard_map/cond/branch_1_fun/core_swap/ppermute | solution.py:163
  89.9 15.1 %collective-permute-start.13 = (bf16[384,640]{1,0:T(8,128)(2,1)}, bf16[384,640]{1,0:T(8,128)(2,1)S(1)}, u32[]{:S(2)}, u32[]{:S(2)}) collective-permute-start(bf16[384,640]{1,0:T(8,128)(2,1)} %get-tuple-element.88), channel_id=1, source_target_pairs={{0,1},{2,3},{4,6},{6,4},{8,11},{10,9},{12,12},{14,14},{17,17},{19,... | collective-permute-start | bytes 1474568 | tf_op jit(solution)/shard_map/sums_3/ppermute | solution.py:163
  91.8 14.7 %collective-permute-start.14 = (bf16[384,640]{1,0:T(8,128)(2,1)}, bf16[384,640]{1,0:T(8,128)(2,1)S(1)}, u32[]{:S(2)}, u32[]{:S(2)}) collective-permute-start(bf16[384,640]{1,0:T(8,128)(2,1)} %get-tuple-element.88), channel_id=1, source_target_pairs={{1,17},{3,19},{5,22},{7,20},{9,27},{11,25},{13,28},{15,30},{16,1},... | collective-permute-start | bytes 1474568 | tf_op jit(solution)/shard_map/sums_cross_3/ppermute | solution.py:163
  93.2 1.5 %copy-start.1 = (f32[384,1280]{1,0:T(8,128)S(1)}, f32[384,1280]{1,0:T(8,128)}, u32[]{:S(2)}) copy-start(f32[384,1280]{1,0:T(8,128)} %refs_6_.1) | copy-start | bytes 5898244

commit v9 on v8

--- a/solution.py
+++ b/solution.py
@@ -269,7 +269,6 @@
     rows_sib = jnp.where(here, first, second)
     s1 = region(token, begin, rows_own, rows_sib, w1)
     middle = to_owners(s1, (1, 1), "1")
-    w2, s1 = tie((w2, s1))
     w3 = send(w0, back, "ring_after")
     low_sum, high_sum = region(token, mix, rows_own, rows_sib, w0, v0, w2)
     low_sum, high_sum, *middle = tie((low_sum, high_sum, *middle))

time: 109 us -> 109 us (level)
  no operation moved by 1% of the time
where the time goes in v9:
time: 109 us; the launch traced here: 108 us
  waiting for transfers between devices  41.9 us (38%)
  starting transfers between devices  31.9 us (29%)
  matrix products  14.9 us (14%)
  Pallas kernels  11.5 us (11%)
  local copies, waits for them, and re-layouts  5.42 us (5%)
  other arithmetic  1.57 us (1%)
    ppermute x17, starting transfers between devices, send(): return lax.ppermute(array, AXES, route)  25.9 us
    ppermute x17, waiting for transfers between devices, send(): return lax.ppermute(array, AXES, route)  21.7 us
    ppermute x1, waiting for transfers between devices, halos(): lax.ppermute(keyvals, 'frame', forward)  18.7 us
    pallas_call x1, Pallas kernels, attend(): pl.pallas_call(attend_kernel, out_shape=jax.ShapeDtypeStruct((rows, width...  7.66 us
    dot_general x4, matrix products, sums(): total = jnp.dot(rows_own, own, preferred_element_type=jnp.float32)  7.62 us
    dot_general x4, matrix products, sums(): total = total + jnp.dot(rows_sib, sib, preferred_element_type=jnp.float32)  7.28 us
    unnamed x14, local copies, waits for them, and re-layouts  4.44 us
    ppermute x1, starting transfers between devices, halos(): lax.ppermute(keyvals, 'frame', forward)  3.61 us
  transfers between devices with their start and end apart: 19, of which 11 were waited for; matrix products, arithmetic and copies ran while one was open for 16% of the time, Pallas kernels for 9%

profile of v9, /device:TPU:8, one launch (start us, length us, event | category | flops | bytes accessed | tf_op | source)
XLA Modules:
  0.0 108.0 jit_solution(13996724928161733589)
XLA Ops:
  0.0 3.6 %collective-permute-start.3 = (bf16[2,384,640]{2,1,0:T(8,128)(2,1)}, bf16[2,384,640]{2,1,0:T(8,128)(2,1)S(1)}, u32[]{:S(2)}, u32[]{:S(2)}) collective-permute-start(bf16[2,384,640]{2,1,0:T(8,128)(2,1)} %own_ref.1), channel_id=1, source_target_pairs={{0,4},{4,8},{8,12},{1,5},{5,9},{9,13},{2,6},{6,10},{10,14},{3,7},{... | collective-permute-start | bytes 2949128 | tf_op jit(solution)/shard_map/ppermute | solution.py:120
  3.6 2.4 %collective-permute-start.4 = (bf16[2,384,640]{2,1,0:T(8,128)(2,1)}, bf16[2,384,640]{2,1,0:T(8,128)(2,1)}, u32[]{:S(2)}, u32[]{:S(2)}) collective-permute-start(bf16[2,384,640]{2,1,0:T(8,128)(2,1)} %own_ref.1), channel_id=1, source_target_pairs={{4,0},{8,4},{12,8},{5,1},{9,5},{13,9},{6,2},{10,6},{14,10},{7,3},{... | collective-permute-start | bytes 2949128 | tf_op jit(solution)/shard_map/ppermute | solution.py:120
  6.1 1.0 constant_dynamic-slice_fusion
  7.0 18.7 %collective-permute-done.3.low_ref = bf16[2,384,640]{2,1,0:T(8,128)(2,1)S(1)} collective-permute-done((bf16[2,384,640]{2,1,0:T(8,128)(2,1)}, bf16[2,384,640]{2,1,0:T(8,128)(2,1)S(1)}, u32[]{:S(2)}, u32[]{:S(2)}) %collective-permute-start.3) | collective-permute-done | bytes 983072 | tf_op jit(solution)/shard_map/ppermute | solution.py:120
  25.7 1.6 %collective-permute-start.7 = (bf16[640,640]{1,0:T(8,128)(2,1)}, bf16[640,640]{1,0:T(8,128)(2,1)}, u32[]{:S(2)}, u32[]{:S(2)}) collective-permute-start(bf16[640,640]{1,0:T(8,128)(2,1)} %constant_dynamic-slice_fusion), channel_id=1, source_target_pairs={{0,4},{1,5},{2,14},{3,15},{4,8},{5,9},{6,2},{7,3},{8,12},{9,13},{1... | collective-permute-start | bytes 2457608 | tf_op jit(solution)/shard_map/ring_1/ppermute | solution.py:163
  27.3 0.7 subtract_clamp_fusion.ids
  28.0 1.5 %collective-permute-done.4.high_ref = bf16[2,384,640]{2,1,0:T(8,128)(2,1)} collective-permute-done((bf16[2,384,640]{2,1,0:T(8,128)(2,1)}, bf16[2,384,640]{2,1,0:T(8,128)(2,1)}, u32[]{:S(2)}, u32[]{:S(2)}) %collective-permute-start.4) | collective-permute-done | bytes 983072 | tf_op jit(solution)/shard_map/ppermute | solution.py:120
  29.5 1.2 %copy-done.2 = bf16[2,384,640]{2,1,0:T(8,128)(2,1)S(1)} copy-done((bf16[2,384,640]{2,1,0:T(8,128)(2,1)S(1)}, bf16[2,384,640]{2,1,0:T(8,128)(2,1)}, u32[]{:S(2)}) %copy-start.2) | copy-done | bytes 983064
  30.7 1.0 copy-done.3
  31.7 0.7 copy-done.4
  32.4 7.7 %attend.1 = bf16[384,640]{1,0:T(8,128)(2,1)S(1)} custom-call(s32[6,8]{1,0:T(8,128)S(1)} %subtract_clamp_fusion.ids, s32[6]{0:T(128)S(1)} %copy-done.4, bf16[384,640]{1,0:T(8,128)(2,1)S(1)} %copy-done.3, bf16[2,384,640]{2,1,0:T(8,128)(2,1)S(1)} %copy-done.2, bf16[2,384,640]{2,1,0:T(8,128)(2,1)S(1)} %collective-permute-done.3.low_ref, ...), custom_call_target="tpu_custom_call" | custom-call | flops 8000000000 | bytes 24000000 | tf_op jit(solution)/shard_map/attend/pallas_call | solution.py:101
  40.0 1.5 %collective-permute-start.5 = (bf16[384,640]{1,0:T(8,128)(2,1)S(1)}, bf16[384,640]{1,0:T(8,128)(2,1)S(1)}, u32[]{:S(2)}, u32[]{:S(2)}) collective-permute-start(bf16[384,640]{1,0:T(8,128)(2,1)S(1)} %attend.1), channel_id=1, source_target_pairs={{0,16},{1,0},{2,18},{3,2},{4,20},{5,4},{6,22},{7,6},{8,24},{9,8},{... | collective-permute-start | bytes 1474568 | tf_op jit(solution)/shard_map/rows_1/ppermute | solution.py:163
  41.6 0.7 collective-permute-start.6
  42.3 3.0 %collective-permute-done.7 = bf16[640,640]{1,0:T(8,128)(2,1)} collective-permute-done((bf16[640,640]{1,0:T(8,128)(2,1)}, bf16[640,640]{1,0:T(8,128)(2,1)}, u32[]{:S(2)}, u32[]{:S(2)}) %collective-permute-start.7) | collective-permute-done | bytes 819232 | tf_op jit(solution)/shard_map/ring_1/ppermute | solution.py:163
  45.3 1.6 %collective-permute-start.10 = (bf16[640,640]{1,0:T(8,128)(2,1)}, bf16[640,640]{1,0:T(8,128)(2,1)}, u32[]{:S(2)}, u32[]{:S(2)}) collective-permute-start(bf16[640,640]{1,0:T(8,128)(2,1)} %collective-permute-done.7), channel_id=1, source_target_pairs={{0,4},{1,5},{2,14},{3,15},{4,8},{5,9},{6,2},{7,3},{8,12},{9,13},{1... | collective-permute-start | bytes 2457608 | tf_op jit(solution)/shard_map/ring_2/ppermute | solution.py:163
  46.8 0.6 fence.1
  47.4 4.4 %collective-permute-done.5 = bf16[384,640]{1,0:T(8,128)(2,1)S(1)} collective-permute-done((bf16[384,640]{1,0:T(8,128)(2,1)S(1)}, bf16[384,640]{1,0:T(8,128)(2,1)S(1)}, u32[]{:S(2)}, u32[]{:S(2)}) %collective-permute-start.5) | collective-permute-done | bytes 491552 | tf_op jit(solution)/shard_map/rows_1/ppermute | solution.py:163
  52.4 0.9 broadcast_select_fusion.2
  53.3 5.1 %conditional.4 = (bf16[384,640]{1,0:T(8,128)(2,1)}) conditional(s32[]{:T(128)} %bitcast.1, () %tuple.36, (bf16[384,640]{1,0:T(8,128)(2,1)}, bf16[640,640]{1,0:T(8,128)(2,1)}, bf16[384,640]{1,0:T(8,128)(2,1)S(1)}) %tuple.37), branch_computations={%region_2.3_spmd, %region_3.4_spmd} | conditional | flops 629637120 | bytes 8355888 | solution.py:238
  53.3 1.5 %collective-permute-start.1 = (bf16[640,640]{1,0:T(8,128)(2,1)}, bf16[640,640]{1,0:T(8,128)(2,1)S(1)}, u32[]{:S(2)}, u32[]{:S(2)}) collective-permute-start(bf16[640,640]{1,0:T(8,128)(2,1)} %get-tuple-element.44), channel_id=1, source_target_pairs={{0,1},{1,0},{2,3},{3,2},{4,5},{5,4},{6,7},{7,6},{8,9},{9,8},{10,11... | collective-permute-start | bytes 2457608 | tf_op jit(solution)/shard_map/cond/branch_1_fun/core_swap/ppermute | solution.py:163
  54.8 1.9 %fusion.6 = f32[384,640]{1,0:T(8,128)S(1)} fusion(bf16[384,640]{1,0:T(8,128)(2,1)} %get-tuple-element.43, bf16[640,640]{1,0:T(8,128)(2,1)} %get-tuple-element.44), kind=kOutput, calls=%fused_computation.16 | convolution fusion | flops 314572800 | bytes 2293760 | tf_op jit(solution)/shard_map/cond/branch_1_fun/dot_general | solution.py:246
  56.9 1.4 %fusion.2 = bf16[384,640]{1,0:T(8,128)(2,1)} fusion(f32[384,640]{1,0:T(8,128)S(1)} %fusion.6, bf16[384,640]{1,0:T(8,128)(2,1)S(1)} %get-tuple-element.45, bf16[640,640]{1,0:T(8,128)(2,1)S(1)} %collective-permute-done.1), kind=kOutput, calls=%fused_computation.7 | convolution fusion | flops 315064320 | bytes 2785280 | tf_op jit(solution)/shard_map/cond/branch_1_fun/dot_general | solution.py:247
  58.3 1.7 %collective-permute-start.11 = (bf16[384,640]{1,0:T(8,128)(2,1)}, bf16[384,640]{1,0:T(8,128)(2,1)S(1)}, u32[]{:S(2)}, u32[]{:S(2)}) collective-permute-start(bf16[384,640]{1,0:T(8,128)(2,1)} %get-tuple-element.85), channel_id=1, source_target_pairs={{0,3},{2,1},{4,4},{6,6},{8,9},{10,11},{12,14},{14,12},{17,19},{19,... | collective-permute-start | bytes 1474568 | tf_op jit(solution)/shard_map/sums_1/ppermute | solution.py:163
  60.0 1.3 %collective-permute-start.12 = (bf16[384,640]{1,0:T(8,128)(2,1)}, bf16[384,640]{1,0:T(8,128)(2,1)S(1)}, u32[]{:S(2)}, u32[]{:S(2)}) collective-permute-start(bf16[384,640]{1,0:T(8,128)(2,1)} %get-tuple-element.85), channel_id=1, source_target_pairs={{1,19},{3,17},{5,20},{7,22},{9,25},{11,27},{13,30},{15,28},{16,3},... | collective-permute-start | bytes 1474568 | tf_op jit(solution)/shard_map/sums_cross_1/ppermute | solution.py:163
  61.3 2.7 %collective-permute-start.8 = (bf16[640,640]{1,0:T(8,128)(2,1)}, bf16[640,640]{1,0:T(8,128)(2,1)}, u32[]{:S(2)}, u32[]{:S(2)}) collective-permute-start(bf16[640,640]{1,0:T(8,128)(2,1)} %constant_dynamic-slice_fusion), channel_id=1, source_target_pairs={{4,0},{5,1},{14,2},{15,3},{8,4},{9,5},{2,6},{3,7},{12,8},{13,9},{6... | collective-permute-start | bytes 2457608 | tf_op jit(solution)/shard_map/ring_after/ppermute | solution.py:163
  64.0 2.4 %collective-permute-done.10 = bf16[640,640]{1,0:T(8,128)(2,1)} collective-permute-done((bf16[640,640]{1,0:T(8,128)(2,1)}, bf16[640,640]{1,0:T(8,128)(2,1)}, u32[]{:S(2)}, u32[]{:S(2)}) %collective-permute-start.10) | collective-permute-done | bytes 819232 | tf_op jit(solution)/shard_map/ring_2/ppermute | solution.py:163
  66.4 9.0 %conditional.3 = (bf16[384,640]{1,0:T(8,128)(2,1)}, bf16[384,640]{1,0:T(8,128)(2,1)}) conditional(s32[]{:T(128)} %bitcast.1, () %tuple.34, (s32[]{:T(128)}, bf16[384,640]{1,0:T(8,128)(2,1)}, bf16[640,640]{1,0:T(8,128)(2,1)}, bf16[384,640]{1,0:T(8,128)(2,1)S(1)}, bf16[640,640]{1,0:T(8,128)(2,1)}, /*index=5*/bf16[640,640]{1,0:T(8,128)(2,1)}) %tuple.35), branch_computations={%region_0.1_spmd, %region_1.2_spmd} | conditional | flops 1259765760 | bytes 14417986 | solution.py:238
  66.4 0.7 collective-permute-start
  67.1 1.9 %fusion.5 = f32[384,640]{1,0:T(8,128)S(1)} fusion(bf16[384,640]{1,0:T(8,128)(2,1)} %get-tuple-element.38, bf16[640,640]{1,0:T(8,128)(2,1)} %get-tuple-element.42), kind=kOutput, calls=%fused_computation.15 | convolution fusion | flops 314572800 | bytes 2293760 | tf_op jit(solution)/shard_map/cond/branch_1_fun/dot_general | solution.py:246
  69.0 1.9 %fusion.4 = f32[384,640]{1,0:T(8,128)S(1)} fusion(bf16[384,640]{1,0:T(8,128)(2,1)} %get-tuple-element.38, bf16[640,640]{1,0:T(8,128)(2,1)} %get-tuple-element.39), kind=kOutput, calls=%fused_computation.14 | convolution fusion | flops 314572800 | bytes 2293760 | tf_op jit(solution)/shard_map/cond/branch_1_fun/dot_general | solution.py:246
  70.9 1.7 %fusion = bf16[384,640]{1,0:T(8,128)(2,1)S(1)} fusion(f32[384,640]{1,0:T(8,128)S(1)} %fusion.4, bf16[384,640]{1,0:T(8,128)(2,1)S(1)} %get-tuple-element.40, bf16[640,640]{1,0:T(8,128)(2,1)} %get-tuple-element.41), kind=kOutput, calls=%fused_computation.2 | convolution fusion | flops 315064320 | bytes 2785280 | tf_op jit(solution)/shard_map/cond/branch_1_fun/dot_general | solution.py:247
  72.7 2.8 %broadcast_select_fusion = (bf16[384,640]{1,0:T(8,128)(2,1)}, bf16[384,640]{1,0:T(8,128)(2,1)}) fusion(bf16[384,640]{1,0:T(8,128)(2,1)S(1)} %fusion, pred[]{:T(512)S(6)} %eq.5, f32[384,640]{1,0:T(8,128)S(1)} %fusion.5, bf16[384,640]{1,0:T(8,128)(2,1)S(1)} %get-tuple-element.40, bf16[640,640]{1,0:T(8,128)(2,1)} %collective-permute-done), kind=kOutput, calls=%fused_computation.4 | convolution fusion | flops 315555840 | bytes 3768321 | tf_op jit(solution)/shard_map/cond/branch_1_fun/dot_general | solution.py:247
  75.4 2.0 %collective-permute-start.15 = (bf16[384,640]{1,0:T(8,128)(2,1)}, bf16[384,640]{1,0:T(8,128)(2,1)S(1)}, u32[]{:S(2)}, u32[]{:S(2)}) collective-permute-start(bf16[384,640]{1,0:T(8,128)(2,1)} %get-tuple-element.72), channel_id=1, source_target_pairs={{0,0},{2,2},{4,5},{6,7},{8,10},{10,8},{12,15},{14,13},{17,16},{19,... | collective-permute-start | bytes 1474568 | tf_op jit(solution)/shard_map/sums_02/ppermute | solution.py:163
  77.4 1.5 %collective-permute-start.17 = (bf16[384,640]{1,0:T(8,128)(2,1)}, bf16[384,640]{1,0:T(8,128)(2,1)}, u32[]{:S(2)}, u32[]{:S(2)}) collective-permute-start(bf16[384,640]{1,0:T(8,128)(2,1)} %get-tuple-element.72), channel_id=1, source_target_pairs={{1,16},{3,18},{5,21},{7,23},{9,26},{11,24},{13,31},{15,29},{16,0},... | collective-permute-start | bytes 1474568 | tf_op jit(solution)/shard_map/sums_cross_02/ppermute | solution.py:163
  78.8 4.6 %collective-permute-start.16 = (bf16[384,640]{1,0:T(8,128)(2,1)}, bf16[384,640]{1,0:T(8,128)(2,1)}, u32[]{:S(2)}, u32[]{:S(2)}) collective-permute-start(bf16[384,640]{1,0:T(8,128)(2,1)} %get-tuple-element.73), channel_id=1, source_target_pairs={{0,2},{2,0},{4,7},{6,5},{8,8},{10,10},{12,13},{14,15},{17,18},{19,... | collective-permute-start | bytes 1474568 | tf_op jit(solution)/shard_map/sums_20/ppermute | solution.py:163
  83.4 1.4 %collective-permute-start.18 = (bf16[384,640]{1,0:T(8,128)(2,1)}, bf16[384,640]{1,0:T(8,128)(2,1)}, u32[]{:S(2)}, u32[]{:S(2)}) collective-permute-start(bf16[384,640]{1,0:T(8,128)(2,1)} %get-tuple-element.73), channel_id=1, source_target_pairs={{1,18},{3,16},{5,23},{7,21},{9,24},{11,26},{13,29},{15,31},{16,2},... | collective-permute-start | bytes 1474568 | tf_op jit(solution)/shard_map/sums_cross_20/ppermute | solution.py:163
  84.8 1.1 %collective-permute-done.8 = bf16[640,640]{1,0:T(8,128)(2,1)} collective-permute-done((bf16[640,640]{1,0:T(8,128)(2,1)}, bf16[640,640]{1,0:T(8,128)(2,1)}, u32[]{:S(2)}, u32[]{:S(2)}) %collective-permute-start.8) | collective-permute-done | bytes 819232 | tf_op jit(solution)/shard_map/ring_after/ppermute | solution.py:163
  86.0 3.9 %conditional.5 = (bf16[384,640]{1,0:T(8,128)(2,1)}) conditional(s32[]{:T(128)} %bitcast.1, () %tuple.33, (bf16[384,640]{1,0:T(8,128)(2,1)}, bf16[640,640]{1,0:T(8,128)(2,1)}, bf16[384,640]{1,0:T(8,128)(2,1)}) %tuple.49), branch_computations={%region_4.5_spmd, %region_5.6_spmd} | conditional | flops 629637120 | bytes 10321996 | solution.py:238
  86.1 1.9 %fusion.7 = f32[384,640]{1,0:T(8,128)S(1)} fusion(bf16[384,640]{1,0:T(8,128)(2,1)} %get-tuple-element.46, bf16[640,640]{1,0:T(8,128)(2,1)} %get-tuple-element.47), kind=kOutput, calls=%fused_computation.17 | convolution fusion | flops 314572800 | bytes 2293760 | tf_op jit(solution)/shard_map/cond/branch_1_fun/dot_general | solution.py:246
  88.0 0.5 collective-permute-done.2
  88.5 1.4 %fusion.3 = bf16[384,640]{1,0:T(8,128)(2,1)} fusion(f32[384,640]{1,0:T(8,128)S(1)} %fusion.7, bf16[384,640]{1,0:T(8,128)(2,1)S(1)} %copy-done.6, bf16[640,640]{1,0:T(8,128)(2,1)S(1)} %collective-permute-done.2), kind=kOutput, calls=%fused_computation.9 | convolution fusion | flops 315064320 | bytes 2785280 | tf_op jit(solution)/shard_map/cond/branch_1_fun/dot_general | solution.py:247
  89.9 1.9 %collective-permute-start.13 = (bf16[384,640]{1,0:T(8,128)(2,1)}, bf16[384,640]{1,0:T(8,128)(2,1)S(1)}, u32[]{:S(2)}, u32[]{:S(2)}) collective-permute-start(bf16[384,640]{1,0:T(8,128)(2,1)} %get-tuple-element.86), channel_id=1, source_target_pairs={{0,1},{2,3},{4,6},{6,4},{8,11},{10,9},{12,12},{14,14},{17,17},{19,... | collective-permute-start | bytes 1474568 | tf_op jit(solution)/shard_map/sums_3/ppermute | solution.py:163
  91.8 1.3 %collective-permute-start.14 = (bf16[384,640]{1,0:T(8,128)(2,1)}, bf16[384,640]{1,0:T(8,128)(2,1)S(1)}, u32[]{:S(2)}, u32[]{:S(2)}) collective-permute-start(bf16[384,640]{1,0:T(8,128)(2,1)} %get-tuple-element.86), channel_id=1, source_target_pairs={{1,17},{3,19},{5,22},{7,20},{9,27},{11,25},{13,28},{15,30},{16,1},... | collective-permute-start | bytes 1474568 | tf_op jit(solution)/shard_map/sums_cross_3/ppermute | solution.py:163
  93.2 1.5 %copy-done.1 = f32[384,1280]{1,0:T(8,128)S(1)} copy-done((f32[384,1280]{1,0:T(8,128)S(1)}, f32[384,1280]{1,0:T(8,128)}, u32[]{:S(2)}) %copy-start.1) | copy-done | bytes 1966104
  94.8 1.9 %finish.2.refs_2_ = f32[384,1280]{1,0:T(8,128)S(1)} custom-call(s32[1]{0:T(128)} %bitcast.spot, bf16[384,640]{1,0:T(8,128)(2,1)S(1)} %collective-permute-done.11.refs_0_, bf16[384,640]{1,0:T(8,128)(2,1)S(1)} %collective-permute-done.15.refs_1_, bf16[384,640]{1,0:T(8,128)(2,1)} %collective-permute-done.16.refs_2_, ...), custom_call_target="tpu_custom_call" | custom-call | tf_op jit(solution)/shard_map/finish/pallas_call | solution.py:187
  96.7 8.3 %collective-permute-done.13.refs_0_ = bf16[384,640]{1,0:T(8,128)(2,1)S(1)} collective-permute-done((bf16[384,640]{1,0:T(8,128)(2,1)}, bf16[384,640]{1,0:T(8,128)(2,1)S(1)}, u32[]{:S(2)}, u32[]{:S(2)}) %collective-permute-start.13) | collective-permute-done | bytes 491552 | tf_op jit(solution)/shard_map/sums_3/ppermute | solution.py:163
  105.0 1.6 %collective-permute-done.14.refs_1_ = bf16[384,640]{1,0:T(8,128)(2,1)S(1)} collective-permute-done((bf16[384,640]{1,0:T(8,128)(2,1)}, bf16[384,640]{1,0:T(8,128)(2,1)S(1)}, u32[]{:S(2)}, u32[]{:S(2)}) %collective-permute-start.14) | collective-permute-done | bytes 491552 | tf_op jit(solution)/shard_map/sums_cross_3/ppermute | solution.py:163
  106.6 1.4 %finish.3 = f32[384,1280]{1,0:T(8,128)} custom-call(s32[1]{0:T(128)} %bitcast.spot, bf16[384,640]{1,0:T(8,128)(2,1)S(1)} %collective-permute-done.13.refs_0_, bf16[384,640]{1,0:T(8,128)(2,1)S(1)} %collective-permute-done.14.refs_1_, f32[384,1280]{1,0:T(8,128)S(1)} %finish.2.refs_2_, f32[1,1280]{1,0:T(1,128)S(1)} %broadcast_in_dim.4.refs_7_.refs_3_), custom_call_target="tpu_custom_call" | custom-call | tf_op jit(solution)/shard_map/finish/pallas_call | solution.py:187
  (25 shorter events, 0.5 us)
Async XLA Ops:
  0.0 6.1 %copy-start = (bf16[640,1280]{1,0:T(8,128)(2,1)S(1)}, bf16[640,1280]{1,0:T(8,128)(2,1)}, u32[]{:S(2)}) copy-start(bf16[640,1280]{1,0:T(8,128)(2,1)} %param.17) | copy-start | bytes 4915204
  0.0 25.7 %collective-permute-start.3 = (bf16[2,384,640]{2,1,0:T(8,128)(2,1)}, bf16[2,384,640]{2,1,0:T(8,128)(2,1)S(1)}, u32[]{:S(2)}, u32[]{:S(2)}) collective-permute-start(bf16[2,384,640]{2,1,0:T(8,128)(2,1)} %own_ref.1), channel_id=1, source_target_pairs={{0,4},{4,8},{8,12},{1,5},{5,9},{9,13},{2,6},{6,10},{10,14},{3,7},{... | collective-permute-start | bytes 2949128 | tf_op jit(solution)/shard_map/ppermute | solution.py:120
  3.6 25.9 %collective-permute-start.4 = (bf16[2,384,640]{2,1,0:T(8,128)(2,1)}, bf16[2,384,640]{2,1,0:T(8,128)(2,1)}, u32[]{:S(2)}, u32[]{:S(2)}) collective-permute-start(bf16[2,384,640]{2,1,0:T(8,128)(2,1)} %own_ref.1), channel_id=1, source_target_pairs={{4,0},{8,4},{12,8},{5,1},{9,5},{13,9},{6,2},{10,6},{14,10},{7,3},{... | collective-permute-start | bytes 2949128 | tf_op jit(solution)/shard_map/ppermute | solution.py:120
  7.0 57.0 %collective-permute-start.9 = (bf16[640,640]{1,0:T(8,128)(2,1)}, bf16[640,640]{1,0:T(8,128)(2,1)}, u32[]{:S(2)}, u32[]{:S(2)}) collective-permute-start(bf16[640,640]{1,0:T(8,128)(2,1)} %constant_dynamic-slice_fusion), channel_id=1, source_target_pairs={{0,1},{1,0},{2,3},{3,2},{4,5},{5,4},{6,7},{7,6},{8,9},{9,8},{10,11... | collective-permute-start | bytes 2457608 | tf_op jit(solution)/shard_map/core_swap_0/ppermute | solution.py:163
  25.7 19.5 %collective-permute-start.7 = (bf16[640,640]{1,0:T(8,128)(2,1)}, bf16[640,640]{1,0:T(8,128)(2,1)}, u32[]{:S(2)}, u32[]{:S(2)}) collective-permute-start(bf16[640,640]{1,0:T(8,128)(2,1)} %constant_dynamic-slice_fusion), channel_id=1, source_target_pairs={{0,4},{1,5},{2,14},{3,15},{4,8},{5,9},{6,2},{7,3},{8,12},{9,13},{1... | collective-permute-start | bytes 2457608 | tf_op jit(solution)/shard_map/ring_1/ppermute | solution.py:163
  29.5 1.2 %copy-start.2 = (bf16[2,384,640]{2,1,0:T(8,128)(2,1)S(1)}, bf16[2,384,640]{2,1,0:T(8,128)(2,1)}, u32[]{:S(2)}) copy-start(bf16[2,384,640]{2,1,0:T(8,128)(2,1)} %own_ref.1) | copy-start | bytes 2949124
  30.7 1.0 copy-start.3
  31.7 0.7 copy-start.4
  40.0 11.8 %collective-permute-start.5 = (bf16[384,640]{1,0:T(8,128)(2,1)S(1)}, bf16[384,640]{1,0:T(8,128)(2,1)S(1)}, u32[]{:S(2)}, u32[]{:S(2)}) collective-permute-start(bf16[384,640]{1,0:T(8,128)(2,1)S(1)} %attend.1), channel_id=1, source_target_pairs={{0,16},{1,0},{2,18},{3,2},{4,20},{5,4},{6,22},{7,6},{8,24},{9,8},{... | collective-permute-start | bytes 1474568 | tf_op jit(solution)/shard_map/rows_1/ppermute | solution.py:163
  41.6 10.2 %collective-permute-start.6 = (bf16[384,640]{1,0:T(8,128)(2,1)S(1)}, bf16[384,640]{1,0:T(8,128)(2,1)S(1)}, u32[]{:S(2)}, u32[]{:S(2)}) collective-permute-start(bf16[384,640]{1,0:T(8,128)(2,1)S(1)} %attend.1), channel_id=1, source_target_pairs={{1,16},{3,18},{5,20},{7,22},{9,24},{11,26},{13,28},{15,30},{16,1},... | collective-permute-start | bytes 1474568 | tf_op jit(solution)/shard_map/rows_2/ppermute | solution.py:163
  45.3 21.2 %collective-permute-start.10 = (bf16[640,640]{1,0:T(8,128)(2,1)}, bf16[640,640]{1,0:T(8,128)(2,1)}, u32[]{:S(2)}, u32[]{:S(2)}) collective-permute-start(bf16[640,640]{1,0:T(8,128)(2,1)} %collective-permute-done.7), channel_id=1, source_target_pairs={{0,4},{1,5},{2,14},{3,15},{4,8},{5,9},{6,2},{7,3},{8,12},{9,13},{1... | collective-permute-start | bytes 2457608 | tf_op jit(solution)/shard_map/ring_2/ppermute | solution.py:163
  53.3 13.2 %copy-start.5 = (bf16[384,640]{1,0:T(8,128)(2,1)}, bf16[384,640]{1,0:T(8,128)(2,1)S(1)}, u32[]{:S(2)}) copy-start(bf16[384,640]{1,0:T(8,128)(2,1)S(1)} %get-tuple-element.79) | copy-start | bytes 1474564
  53.3 3.7 %collective-permute-start.1 = (bf16[640,640]{1,0:T(8,128)(2,1)}, bf16[640,640]{1,0:T(8,128)(2,1)S(1)}, u32[]{:S(2)}, u32[]{:S(2)}) collective-permute-start(bf16[640,640]{1,0:T(8,128)(2,1)} %get-tuple-element.44), channel_id=1, source_target_pairs={{0,1},{1,0},{2,3},{3,2},{4,5},{5,4},{6,7},{7,6},{8,9},{9,8},{10,11... | collective-permute-start | bytes 2457608 | tf_op jit(solution)/shard_map/cond/branch_1_fun/core_swap/ppermute | solution.py:163
  58.3 17.1 %collective-permute-start.11 = (bf16[384,640]{1,0:T(8,128)(2,1)}, bf16[384,640]{1,0:T(8,128)(2,1)S(1)}, u32[]{:S(2)}, u32[]{:S(2)}) collective-permute-start(bf16[384,640]{1,0:T(8,128)(2,1)} %get-tuple-element.85), channel_id=1, source_target_pairs={{0,3},{2,1},{4,4},{6,6},{8,9},{10,11},{12,14},{14,12},{17,19},{19,... | collective-permute-start | bytes 1474568 | tf_op jit(solution)/shard_map/sums_1/ppermute | solution.py:163
  60.0 15.4 %collective-permute-start.12 = (bf16[384,640]{1,0:T(8,128)(2,1)}, bf16[384,640]{1,0:T(8,128)(2,1)S(1)}, u32[]{:S(2)}, u32[]{:S(2)}) collective-permute-start(bf16[384,640]{1,0:T(8,128)(2,1)} %get-tuple-element.85), channel_id=1, source_target_pairs={{1,19},{3,17},{5,20},{7,22},{9,25},{11,27},{13,30},{15,28},{16,3},... | collective-permute-start | bytes 1474568 | tf_op jit(solution)/shard_map/sums_cross_1/ppermute | solution.py:163
  61.3 24.7 %collective-permute-start.8 = (bf16[640,640]{1,0:T(8,128)(2,1)}, bf16[640,640]{1,0:T(8,128)(2,1)}, u32[]{:S(2)}, u32[]{:S(2)}) collective-permute-start(bf16[640,640]{1,0:T(8,128)(2,1)} %constant_dynamic-slice_fusion), channel_id=1, source_target_pairs={{4,0},{5,1},{14,2},{15,3},{8,4},{9,5},{2,6},{3,7},{12,8},{13,9},{6... | collective-permute-start | bytes 2457608 | tf_op jit(solution)/shard_map/ring_after/ppermute | solution.py:163
  66.4 6.2 %collective-permute-start = (bf16[640,640]{1,0:T(8,128)(2,1)}, bf16[640,640]{1,0:T(8,128)(2,1)}, u32[]{:S(2)}, u32[]{:S(2)}) collective-permute-start(bf16[640,640]{1,0:T(8,128)(2,1)} %get-tuple-element.42), channel_id=1, source_target_pairs={{0,1},{1,0},{2,3},{3,2},{4,5},{5,4},{6,7},{7,6},{8,9},{9,8},{10,11... | collective-permute-start | bytes 2457608 | tf_op jit(solution)/shard_map/cond/branch_1_fun/core_swap/ppermute | solution.py:163
  75.4 16.4 %collective-permute-start.15 = (bf16[384,640]{1,0:T(8,128)(2,1)}, bf16[384,640]{1,0:T(8,128)(2,1)S(1)}, u32[]{:S(2)}, u32[]{:S(2)}) collective-permute-start(bf16[384,640]{1,0:T(8,128)(2,1)} %get-tuple-element.72), channel_id=1, source_target_pairs={{0,0},{2,2},{4,5},{6,7},{8,10},{10,8},{12,15},{14,13},{17,16},{19,... | collective-permute-start | bytes 1474568 | tf_op jit(solution)/shard_map/sums_02/ppermute | solution.py:163
  77.4 15.8 %collective-permute-start.17 = (bf16[384,640]{1,0:T(8,128)(2,1)}, bf16[384,640]{1,0:T(8,128)(2,1)}, u32[]{:S(2)}, u32[]{:S(2)}) collective-permute-start(bf16[384,640]{1,0:T(8,128)(2,1)} %get-tuple-element.72), channel_id=1, source_target_pairs={{1,16},{3,18},{5,21},{7,23},{9,26},{11,24},{13,31},{15,29},{16,0},... | collective-permute-start | bytes 1474568 | tf_op jit(solution)/shard_map/sums_cross_02/ppermute | solution.py:163
  78.8 14.4 %collective-permute-start.16 = (bf16[384,640]{1,0:T(8,128)(2,1)}, bf16[384,640]{1,0:T(8,128)(2,1)}, u32[]{:S(2)}, u32[]{:S(2)}) collective-permute-start(bf16[384,640]{1,0:T(8,128)(2,1)} %get-tuple-element.73), channel_id=1, source_target_pairs={{0,2},{2,0},{4,7},{6,5},{8,8},{10,10},{12,13},{14,15},{17,18},{19,... | collective-permute-start | bytes 1474568 | tf_op jit(solution)/shard_map/sums_20/ppermute | solution.py:163
  83.4 9.8 %collective-permute-start.18 = (bf16[384,640]{1,0:T(8,128)(2,1)}, bf16[384,640]{1,0:T(8,128)(2,1)}, u32[]{:S(2)}, u32[]{:S(2)}) collective-permute-start(bf16[384,640]{1,0:T(8,128)(2,1)} %get-tuple-element.73), channel_id=1, source_target_pairs={{1,18},{3,16},{5,23},{7,21},{9,24},{11,26},{13,29},{15,31},{16,2},... | collective-permute-start | bytes 1474568 | tf_op jit(solution)/shard_map/sums_cross_20/ppermute | solution.py:163
  86.0 7.2 %copy-start.7 = (f32[1280]{0:T(1024)S(1)}, f32[1280]{0:T(1024)}, u32[]{:S(2)}) copy-start(f32[1280]{0:T(1024)} %param.16) | copy-start | bytes 15364
  86.0 2.5 %copy-start.6 = (bf16[384,640]{1,0:T(8,128)(2,1)S(1)}, bf16[384,640]{1,0:T(8,128)(2,1)}, u32[]{:S(2)}) copy-start(bf16[384,640]{1,0:T(8,128)(2,1)} %get-tuple-element.48) | copy-start | bytes 1474564 | tf_op jit(solution)/shard_map/cond
  86.0 2.5 %collective-permute-start.2 = (bf16[640,640]{1,0:T(8,128)(2,1)}, bf16[640,640]{1,0:T(8,128)(2,1)S(1)}, u32[]{:S(2)}, u32[]{:S(2)}) collective-permute-start(bf16[640,640]{1,0:T(8,128)(2,1)} %get-tuple-element.47), channel_id=1, source_target_pairs={{0,1},{1,0},{2,3},{3,2},{4,5},{5,4},{6,7},{7,6},{8,9},{9,8},{10,11... | collective-permute-start | bytes 2457608 | tf_op jit(solution)/shard_map/cond/branch_1_fun/core_swap/ppermute | solution.py:163
  89.9 15.0 %collective-permute-start.13 = (bf16[384,640]{1,0:T(8,128)(2,1)}, bf16[384,640]{1,0:T(8,128)(2,1)S(1)}, u32[]{:S(2)}, u32[]{:S(2)}) collective-permute-start(bf16[384,640]{1,0:T(8,128)(2,1)} %get-tuple-element.86), channel_id=1, source_target_pairs={{0,1},{2,3},{4,6},{6,4},{8,11},{10,9},{12,12},{14,14},{17,17},{19,... | collective-permute-start | bytes 1474568 | tf_op jit(solution)/shard_map/sums_3/ppermute | solution.py:163
  91.8 14.7 %collective-permute-start.14 = (bf16[384,640]{1,0:T(8,128)(2,1)}, bf16[384,640]{1,0:T(8,128)(2,1)S(1)}, u32[]{:S(2)}, u32[]{:S(2)}) collective-permute-start(bf16[384,640]{1,0:T(8,128)(2,1)} %get-tuple-element.86), channel_id=1, source_target_pairs={{1,17},{3,19},{5,22},{7,20},{9,27},{11,25},{13,28},{15,30},{16,1},... | collective-permute-start | bytes 1474568 | tf_op jit(solution)/shard_map/sums_cross_3/ppermute | solution.py:163
  93.2 1.5 %copy-start.1 = (f32[384,1280]{1,0:T(8,128)S(1)}, f32[384,1280]{1,0:T(8,128)}, u32[]{:S(2)}) copy-start(f32[384,1280]{1,0:T(8,128)} %refs_6_.1) | copy-start | bytes 5898244
